TPU v7x, 128 devices: a whole 4x4x4 slice. The times are simulated.
128 devices in a mesh: seq: 16 (over x_lo, z, core), chan: 8 (over y, x_hi).
Axes of the slice: x: 4 (x_hi: 2, x_lo: 2; x = x_hi * 2 + x_lo), y: 4, z: 4, core: 2. Of those that a mesh axis runs over, the one named last changes fastest.
Arguments:
- tokens: bfloat16 [8192, 4096], P('seq', 'chan'), may hold values from -6 to 6
- in_weight: bfloat16 [4096, 3, 4096], P(None, None, 'chan'), may hold values from -0.09375 to 0.09375
- short_weight: float32 [3, 3, 4096], P(None, None, 'chan'), may hold values from -3 to 3
- long_filter: float32 [8192, 4096], P('seq', 'chan'), may hold values from -0.0625 to 0.0625
- skip_gain: float32 [4096], P('chan'), may hold values from -4 to 4
- out_weight: bfloat16 [4096, 4096], P('chan'), may hold values from -0.125 to 0.125
Outputs:
- mixed: bfloat16 [8192, 4096], P('seq', 'chan')
All inputs are finite; a program needn't handle non-finite values.
Results may differ from a plain program's by a relative error of at most 0.019.
Values may be sent and summed in bfloat16 or wider, within the bound.
No kernel may reach another device: no remote copies, remote signals or barrier semaphores. Data moves between devices by JAX's collectives and lax.ppermute only.
A program may use at most 128 MiB of HBM per device.

v0:
```python
import math

import jax
import jax.numpy as jnp
from jax import lax
from jax.sharding import PartitionSpec as P


def shifted(array, axis, by):
    count = lax.axis_size(axis)
    pairs = [(i, i + by) for i in range(count) if 0 <= i + by < count]
    return lax.ppermute(array, axis, pairs)


def angle_table(first, second, period):
    prod = first[:, None] * second[None, :] % period
    angle = prod.astype(jnp.float32) * (2.0 * math.pi / period)
    return (jnp.cos(angle), jnp.sin(angle))


def mult(form, left, right):
    return jnp.einsum(form, left, right, precision=lax.Precision.HIGHEST)


def forward_rows(values, col_index, seqs, total):
    row_cos, row_sin = angle_table(jnp.arange(2 * seqs), jnp.arange(seqs), 2 * seqs)
    real_part = mult("kn,nqc->kqc", row_cos, values)
    imag_part = -mult("kn,nqc->kqc", row_sin, values)
    tw_cos, tw_sin = angle_table(jnp.arange(2 * seqs), col_index, total)
    tw_cos = tw_cos[:, :, None]
    tw_sin = tw_sin[:, :, None]
    return (real_part * tw_cos + imag_part * tw_sin, imag_part * tw_cos - real_part * tw_sin)


def forward_cols(real_part, imag_part, rows):
    col_cos, col_sin = angle_table(jnp.arange(rows), jnp.arange(rows), rows)
    out_real = mult("kn,jnc->jkc", col_cos, real_part) + mult("kn,jnc->jkc", col_sin, imag_part)
    out_imag = mult("kn,jnc->jkc", col_cos, imag_part) - mult("kn,jnc->jkc", col_sin, real_part)
    return (out_real, out_imag)


def inverse_cols(real_part, imag_part, row_index, rows, total):
    col_cos, col_sin = angle_table(jnp.arange(rows), jnp.arange(rows), rows)
    back_real = mult("kn,jnc->jkc", col_cos, real_part) - mult("kn,jnc->jkc", col_sin, imag_part)
    back_imag = mult("kn,jnc->jkc", col_cos, imag_part) + mult("kn,jnc->jkc", col_sin, real_part)
    tw_cos, tw_sin = angle_table(row_index, jnp.arange(rows), total)
    tw_cos = tw_cos[:, :, None]
    tw_sin = tw_sin[:, :, None]
    return (back_real * tw_cos - back_imag * tw_sin, back_imag * tw_cos + back_real * tw_sin)


def inverse_rows(real_part, imag_part, seqs, total):
    row_cos, row_sin = angle_table(jnp.arange(2 * seqs), jnp.arange(seqs), 2 * seqs)
    result = mult("kn,kqc->nqc", row_cos, real_part) - mult("kn,kqc->nqc", row_sin, imag_part)
    return result * (1.0 / total)


def spectral_product(fil_re, fil_im, sig_re, sig_im):
    return (sig_re * fil_re - sig_im * fil_im, sig_re * fil_im + sig_im * fil_re)


def shards(tokens, in_weight, short_weight, long_filter, skip_gain, out_weight):
    rows = tokens.shape[0]
    width = in_weight.shape[2]
    model = in_weight.shape[0]
    flat_weight = in_weight.reshape(model, 3 * width)
    proj = jnp.dot(
        lax.all_gather(tokens, "chan", axis=1, tiled=True),
        flat_weight,
        preferred_element_type=jnp.float32,
    ).astype(jnp.bfloat16)
    prior = shifted(proj[rows - 2 :], "seq", 1)
    extended = (
        jnp.concatenate([prior, proj], axis=0).astype(jnp.float32).reshape(rows + 2, 3, width)
    )
    short = (
        short_weight[0] * extended[0:rows]
        + short_weight[1] * extended[1 : rows + 1]
        + short_weight[2] * extended[2 : rows + 2]
    )
    gate_out = short[:, 0, :]
    signal = short[:, 2, :] * short[:, 1, :]
    seqs = lax.axis_size("seq")
    total = 2 * rows * seqs
    slice_rows = rows // seqs
    position = lax.axis_index("seq")
    first = (
        lax.all_to_all(long_filter[None], "seq", split_axis=1, concat_axis=0, tiled=True),
        lax.all_to_all(signal[None], "seq", split_axis=1, concat_axis=0, tiled=True),
    )
    col_index = position * slice_rows + jnp.arange(slice_rows)
    fil_re, fil_im = forward_rows(first[0], col_index, seqs, total)
    sig_re, sig_im = forward_rows(first[1], col_index, seqs, total)
    second = (
        lax.all_to_all(fil_re, "seq", split_axis=0, concat_axis=1, tiled=True),
        lax.all_to_all(fil_im, "seq", split_axis=0, concat_axis=1, tiled=True),
        lax.all_to_all(sig_re, "seq", split_axis=0, concat_axis=1, tiled=True),
        lax.all_to_all(sig_im, "seq", split_axis=0, concat_axis=1, tiled=True),
    )
    fil_re, fil_im = forward_cols(second[0], second[1], rows)
    sig_re, sig_im = forward_cols(second[2], second[3], rows)
    prod_re, prod_im = spectral_product(fil_re, fil_im, sig_re, sig_im)
    row_index = position * 2 + jnp.arange(2)
    back_re, back_im = inverse_cols(prod_re, prod_im, row_index, rows, total)
    third = (
        lax.all_to_all(
            back_re.astype(jnp.bfloat16), "seq", split_axis=1, concat_axis=0, tiled=True
        ).astype(back_re.dtype),
        lax.all_to_all(
            back_im.astype(jnp.bfloat16), "seq", split_axis=1, concat_axis=0, tiled=True
        ).astype(back_im.dtype),
    )
    result = inverse_rows(third[0], third[1], seqs, total)
    conv = lax.all_to_all(
        result.astype(jnp.bfloat16), "seq", split_axis=0, concat_axis=1, tiled=True
    ).astype(result.dtype)[0]
    conv = conv + skip_gain * signal
    gated = (conv * gate_out).astype(jnp.bfloat16)
    term = jnp.dot(gated, out_weight, preferred_element_type=jnp.float32)
    return lax.psum_scatter(term.astype(jnp.bfloat16), "chan", scatter_dimension=1, tiled=True)


def solution(mesh):
    in_specs = (
        P("seq", "chan"),
        P(None, None, "chan"),
        P(None, None, "chan"),
        P("seq", "chan"),
        P("chan"),
        P("chan", None),
    )
    out_specs = P("seq", "chan")
    return jax.shard_map(shards, mesh=mesh, in_specs=in_specs, out_specs=out_specs, check_vma=False)
```

profile of v0, /device:TPU:0, one launch (start us, length us, event | category | flops | bytes accessed | tf_op | source)
XLA Modules:
  0.0 574.6 jit_solution(2536122358812842071)
XLA Ops:
  7.3 2.9 broadcast_in_dim.2
  10.2 6.5 %all-to-all-start.3 = ((f32[1,512,512]{2,0,1:T(1,128)}), f32[1,512,512]{2,0,1:T(1,128)}, u32[]{:S(2)}, u32[]{:S(2)}) async-start(f32[1,512,512]{2,0,1:T(1,128)} %broadcast_in_dim.2), calls=%async_computation.3 | async-start | bytes 2097152 | tf_op jit(solution)/shard_map/all_to_all | solution.py:88
  16.7 17.0 %copy.71 = bf16[4096,3,512]{0,2,1:T(8,128)(2,1)} copy(bf16[4096,3,512]{2,0,1:T(8,128)(2,1)} %param.7) | data formatting | bytes 25165824 | tf_op args[1]
  33.7 58.1 %all-gather.2.cloned.1.call-done = bf16[512,4096]{1,0:T(8,128)(2,1)} async-done(((bf16[512,512]{1,0:T(8,128)(2,1)}), bf16[512,4096]{1,0:T(8,128)(2,1)}) %all-gather.2.cloned.1.call-update) | async-done | bytes 4194320 | tf_op jit(solution)/shard_map/all_gather | solution.py:68
  91.8 10.9 %convolution_convert_fusion.1 = bf16[512,1536]{1,0:T(8,128)(2,1)S(1)} fusion(bf16[512,4096]{1,0:T(8,128)(2,1)} %all-gather.2.cloned.1.call-done, bf16[4096,1536]{0,1:T(8,128)(2,1)} %bitcast.136), kind=kOutput, calls=%fused_computation.2 | convolution fusion | flops 6443237376 | bytes 18350080 | tf_op jit(solution)/shard_map/dot_general | solution.py:67
  105.4 3.6 fusion.174
  109.0 3.5 copy.72
  112.6 3.6 copy.73
  118.5 4.2 multiply_add_fusion
  123.9 3.6 copy.75
  127.5 7.6 %all-to-all-start = ((f32[1,512,512]{2,0,1:T(1,128)}), f32[1,512,512]{2,0,1:T(1,128)}, u32[]{:S(2)}, u32[]{:S(2)}) async-start(f32[1,512,512]{2,0,1:T(1,128)} %copy.75), calls=%async_computation | async-start | bytes 2097152 | tf_op jit(solution)/shard_map/all_to_all | solution.py:89
  137.5 3.6 fusion.43
  141.1 10.6 %all-to-all-done = f32[1,512,512]{2,0,1:T(1,128)} async-done(((f32[1,512,512]{2,0,1:T(1,128)}), f32[1,512,512]{2,0,1:T(1,128)}, u32[]{:S(2)}, u32[]{:S(2)}) %all-to-all-start) | async-done | bytes 1048608 | tf_op jit(solution)/shard_map/all_to_all | solution.py:89
  157.5 4.9 multiply_subtract_fusion.1
  162.4 2.6 copy.86
  165.0 4.4 all-to-all-start.4
  169.4 4.2 copy.89
  173.6 24.7 %all-to-all-done.4 = f32[32,32,512]{2,1,0:T(8,128)} async-done(((f32[32,32,512]{2,1,0:T(8,128)}), f32[32,32,512]{2,1,0:T(8,128)}, u32[]{:S(2)}, u32[]{:S(2)}) %all-to-all-start.4) | async-done | bytes 2097184 | tf_op jit(solution)/shard_map/all_to_all | solution.py:95
  198.3 5.6 all-to-all-start.5
  203.9 4.2 copy.78
  208.1 24.6 %all-to-all-done.5 = f32[32,32,512]{2,1,0:T(8,128)} async-done(((f32[32,32,512]{2,1,0:T(8,128)}), f32[32,32,512]{2,1,0:T(8,128)}, u32[]{:S(2)}, u32[]{:S(2)}) %all-to-all-start.5) | async-done | bytes 2097184 | tf_op jit(solution)/shard_map/all_to_all | solution.py:96
  232.7 5.7 all-to-all-start.1
  238.3 4.2 copy.81
  242.5 24.6 %all-to-all-done.1 = f32[32,32,512]{2,1,0:T(8,128)} async-done(((f32[32,32,512]{2,1,0:T(8,128)}), f32[32,32,512]{2,1,0:T(8,128)}, u32[]{:S(2)}, u32[]{:S(2)}) %all-to-all-start.1) | async-done | bytes 2097184 | tf_op jit(solution)/shard_map/all_to_all | solution.py:97
  267.2 5.6 all-to-all-start.2
  279.0 10.9 %fusion.36 = f32[2,512,512]{2,1,0:T(8,128)S(1)} fusion(f32[2,512,512]{2,1,0:T(8,128)S(1)} %bitcast.146), kind=kOutput, calls=%fused_computation.55 | convolution fusion | flops 3224895488 | bytes 4194304 | tf_op jit(solution)/shard_map/kn,jnc->jkc/dot_general | solution.py:22
  290.0 11.6 %fusion.38 = f32[2,512,512]{2,1,0:T(8,128)} fusion(f32[2,512,512]{2,1,0:T(8,128)S(1)} %bitcast.144), kind=kOutput, calls=%fused_computation.57 | convolution fusion | flops 3224895488 | bytes 4194304 | tf_op jit(solution)/shard_map/kn,jnc->jkc/dot_general | solution.py:22
  301.5 11.7 %fusion.32 = f32[2,512,512]{2,1,0:T(8,128)} fusion(f32[2,512,512]{2,1,0:T(8,128)S(1)} %bitcast.148), kind=kOutput, calls=%fused_computation.51 | convolution fusion | flops 3224895488 | bytes 4194304 | tf_op jit(solution)/shard_map/kn,jnc->jkc/dot_general | solution.py:22
  313.2 11.6 %convolution_add_fusion = f32[2,512,512]{2,1,0:T(8,128)} fusion(f32[2,512,512]{2,1,0:T(8,128)S(1)} %fusion.36, f32[2,512,512]{2,1,0:T(8,128)S(1)} %bitcast.149), kind=kOutput, calls=%fused_computation.23 | convolution fusion | flops 3225419776 | bytes 6291456 | tf_op jit(solution)/shard_map/kn,jnc->jkc/dot_general | solution.py:22
  326.6 11.1 %fusion.34 = f32[2,512,512]{2,1,0:T(8,128)S(1)} fusion(f32[2,512,512]{2,1,0:T(8,128)S(1)} %bitcast.150), kind=kOutput, calls=%fused_computation.53 | convolution fusion | flops 3224895488 | bytes 4194304 | tf_op jit(solution)/shard_map/kn,jnc->jkc/dot_general | solution.py:22
  337.7 11.2 %convolution_add_fusion.1 = f32[2,512,512]{2,1,0:T(8,128)S(1)} fusion(f32[2,512,512]{2,1,0:T(8,128)S(1)} %copy-done.9, f32[2,512,512]{2,1,0:T(8,128)S(1)} %bitcast.151), kind=kOutput, calls=%fused_computation.24 | convolution fusion | flops 3225419776 | bytes 6291456 | tf_op jit(solution)/shard_map/kn,jnc->jkc/dot_general | solution.py:22
  349.0 11.6 %convolution_subtract_fusion = f32[2,512,512]{2,1,0:T(8,128)S(1)} fusion(f32[2,512,512]{2,1,0:T(8,128)S(1)} %copy-done.8, f32[2,512,512]{2,1,0:T(8,128)S(1)} %bitcast.147), kind=kOutput, calls=%fused_computation.21 | convolution fusion | flops 3225419776 | bytes 6291456 | tf_op jit(solution)/shard_map/kn,jnc->jkc/dot_general | solution.py:22
  360.6 11.6 %multiply_subtract_fusion = (f32[2,512,512]{2,1,0:T(8,128)S(1)}, f32[2,512,512]{2,1,0:T(8,128)S(1)}) fusion(f32[2,512,512]{2,1,0:T(8,128)S(1)} %convolution_subtract_fusion, f32[2,512,512]{2,1,0:T(8,128)S(1)} %convolution_add_fusion.1, f32[2,512,512]{2,1,0:T(8,128)S(1)} %copy-done.2, f32[2,512,512]{2,1,0:T(8,128)S(1)} %fusion.34, ...), kind=kOutput, calls=%fused_computation.14 | convolution fusion | flops 3228565504 | bytes 14680064 | tf_op jit(solution)/shard_map/kn,jnc->jkc/dot_general | solution.py:22
  372.3 8.6 %fusion.2 = f32[2,512,512]{2,1,0:T(8,128)S(1)} fusion(f32[2,512,512]{2,1,0:T(8,128)S(1)} %get-tuple-element.6), kind=kOutput, calls=%fused_computation.5 | convolution fusion | flops 3224895488 | bytes 4194304 | tf_op jit(solution)/shard_map/kn,jnc->jkc/dot_general | solution.py:22
  380.9 8.4 %fusion = f32[2,512,512]{2,1,0:T(8,128)S(1)} fusion(f32[2,512,512]{2,1,0:T(8,128)S(1)} %get-tuple-element.6), kind=kOutput, calls=%fused_computation.3 | convolution fusion | flops 3224895488 | bytes 4194304 | tf_op jit(solution)/shard_map/kn,jnc->jkc/dot_general | solution.py:22
  389.3 8.7 %fusion.8 = f32[2,512,512]{2,1,0:T(8,128)S(1)} fusion(f32[2,512,512]{2,1,0:T(8,128)S(1)} %fusion.2, f32[2,512,512]{2,1,0:T(8,128)S(1)} %get-tuple-element.5), kind=kOutput, calls=%fused_computation.19 | convolution fusion | flops 3225419776 | bytes 6291456 | tf_op jit(solution)/shard_map/kn,jnc->jkc/dot_general | solution.py:22
  397.9 8.8 %fusion.20 = (bf16[2,512,512]{1,2,0:T(8,128)(2,1)}, bf16[2,512,512]{1,2,0:T(8,128)(2,1)}) fusion(f32[2,512,512]{2,1,0:T(8,128)S(1)} %fusion.8, f32[2,512]{1,0:T(2,128)S(1)} %get-tuple-element.22, f32[2,512]{1,0:T(2,128)S(1)} %get-tuple-element.21, f32[2,512,512]{2,1,0:T(8,128)S(1)} %fusion, f32[2,512,512]{2,1,0:T(8,128)S(1)} %get-tuple-element.5), kind=kOutput, calls=%fused_computation.36 | convolution fusion | flops 3229614080 | bytes 8396800 | tf_op jit(solution)/shard_map/kn,jnc->jkc/dot_general | solution.py:22
  406.8 3.7 copy.96
  410.4 5.7 all-to-all-start.6
  416.2 3.6 copy.99
  419.8 13.0 %all-to-all-done.6 = bf16[2,512,512]{2,0,1:T(2,128)(2,1)} async-done(((bf16[2,512,512]{2,0,1:T(2,128)(2,1)}), bf16[2,512,512]{2,0,1:T(2,128)(2,1)}, u32[]{:S(2)}, u32[]{:S(2)}) %all-to-all-start.6) | async-done | bytes 1048608 | tf_op jit(solution)/shard_map/all_to_all | solution.py:106
  432.8 4.3 all-to-all-start.7
  443.1 2.8 fusion.80
  446.0 7.8 %all-to-all-done.7 = bf16[2,512,512]{2,0,1:T(2,128)(2,1)} async-done(((bf16[2,512,512]{2,0,1:T(2,128)(2,1)}), bf16[2,512,512]{2,0,1:T(2,128)(2,1)}, u32[]{:S(2)}, u32[]{:S(2)}) %all-to-all-start.7) | async-done | bytes 1048608 | tf_op jit(solution)/shard_map/all_to_all | solution.py:109
  462.0 13.5 %all_to_all.141 = bf16[16,32,512]{2,1,0:T(8,128)(2,1)S(1)} all-to-all(bf16[16,32,512]{2,1,0:T(8,128)(2,1)S(1)} %copy.102), channel_id=1, replica_groups=mesh['seq'=16,'chan'=8] {'seq'}, dimensions={0} | all-to-all | bytes 1048576 | tf_op jit(solution)/shard_map/all_to_all | solution.py:114
  476.6 2.6 copy.103
  479.2 7.1 %convolution_convert_fusion = bf16[512,4096]{1,0:T(8,128)(2,1)} fusion(bf16[512,4096]{1,0:T(8,128)(2,1)} %param.11, f32[512,3,512]{0,2,1:T(8,128)S(1)} %multiply_add_fusion, f32[512,512]{0,1:T(8,128)} %copy.103, f32[512]{0:T(512)S(1)} %copy-done.10), kind=kOutput, calls=%fused_computation | convolution fusion | flops 2150891520 | bytes 12584960 | tf_op jit(solution)/shard_map/dot_general | solution.py:119
  486.3 81.2 %reduce-scatter.2.cloned.1.call-done = bf16[512,512]{1,0:T(8,128)(2,1)} async-done(((bf16[512,4096]{1,0:T(8,128)(2,1)}), bf16[512,512]{1,0:T(8,128)(2,1)}) %reduce-scatter.2.cloned.1.call-update) | async-done | bytes 524304 | tf_op jit(solution)/shard_map/reduce_scatter | solution.py:120
  (58 shorter events, 38.5 us)
Async XLA Ops:
  6.5 85.3 %all-gather.2.cloned.1.call-start = ((), (), s32[]{:S(2)}) async-start(), calls=%async_computation.10 | async-start | bytes 4718592 | tf_op jit(solution)/shard_map/all_gather | solution.py:68
  10.2 117.3 %all-to-all-start.3 = ((f32[1,512,512]{2,0,1:T(1,128)}), f32[1,512,512]{2,0,1:T(1,128)}, u32[]{:S(2)}, u32[]{:S(2)}) async-start(f32[1,512,512]{2,0,1:T(1,128)} %broadcast_in_dim.2), calls=%async_computation.3 | async-start | bytes 2097152 | tf_op jit(solution)/shard_map/all_to_all | solution.py:88
  91.8 12.3 %copy-start.11 = (f32[3,3,512]{2,1,0:T(4,128)S(1)}, f32[3,3,512]{2,1,0:T(4,128)}, u32[]{:S(2)}) copy-start(f32[3,3,512]{2,1,0:T(4,128)} %param.8) | copy-start | bytes 55300
  102.8 2.1 collective-permute-start
  127.5 24.2 %all-to-all-start = ((f32[1,512,512]{2,0,1:T(1,128)}), f32[1,512,512]{2,0,1:T(1,128)}, u32[]{:S(2)}, u32[]{:S(2)}) async-start(f32[1,512,512]{2,0,1:T(1,128)} %copy.75), calls=%async_computation | async-start | bytes 2097152 | tf_op jit(solution)/shard_map/all_to_all | solution.py:89
  136.5 1.0 copy-start
  155.2 2.3 copy-start.1
  155.2 2.3 copy-start.7
  165.0 33.3 %all-to-all-start.4 = ((f32[32,32,512]{2,1,0:T(8,128)}), f32[32,32,512]{2,1,0:T(8,128)}, u32[]{:S(2)}, u32[]{:S(2)}) async-start(f32[32,32,512]{2,1,0:T(8,128)} %copy.86), calls=%async_computation.4 | async-start | bytes 4194304 | tf_op jit(solution)/shard_map/all_to_all | solution.py:95
  198.3 34.4 %all-to-all-start.5 = ((f32[32,32,512]{2,1,0:T(8,128)}), f32[32,32,512]{2,1,0:T(8,128)}, u32[]{:S(2)}, u32[]{:S(2)}) async-start(f32[32,32,512]{2,1,0:T(8,128)} %copy.89), calls=%async_computation.5 | async-start | bytes 4194304 | tf_op jit(solution)/shard_map/all_to_all | solution.py:96
  232.7 34.5 %all-to-all-start.1 = ((f32[32,32,512]{2,1,0:T(8,128)}), f32[32,32,512]{2,1,0:T(8,128)}, u32[]{:S(2)}, u32[]{:S(2)}) async-start(f32[32,32,512]{2,1,0:T(8,128)} %copy.78), calls=%async_computation.1 | async-start | bytes 4194304 | tf_op jit(solution)/shard_map/all_to_all | solution.py:97
  267.2 57.6 %all-to-all-start.2 = ((f32[32,32,512]{2,1,0:T(8,128)}), f32[32,32,512]{2,1,0:T(8,128)}, u32[]{:S(2)}, u32[]{:S(2)}) async-start(f32[32,32,512]{2,1,0:T(8,128)} %copy.81), calls=%async_computation.2 | async-start | bytes 4194304 | tf_op jit(solution)/shard_map/all_to_all | solution.py:98
  274.7 4.3 copy-start.5
  279.0 10.9 %copy-start.3 = (f32[2,16,32,512]{3,2,1,0:T(8,128)}, f32[2,16,32,512]{3,2,1,0:T(8,128)S(1)}, u32[]{:S(2)}) copy-start(f32[2,16,32,512]{3,2,1,0:T(8,128)S(1)} %copy.79) | copy-start | bytes 6291460
  326.6 11.1 %copy-start.9 = (f32[2,512,512]{2,1,0:T(8,128)S(1)}, f32[2,512,512]{2,1,0:T(8,128)}, u32[]{:S(2)}) copy-start(f32[2,512,512]{2,1,0:T(8,128)} %fusion.38) | copy-start | bytes 6291460
  337.7 11.3 %copy-start.6 = (f32[2,16,32,512]{3,2,1,0:T(8,128)S(1)}, f32[2,16,32,512]{3,2,1,0:T(8,128)}, u32[]{:S(2)}) copy-start(f32[2,16,32,512]{3,2,1,0:T(8,128)} %copy-done.5) | copy-start | bytes 6291460
  337.7 11.3 %copy-start.8 = (f32[2,512,512]{2,1,0:T(8,128)S(1)}, f32[2,512,512]{2,1,0:T(8,128)}, u32[]{:S(2)}) copy-start(f32[2,512,512]{2,1,0:T(8,128)} %fusion.32) | copy-start | bytes 6291460
  349.0 11.6 %copy-start.2 = (f32[2,512,512]{2,1,0:T(8,128)S(1)}, f32[2,512,512]{2,1,0:T(8,128)}, u32[]{:S(2)}) copy-start(f32[2,512,512]{2,1,0:T(8,128)} %convolution_add_fusion) | copy-start | bytes 6291460
  349.0 11.6 %copy-start.4 = (f32[2,16,32,512]{3,2,1,0:T(8,128)S(1)}, f32[2,16,32,512]{3,2,1,0:T(8,128)}, u32[]{:S(2)}) copy-start(f32[2,16,32,512]{3,2,1,0:T(8,128)} %copy-done.3) | copy-start | bytes 6291460
  410.4 22.4 %all-to-all-start.6 = ((bf16[2,512,512]{2,0,1:T(2,128)(2,1)}), bf16[2,512,512]{2,0,1:T(2,128)(2,1)}, u32[]{:S(2)}, u32[]{:S(2)}) async-start(bf16[2,512,512]{2,0,1:T(2,128)(2,1)} %copy.96), calls=%async_computation.6 | async-start | bytes 2097152 | tf_op jit(solution)/shard_map/all_to_all | solution.py:106
  432.8 20.9 %all-to-all-start.7 = ((bf16[2,512,512]{2,0,1:T(2,128)(2,1)}), bf16[2,512,512]{2,0,1:T(2,128)(2,1)}, u32[]{:S(2)}, u32[]{:S(2)}) async-start(bf16[2,512,512]{2,0,1:T(2,128)(2,1)} %copy.99), calls=%async_computation.7 | async-start | bytes 2097152 | tf_op jit(solution)/shard_map/all_to_all | solution.py:109
  437.2 130.3 %reduce-scatter.2.cloned.1.call-start = ((), (), s32[]{:S(2)}) async-start(), calls=%async_computation.11 | async-start | bytes 4718592 | tf_op jit(solution)/shard_map/reduce_scatter | solution.py:120
  475.4 3.7 copy-start.10
Sparse Core Ops, SparseCore 0:
  9.5 82.2 all-gather.1
  486.4 81.0 reduce-scatter.1
where the time goes:
time: 582 us; the launch traced here: 575 us
  waiting for transfers between devices  246 us (42%)
  matrix products  162 us (28%)
  local copies, waits for them, and re-layouts  85.1 us (15%)
  starting transfers between devices  46.8 us (8%)
  between operations  14.1 us (2%)
  blocking collectives  13.5 us (2%)
  other arithmetic  7.26 us (1%)
    dot_general x18, matrix products, mult(): return jnp.einsum(form, left, right, precision=lax.Precision.HIGHEST)  144 us
    reduce_scatter x1, waiting for transfers between devices, shards(): lax.psum_scatter(term.astype(jnp.bfloat16), 'chan', scatter_dimension=1,...  81.2 us
    all_gather x1, waiting for transfers between devices, shards(): lax.all_gather(tokens, 'chan', axis=1, tiled=True)  58.1 us
    all_to_all x1, waiting for transfers between devices, shards(): lax.all_to_all(fil_re, 'seq', split_axis=0, concat_axis=1, tiled=True)  24.7 us
    all_to_all x1, waiting for transfers between devices, shards(): lax.all_to_all(sig_re, 'seq', split_axis=0, concat_axis=1, tiled=True)  24.6 us
    all_to_all x1, waiting for transfers between devices, shards(): lax.all_to_all(fil_im, 'seq', split_axis=0, concat_axis=1, tiled=True)  24.6 us
    unnamed x27, local copies, waits for them, and re-layouts  20.6 us
    all_to_all x1, blocking collectives, shards(): lax.all_to_all(result.astype(jnp.bfloat16), 'seq', split_axis=0, concat_a...  13.5 us
  transfers between devices with their start and end apart: 11, of which 9 were waited for; matrix products, arithmetic and copies ran while one was open for 23% of the time, Pallas kernels for 0%

commit v1 on v0

v1 whole, which is shorter than its diff:
```python
import functools

import numpy as np
import jax
import jax.numpy as jnp
import ml_dtypes
from jax import lax
from jax.experimental import pallas as pl
from jax.experimental.pallas import tpu as pltpu
from jax.sharding import PartitionSpec as P

K1 = 72
GROUP = 8


def fourier_tables(seqs, rows):
    total = 2 * seqs * rows
    fine = 128
    coarse = total // fine
    half = coarse // 2
    per = rows // fine
    n1 = (np.arange(seqs)[None, :] * per + np.arange(per)[:, None]).reshape(-1)
    k1 = np.arange(half + 1)
    ang = 2 * np.pi * ((k1[:, None] * n1[None, :]) % coarse) / coarse
    pad = ((0, K1 - half - 1), (0, 0))
    first = np.concatenate([np.pad(np.cos(ang), pad), np.pad(-np.sin(ang), pad)])
    weight = np.where((k1 == 0) | (k1 == half), 1.0, 2.0)[:, None]
    last = np.concatenate([np.pad(weight * np.cos(ang), pad), np.pad(-weight * np.sin(ang), pad)]).T
    n2 = np.arange(fine)
    tw = 2 * np.pi * (k1[:, None] * n2[None, :]) / total
    tw_cos, tw_sin = np.pad(np.cos(tw), pad), np.pad(np.sin(tw), pad)
    ang2 = 2 * np.pi * ((n2[:, None] * n2[None, :]) % fine) / fine
    c, s = np.cos(ang2), np.sin(ang2)
    forward = np.block([[c, -s], [s, c]])
    backward = np.block([[c, s], [-s, c]])
    bf = ml_dtypes.bfloat16
    twiddle = np.stack([tw_cos, tw_sin]).astype(np.float32)
    return first.astype(bf), twiddle, forward.astype(bf), backward.astype(bf), last.astype(bf)


def spectrum_of(xs, base, seqs, chans, first, tw, forward):
    cols = []
    for i in range(GROUP):
        cols.append(jnp.concatenate([xs[p, pl.ds(base + i, seqs, stride=chans), :] for p in range(xs.shape[0])], axis=0))
    x = jnp.concatenate(cols, axis=1).astype(jnp.bfloat16)
    s = jnp.dot(first[...], x, preferred_element_type=jnp.float32)
    tc, ts = tw[0], tw[1]
    z = []
    for i in range(GROUP):
        re, im = s[:K1, i * 128:(i + 1) * 128], s[K1:, i * 128:(i + 1) * 128]
        z.append(jnp.concatenate([re * tc + im * ts, im * tc - re * ts], axis=1))
    z = jnp.concatenate(z, axis=0).astype(jnp.bfloat16)
    return jnp.dot(z, forward[...], preferred_element_type=jnp.float32)


def filter_kernel(seqs, chans, x_ref, first, tw, forward, out, xs):
    for p in range(xs.shape[0]):
        xs[p] = x_ref[:, p * 128:(p + 1) * 128].astype(jnp.float32)
    @pl.loop(0, chans // GROUP)
    def _(g):
        q = spectrum_of(xs, g * GROUP, seqs, chans, first, tw, forward)
        out[pl.ds(pl.multiple_of(g * (GROUP * K1), GROUP * K1), GROUP * K1), :] = q


def conv_kernel(seqs, chans, scale, x_ref, h_ref, first, tw, forward, backward, last, out, xs, ys):
    for p in range(xs.shape[0]):
        xs[p] = x_ref[:, p * 128:(p + 1) * 128].astype(jnp.float32)
    @pl.loop(0, chans // GROUP)
    def _(g):
        q = spectrum_of(xs, g * GROUP, seqs, chans, first, tw, forward)
        h = h_ref[pl.ds(pl.multiple_of(g * (GROUP * K1), GROUP * K1), GROUP * K1), :]
        qr, qi, hr, hi = q[:, :128], q[:, 128:], h[:, :128], h[:, 128:]
        p = jnp.concatenate([qr * hr - qi * hi, qr * hi + qi * hr], axis=1).astype(jnp.bfloat16)
        u = jnp.dot(p, backward[...], preferred_element_type=jnp.float32)
        tc, ts = tw[0] * scale, tw[1] * scale
        v = []
        for i in range(GROUP):
            re, im = u[i * K1:(i + 1) * K1, :128], u[i * K1:(i + 1) * K1, 128:]
            v.append(jnp.concatenate([re * tc - im * ts, im * tc + re * ts], axis=0))
        v = jnp.concatenate(v, axis=1).astype(jnp.bfloat16)
        y = jnp.dot(last[...], v, preferred_element_type=jnp.float32)
        for i in range(GROUP):
            yi = y[:, i * 128:(i + 1) * 128]
            for p in range(ys.shape[0]):
                ys[p, pl.ds(g * GROUP + i, seqs, stride=chans), :] = yi[p * seqs:(p + 1) * seqs]
    for p in range(ys.shape[0]):
        out[:, p * 128:(p + 1) * 128] = ys[p].astype(jnp.bfloat16)


def whole():
    return pl.BlockSpec(memory_space=pltpu.VMEM)

VM = 56 * 1024 * 1024

def filter_spectrum(x, tables, seqs):
    rows = x.shape[1]
    chans = x.shape[0] // seqs
    first, tw, forward, _, _ = tables
    return pl.pallas_call(
        functools.partial(filter_kernel, seqs, chans),
        out_shape=jax.ShapeDtypeStruct((chans * K1, 256), jnp.float32),
        in_specs=[whole()] * 4, out_specs=whole(),
        scratch_shapes=[pltpu.VMEM((x.shape[1] // 128, x.shape[0], 128), jnp.float32)],
        compiler_params=pltpu.CompilerParams(vmem_limit_bytes=VM),
        name="filter_spectrum",
        cost_estimate=pl.CostEstimate(flops=4_000_000_000, bytes_accessed=4_000_000, transcendentals=0),
    )(x, first, tw, forward)


def convolve(x, spec, tables, seqs):
    rows = x.shape[1]
    chans = x.shape[0] // seqs
    first, tw, forward, backward, last = tables
    return pl.pallas_call(
        functools.partial(conv_kernel, seqs, chans, 1.0 / (2 * seqs * rows)),
        out_shape=jax.ShapeDtypeStruct(x.shape, jnp.bfloat16),
        in_specs=[whole()] * 7, out_specs=whole(),
        scratch_shapes=[pltpu.VMEM((x.shape[1] // 128, x.shape[0], 128), jnp.float32)] * 2,
        compiler_params=pltpu.CompilerParams(vmem_limit_bytes=VM),
        name="convolve",
        cost_estimate=pl.CostEstimate(flops=5_000_000_000, bytes_accessed=4_000_000, transcendentals=0),
    )(x, spec, first, tw, forward, backward, last)


def shifted(array, axis, by):
    count = lax.axis_size(axis)
    pairs = [(i, i + by) for i in range(count) if 0 <= i + by < count]
    return lax.ppermute(array, axis, pairs)


def ring(array, by):
    count = lax.axis_size("chan")
    return lax.ppermute(array, "chan", [(i, (i + 2 * by) % count) for i in range(count)])


def cross(array):
    count = lax.axis_size("chan")
    return lax.ppermute(array, "chan", [(i, i ^ 1) for i in range(count)])


def params(**more):
    return pltpu.CompilerParams(vmem_limit_bytes=VM, **more)


def transpose_kernel(x_ref, out):
    out[...] = x_ref[...].T.astype(jnp.bfloat16)


def transposed(x):
    return pl.pallas_call(
        transpose_kernel,
        out_shape=jax.ShapeDtypeStruct(x.shape[::-1], jnp.bfloat16),
        in_specs=[whole()], out_specs=whole(),
        compiler_params=params(), name="transposed",
        cost_estimate=pl.CostEstimate(flops=0, bytes_accessed=6 * x.size, transcendentals=0),
    )(x)


def halo_kernel(x_ref, w_ref, out):
    out[0] = jnp.dot(x_ref[...], w_ref[0], preferred_element_type=jnp.float32).astype(jnp.bfloat16)


def halo_projection(halo, weight):
    branches, model, width = weight.shape
    rows = halo.shape[0]
    return pl.pallas_call(
        halo_kernel,
        grid=(branches,),
        out_shape=jax.ShapeDtypeStruct((branches, rows, width), jnp.bfloat16),
        in_specs=[pl.BlockSpec((rows, model), lambda j: (0, 0)), pl.BlockSpec((1, model, width), lambda j: (j, 0, 0))],
        out_specs=pl.BlockSpec((1, rows, width), lambda j: (j, 0, 0)),
        compiler_params=params(), name="halo_projection",
        cost_estimate=pl.CostEstimate(flops=2 * rows * weight.size, bytes_accessed=2 * weight.size, transcendentals=0),
    )(halo, weight)


def round_kernel(pieces, has_acc, owners, *refs):
    refs = list(refs)
    acc = refs.pop(0)[0] if has_acc else None
    blocks = [[refs.pop(0)[...] for _ in range(n)] for n in pieces]
    weights = [refs.pop(0) for _ in pieces]
    out = refs[0]
    for block, weight in zip(blocks, weights):
        block = block[0] if len(block) == 1 else jnp.concatenate(block, axis=0)
        term = jnp.dot(block, weight[0], preferred_element_type=jnp.float32)
        acc = term if acc is None else acc + term
    out[0] = acc


def project_round(acc, blocks, owners, weight):
    branches, _, width = weight.shape
    rows = sum(b.shape[0] for b in blocks[0])
    depth = blocks[0][0].shape[1]
    acc_spec = pl.BlockSpec((1, rows, width), lambda j, o: (j, 0, 0))
    specs = [acc_spec] if acc is not None else []
    flat = [p for b in blocks for p in b]
    specs += [pl.BlockSpec(p.shape, lambda j, o: (0, 0)) for p in flat]
    specs += [pl.BlockSpec((1, depth, width), lambda j, o, k=k: (j, o[k], 0)) for k in range(len(blocks))]
    args = ([acc] if acc is not None else []) + flat + [weight] * len(blocks)
    return pl.pallas_call(
        functools.partial(round_kernel, [len(b) for b in blocks], acc is not None),
        out_shape=jax.ShapeDtypeStruct((branches, rows, width), jnp.float32),
        grid_spec=pltpu.PrefetchScalarGridSpec(num_scalar_prefetch=1, grid=(branches,), in_specs=specs, out_specs=acc_spec),
        compiler_params=params(), name="project_round",
        cost_estimate=pl.CostEstimate(flops=2 * len(blocks) * rows * depth * branches * width, bytes_accessed=2 * len(blocks) * depth * branches * width, transcendentals=0),
    )(owners, *args)


def signal_kernel(owners, acc, lo, hi, weight, halo, taps, signal_t, signal, gate_out):
    rows = acc.shape[1]
    block = jnp.concatenate([lo[...], hi[...]], axis=0)
    short = []
    for j in range(3):
        proj = acc[j] + jnp.dot(block, weight[j], preferred_element_type=jnp.float32)
        proj = proj.astype(jnp.bfloat16).astype(jnp.float32)
        ext = jnp.concatenate([halo[j].astype(jnp.float32)[8:], proj], axis=0)
        short.append(taps[0, j:j + 1] * ext[6:6 + rows] + taps[1, j:j + 1] * ext[7:7 + rows] + taps[2, j:j + 1] * proj)
    sig = short[2] * short[1]
    gate_out[...] = short[0]
    signal[...] = sig
    signal_t[...] = sig.T.astype(jnp.bfloat16)


def signal_of(acc, lo, hi, owners, weight, halo, taps):
    branches, _, width = weight.shape
    rows = acc.shape[1]
    depth = lo.shape[1]
    cols = 256
    col = lambda c, o: (0, c)
    cube = lambda c, o: (0, 0, c)
    return pl.pallas_call(
        signal_kernel,
        out_shape=(
            jax.ShapeDtypeStruct((width, rows), jnp.bfloat16),
            jax.ShapeDtypeStruct((rows, width), jnp.float32),
            jax.ShapeDtypeStruct((rows, width), jnp.float32),
        ),
        grid_spec=pltpu.PrefetchScalarGridSpec(
            num_scalar_prefetch=1, grid=(width // cols,),
            in_specs=[
                pl.BlockSpec((branches, rows, cols), cube),
                pl.BlockSpec(lo.shape, lambda c, o: (0, 0)),
                pl.BlockSpec(hi.shape, lambda c, o: (0, 0)),
                pl.BlockSpec((branches, depth, cols), lambda c, o: (0, o[0], c)),
                pl.BlockSpec((branches, halo.shape[1], cols), cube),
                pl.BlockSpec((3, branches, cols), cube),
            ],
            out_specs=[pl.BlockSpec((cols, rows), lambda c, o: (c, 0)), pl.BlockSpec((rows, cols), col), pl.BlockSpec((rows, cols), col)],
        ),
        compiler_params=params(), name="signal_of",
    )(owners, acc, lo, hi, weight, halo, taps)


def gate_kernel(owners, conv, signal, gate_out, skip, w0, w1, w2, w3, gated, o0, o1, o2, o3):
    total = conv[...].astype(jnp.float32).T + skip[...] * signal[...]
    g = (total * gate_out[...]).astype(jnp.bfloat16)
    gated[...] = g
    for w, o in ((w0, o0), (w1, o1), (w2, o2), (w3, o3)):
        o[...] = jnp.dot(g, w[...], preferred_element_type=jnp.float32).astype(jnp.bfloat16)


def gate_and_project(part, parts, conv, signal, gate_out, skip, owners, weight):
    width, rows = conv.shape
    cols = weight.shape[1] // 8
    rows //= parts
    row = lambda i, o: (part, 0)
    out = pl.BlockSpec((rows, cols), lambda i, o: (0, 0))
    return pl.pallas_call(
        gate_kernel,
        out_shape=(jax.ShapeDtypeStruct((rows, width), jnp.bfloat16),) + (jax.ShapeDtypeStruct((rows, cols), jnp.bfloat16),) * 4,
        grid_spec=pltpu.PrefetchScalarGridSpec(
            num_scalar_prefetch=1, grid=(1,),
            in_specs=[
                pl.BlockSpec((width, rows), lambda i, o: (0, part)),
                pl.BlockSpec((rows, width), row),
                pl.BlockSpec((rows, width), row),
                pl.BlockSpec((1, width), lambda i, o: (0, 0)),
            ] + [pl.BlockSpec((width, cols), lambda i, o, k=k: (0, o[k])) for k in range(4)],
            out_specs=[pl.BlockSpec((rows, width), lambda i, o: (0, 0))] + [out] * 4,
        ),
        compiler_params=params(), name="gate_and_project",
        cost_estimate=pl.CostEstimate(flops=8 * rows * width * cols, bytes_accessed=8 * width * cols, transcendentals=0),
    )(owners, conv, signal, gate_out, skip, weight, weight, weight, weight)


def out_kernel(owners, g, w0, w1, w2, w3, o0, o1, o2, o3):
    for w, o in ((w0, o0), (w1, o1), (w2, o2), (w3, o3)):
        o[...] = jnp.dot(g[...], w[...], preferred_element_type=jnp.float32).astype(jnp.bfloat16)


def project_out(gated, owners, weight):
    rows, width = gated.shape
    cols = weight.shape[1] // 8
    out = pl.BlockSpec((rows, cols), lambda i, o: (0, 0))
    return pl.pallas_call(
        out_kernel,
        out_shape=(jax.ShapeDtypeStruct((rows, cols), jnp.bfloat16),) * 4,
        grid_spec=pltpu.PrefetchScalarGridSpec(
            num_scalar_prefetch=1, grid=(1,),
            in_specs=[pl.BlockSpec((rows, width), lambda i, o: (0, 0))]
            + [pl.BlockSpec((width, cols), lambda i, o, k=k: (0, o[k])) for k in range(4)],
            out_specs=[out] * 4,
        ),
        compiler_params=params(), name="project_out",
        cost_estimate=pl.CostEstimate(flops=8 * rows * width * cols, bytes_accessed=8 * width * cols, transcendentals=0),
    )(owners, gated, weight, weight, weight, weight)


def added(*terms):
    return sum(t.astype(jnp.float32) for t in terms).astype(jnp.bfloat16)


def shards(tables, tokens, in_weight, short_weight, long_filter, skip_gain, out_weight):
    seqs = lax.axis_size("seq")
    count = lax.axis_size("chan")
    rows, width = tokens.shape
    half = rows // 2
    me = lax.axis_index("chan")
    at = lambda dy, dx: jnp.bitwise_xor((me + 2 * dy) % count, dx).astype(jnp.int32)
    ids = lambda *pairs: jnp.stack([at(dy, dx) for dy, dx in pairs])
    weight = jnp.transpose(in_weight, (1, 0, 2))

    fil = lax.all_to_all(transposed(long_filter), "seq", 0, 0, tiled=True)
    below, above, side = ring(tokens, 1), ring(tokens, -1), cross(tokens)
    side_below, side_above = ring(side, 1), ring(side, -1)
    far_lo, far_hi = ring(below[:half], 1), ring(above[half:], -1)
    side_far_lo, side_far_hi = ring(side_below[:half], 1), ring(side_above[half:], -1)
    halo = lax.all_gather(shifted(tokens[rows - 16:], "seq", 1), "chan", axis=1, tiled=True)

    spec = filter_spectrum(fil, tables, seqs)
    acc = project_round(None, [[tokens]], ids((0, 0)), weight)
    halo = halo_projection(halo, weight)
    acc = project_round(acc, [[below], [above], [side]], ids((-1, 0), (1, 0), (0, 1)), weight)
    acc = project_round(acc, [[side_below], [side_above], [far_lo, far_hi]], ids((-1, 1), (1, 1), (2, 0)), weight)
    signal_t, signal, gate_out = signal_of(acc, side_far_lo, side_far_hi, ids((2, 1)), weight, halo, short_weight)

    conv = convolve(lax.all_to_all(signal_t, "seq", 0, 0, tiled=True), spec, tables, seqs)
    conv = lax.all_to_all(conv, "seq", 0, 0, tiled=True)

    skip = skip_gain.reshape(1, width)
    near = ids((2, 0), (1, 0), (-1, 0), (0, 0))
    wide = ids((2, 1), (1, 1), (-1, 1), (0, 1))
    g_lo, *lo = gate_and_project(0, 2, conv, signal, gate_out, skip, wide, out_weight)
    g_hi, *hi = gate_and_project(1, 2, conv, signal, gate_out, skip, wide, out_weight)

    def reduced(lo, hi):
        far_lo, up_lo, down_lo, own_lo = lo
        far_hi, up_hi, down_hi, own_hi = hi
        from_lo, from_hi = ring(far_lo, 1), ring(far_hi, -1)
        here_hi, here_lo = ring(up_hi, 1), ring(down_lo, -1)
        sum_lo = ring(added(up_lo, from_lo), 1)
        sum_hi = ring(added(down_hi, from_hi), -1)
        return (own_lo, here_lo, sum_lo), (own_hi, here_hi, sum_hi)

    wide_lo, wide_hi = reduced(lo, hi)
    wide_lo, wide_hi = cross(added(*wide_lo)), cross(added(*wide_hi))
    near_lo, near_hi = reduced(project_out(g_lo, near, out_weight), project_out(g_hi, near, out_weight))
    return jnp.concatenate([added(*near_lo, wide_lo), added(*near_hi, wide_hi)], axis=0)


def solution(mesh):
    in_specs = (
        P("seq", "chan"),
        P(None, None, "chan"),
        P(None, None, "chan"),
        P("seq", "chan"),
        P("chan"),
        P("chan", None),
    )
    def run(*args):
        seqs = mesh.shape["seq"]
        tables = tuple(jnp.asarray(t) for t in fourier_tables(seqs, args[0].shape[0] // seqs))
        body = functools.partial(shards, tables)
        return jax.shard_map(body, mesh=mesh, in_specs=in_specs, out_specs=P("seq", "chan"), check_vma=False)(*args)
    return run
```

time: 582 us -> 207 us (0.36); the launches traced: 575 us -> 206 us
  waiting for transfers between devices: 246 us -> 47.1 us
  matrix products: 162 us -> 0 us
  local copies, waits for them, and re-layouts: 85.1 us -> 4.62 us
  Pallas kernels: 0 us -> 61.2 us
  blocking collectives: 13.5 us -> 36.4 us
  between operations: 14.1 us -> 0.37 us
    dot_general x20 -> x0, matrix products: 162 us -> none  [the longest x18 144 us: mult(): return jnp.einsum(form, left, right, precision=lax.Precision.HIGHEST)]
    all_to_all x8 -> x3, waiting for transfers between devices: 105 us -> 16.6 us  [the longest x1 10.2 us: shards(): conv = lax.all_to_all(conv, 'seq', 0, 0, tiled=True)]
    reduce_scatter x1 -> x0, waiting for transfers between devices: 81.2 us -> none  [shards(): lax.psum_scatter(term.astype(jnp.bfloat16), 'chan', scatter_dimension=1,...]
    pallas_call x0 -> x12, Pallas kernels: none -> 61.2 us  [the longest x3 21.1 us: project_round(): pl.pallas_call(functools.partial(round_kernel, [len(b) for b in blocks],...]
    all_gather x1 -> x0, waiting for transfers between devices: 58.1 us -> none  [shards(): lax.all_gather(tokens, 'chan', axis=1, tiled=True)]
    all_gather x0 -> x1, blocking collectives: none -> 36.4 us  [shards(): lax.all_gather(shifted(tokens[rows - 16:], 'seq', 1), 'chan', axis=1, til...]
    ppermute x0 -> x23, starting transfers between devices: none -> 33.4 us  [the longest x20 28.5 us: ring(): lax.ppermute(array, 'chan', [(i, (i + 2 * by) % count) for i in range(cou...]
    ppermute x0 -> x23, waiting for transfers between devices: none -> 30.5 us  [the longest x20 19.2 us: ring(): lax.ppermute(array, 'chan', [(i, (i + 2 * by) % count) for i in range(cou...]
  transfers between devices with their start and end apart: 11 -> 27, of which waited for: 9 -> 8; matrix products, arithmetic and copies ran while one was open for 23% -> 2% of each run, Pallas kernels for 0% -> 25%
where the time goes in v1:
time: 207 us; the launch traced here: 206 us
  Pallas kernels  61.2 us (30%)
  starting transfers between devices  52.2 us (25%)
  waiting for transfers between devices  47.1 us (23%)
  blocking collectives  36.4 us (18%)
  local copies, waits for them, and re-layouts  4.62 us (2%)
  other arithmetic  4.03 us (2%)
    all_gather x1, blocking collectives, shards(): lax.all_gather(shifted(tokens[rows - 16:], 'seq', 1), 'chan', axis=1, til...  36.4 us
    ppermute x20, starting transfers between devices, ring(): lax.ppermute(array, 'chan', [(i, (i + 2 * by) % count) for i in range(cou...  28.5 us
    pallas_call x3, Pallas kernels, project_round(): pl.pallas_call(functools.partial(round_kernel, [len(b) for b in blocks],...  21.1 us
    ppermute x20, waiting for transfers between devices, ring(): lax.ppermute(array, 'chan', [(i, (i + 2 * by) % count) for i in range(cou...  19.2 us
    ppermute x3, waiting for transfers between devices, cross(): return lax.ppermute(array, 'chan', [(i, i ^ 1) for i in range(count)])  11.3 us
    all_to_all x1, waiting for transfers between devices, shards(): conv = lax.all_to_all(conv, 'seq', 0, 0, tiled=True)  10.2 us
    all_to_all x1, starting transfers between devices, shards(): fil = lax.all_to_all(transposed(long_filter), 'seq', 0, 0, tiled=True)  8.36 us
    pallas_call x2, Pallas kernels, gate_and_project(): pl.pallas_call(gate_kernel, out_shape=(jax.ShapeDtypeStruct((rows, width)...  8.12 us
  transfers between devices with their start and end apart: 27, of which 8 were waited for; matrix products, arithmetic and copies ran while one was open for 2% of the time, Pallas kernels for 25%

profile of v1, /device:TPU:0, one launch (start us, length us, event | category | flops | bytes accessed | tf_op | source)
XLA Modules:
  0.0 205.9 jit_solution(15477801215656225038)
XLA Ops:
  0.0 3.1 %collective-permute-start.2 = (bf16[512,512]{1,0:T(8,128)(2,1)}, bf16[512,512]{1,0:T(8,128)(2,1)S(1)}, u32[]{:S(2)}, u32[]{:S(2)}) collective-permute-start(bf16[512,512]{1,0:T(8,128)(2,1)} %refs_0_.1), channel_id=1, source_target_pairs={{0,1},{1,0},{2,3},{3,2},{4,5},{5,4},{6,7},{7,6},{8,9},{9,8},{10,11... | collective-permute-start | bytes 1572872 | tf_op jit(solution)/shard_map/ppermute | solution.py:138
  3.1 1.6 collective-permute-start
  4.7 1.7 collective-permute-start.1
  6.3 8.9 %collective-permute-done.2.refs_3_ = bf16[512,512]{1,0:T(8,128)(2,1)S(1)} collective-permute-done((bf16[512,512]{1,0:T(8,128)(2,1)}, bf16[512,512]{1,0:T(8,128)(2,1)S(1)}, u32[]{:S(2)}, u32[]{:S(2)}) %collective-permute-start.2) | collective-permute-done | bytes 524320 | tf_op jit(solution)/shard_map/ppermute | solution.py:138
  15.2 1.8 collective-permute-start.3
  17.0 1.4 collective-permute-start.4
  18.5 0.7 slice.19
  19.2 1.3 collective-permute-start.9
  20.5 2.2 %transposed.1 = bf16[512,512]{1,0:T(8,128)(2,1)} custom-call(f32[512,512]{1,0:T(8,128)} %x_ref.1), custom_call_target="tpu_custom_call" | custom-call | bytes 1572864 | tf_op jit(solution)/shard_map/transposed/pallas_call | solution.py:150
  22.7 8.4 %all-to-all-start.1 = ((bf16[16,32,512]{2,1,0:T(8,128)(2,1)}), bf16[16,32,512]{2,1,0:T(8,128)(2,1)S(1)}, u32[]{:S(2)}, u32[]{:S(2)}) async-start(bf16[16,32,512]{2,1,0:T(8,128)(2,1)} %bitcast.27), calls=%async_computation.1 | async-start | bytes 1048576 | tf_op jit(solution)/shard_map/all_to_all | solution.py:323
  32.3 4.5 %project_round.3.refs_0_ = f32[3,512,512]{2,1,0:T(8,128)} custom-call(s32[1]{0:T(128)} %bitcast.3.owners, bf16[512,512]{1,0:T(8,128)(2,1)} %refs_0_.1, bf16[3,4096,512]{2,1,0:T(8,128)(2,1)} %bitcast.16), custom_call_target="tpu_custom_call" | custom-call | flops 805306368 | bytes 1572864 | tf_op jit(solution)/shard_map/project_round/pallas_call | solution.py:200
  37.3 2.9 %collective-permute-start.6 = (bf16[256,512]{1,0:T(8,128)(2,1)S(1)}, bf16[256,512]{1,0:T(8,128)(2,1)S(1)}, u32[]{:S(2)}, u32[]{:S(2)}) collective-permute-start(bf16[256,512]{1,0:T(8,128)(2,1)S(1)} %slice.21), channel_id=1, source_target_pairs={{0,6},{1,7},{2,0},{3,1},{4,2},{5,3},{6,4},{7,5},{8,14},{9,15},{10,... | collective-permute-start | bytes 786440 | tf_op jit(solution)/shard_map/ppermute | solution.py:133
  40.3 36.4 %all_gather.3.x_ref = bf16[16,4096]{1,0:T(8,128)(2,1)} all-gather(bf16[16,512]{1,0:T(8,128)(2,1)S(1)} %collective-permute-done.9), channel_id=1, replica_groups=mesh['seq'=16,'chan'=8] {'chan'}, dimensions={1}, use_global_device_ids=true | all-gather | bytes 147456 | tf_op jit(solution)/shard_map/all_gather | solution.py:328
  76.7 6.5 %halo_projection.1.halo = bf16[3,16,512]{2,1,0:T(8,128)(2,1)} custom-call(bf16[16,4096]{1,0:T(8,128)(2,1)} %all_gather.3.x_ref, bf16[3,4096,512]{2,1,0:T(8,128)(2,1)} %bitcast.17), custom_call_target="tpu_custom_call" | custom-call | flops 201326592 | bytes 12582912 | tf_op jit(solution)/shard_map/halo_projection/pallas_call | solution.py:166
  83.3 3.3 %collective-permute-start.8 = (bf16[256,512]{1,0:T(8,128)(2,1)S(1)}, bf16[256,512]{1,0:T(8,128)(2,1)S(1)}, u32[]{:S(2)}, u32[]{:S(2)}) collective-permute-start(bf16[256,512]{1,0:T(8,128)(2,1)S(1)} %slice.23), channel_id=1, source_target_pairs={{0,6},{1,7},{2,0},{3,1},{4,2},{5,3},{6,4},{7,5},{8,14},{9,15},{10,... | collective-permute-start | bytes 786440 | tf_op jit(solution)/shard_map/ppermute | solution.py:133
  86.6 8.3 %project_round.4.refs_0_ = f32[3,512,512]{2,1,0:T(8,128)} custom-call(s32[3]{0:T(128)} %pad_add_fusion.3.owners, f32[3,512,512]{2,1,0:T(8,128)} %project_round.3.refs_0_, bf16[512,512]{1,0:T(8,128)(2,1)} %copy-done.2, bf16[512,512]{1,0:T(8,128)(2,1)} %copy-done.4, bf16[512,512]{1,0:T(8,128)(2,1)} %copy-done.5, bf16[3,4096,512]{2,1,0:T(8,128)(2,1)} %bitcast.18, ...), custom_call_target="tpu_custom_call" | custom-call | flops 2415919104 | bytes 4718592 | tf_op jit(solution)/shard_map/project_round/pallas_call | solution.py:200
  95.0 0.7 copy-done.8
  95.7 0.7 copy-done.9
  96.4 8.3 %project_round.5.acc = f32[3,512,512]{2,1,0:T(8,128)} custom-call(s32[3]{0:T(128)} %pad_add_fusion.2.owners, f32[3,512,512]{2,1,0:T(8,128)} %project_round.4.refs_0_, bf16[512,512]{1,0:T(8,128)(2,1)} %copy-done.1, bf16[512,512]{1,0:T(8,128)(2,1)} %copy-done.3, bf16[256,512]{1,0:T(8,128)(2,1)} %copy-done.8, bf16[256,512]{1,0:T(8,128)(2,1)} %copy-done.9, ...), custom_call_target="tpu_custom_call" | custom-call | flops 2415919104 | bytes 4718592 | tf_op jit(solution)/shard_map/project_round/pallas_call | solution.py:200
  104.7 0.7 copy-done.10
  105.5 5.1 %signal_of.1 = (bf16[512,512]{1,0:T(8,128)(2,1)}, f32[512,512]{1,0:T(8,128)}, f32[512,512]{1,0:T(8,128)}) custom-call(s32[1]{0:T(128)} %bitcast.4.owners, f32[3,512,512]{2,1,0:T(8,128)} %project_round.5.acc, bf16[256,512]{1,0:T(8,128)(2,1)} %copy-done.10, bf16[256,512]{1,0:T(8,128)(2,1)} %copy-done.11, bf16[3,4096,512]{2,1,0:T(8,128)(2,1)} %bitcast.24, ...), custom_call_target="tpu_custom_call" | custom-call | tf_op jit(solution)/shard_map/signal_of/pallas_call | solution.py:231
  110.6 5.6 %all-to-all-start = ((bf16[16,32,512]{2,1,0:T(8,128)(2,1)}), bf16[16,32,512]{2,1,0:T(8,128)(2,1)S(1)}, u32[]{:S(2)}, u32[]{:S(2)}) async-start(bf16[16,32,512]{2,1,0:T(8,128)(2,1)} %bitcast.29), calls=%async_computation | async-start | bytes 1048576 | tf_op jit(solution)/shard_map/all_to_all | solution.py:337
  116.2 4.4 %filter_spectrum.1.h_ref = f32[2304,256]{1,0:T(8,128)} custom-call(bf16[512,512]{1,0:T(8,128)(2,1)} %bitcast.28, bf16[144,64]{1,0:T(8,128)(2,1)} %constant.71.clone.first, f32[2,72,128]{2,1,0:T(8,128)} %constant.72.clone.tw, bf16[256,256]{1,0:T(8,128)(2,1)} %constant.73.clone.forward), custom_call_target="tpu_custom_call" | custom-call | flops 4000000000 | bytes 4000000 | tf_op jit(solution)/shard_map/filter_spectrum/pallas_call | solution.py:99
  120.6 6.4 %all-to-all-done = bf16[16,32,512]{2,1,0:T(8,128)(2,1)S(1)} async-done(((bf16[16,32,512]{2,1,0:T(8,128)(2,1)}), bf16[16,32,512]{2,1,0:T(8,128)(2,1)S(1)}, u32[]{:S(2)}, u32[]{:S(2)}) %all-to-all-start) | async-done | bytes 524320 | tf_op jit(solution)/shard_map/all_to_all | solution.py:337
  127.0 0.8 copy-done.7
  127.8 6.1 %convolve.1 = bf16[512,512]{1,0:T(8,128)(2,1)} custom-call(bf16[512,512]{1,0:T(8,128)(2,1)} %bitcast.30, f32[2304,256]{1,0:T(8,128)} %filter_spectrum.1.h_ref, bf16[144,64]{1,0:T(8,128)(2,1)} %constant.71.clone.first, f32[2,72,128]{2,1,0:T(8,128)} %constant.72.clone.tw, bf16[256,256]{1,0:T(8,128)(2,1)} %constant.73.clone.forward, ...), custom_call_target="tpu_custom_call" | custom-call | flops 5000000000 | bytes 4000000 | tf_op jit(solution)/shard_map/convolve/pallas_call | solution.py:114
  133.9 3.6 %all-to-all-start.2 = ((bf16[16,32,512]{2,1,0:T(8,128)(2,1)}), bf16[16,32,512]{2,1,0:T(8,128)(2,1)S(1)}, u32[]{:S(2)}, u32[]{:S(2)}) async-start(bf16[16,32,512]{2,1,0:T(8,128)(2,1)} %bitcast.31), calls=%async_computation.2 | async-start | bytes 1048576 | tf_op jit(solution)/shard_map/all_to_all | solution.py:338
  138.1 10.2 %all-to-all-done.2 = bf16[16,32,512]{2,1,0:T(8,128)(2,1)S(1)} async-done(((bf16[16,32,512]{2,1,0:T(8,128)(2,1)}), bf16[16,32,512]{2,1,0:T(8,128)(2,1)S(1)}, u32[]{:S(2)}, u32[]{:S(2)}) %all-to-all-start.2) | async-done | bytes 524320 | tf_op jit(solution)/shard_map/all_to_all | solution.py:338
  148.3 0.8 copy-done
  149.1 4.1 %gate_and_project.2 = (bf16[256,512]{1,0:T(8,128)(2,1)}, bf16[256,512]{1,0:T(8,128)(2,1)}, bf16[256,512]{1,0:T(8,128)(2,1)}, bf16[256,512]{1,0:T(8,128)(2,1)}, bf16[256,512]{1,0:T(8,128)(2,1)}) custom-call(s32[4]{0:T(128)} %pad_add_fusion.1.owners, bf16[512,512]{1,0:T(8,128)(2,1)} %bitcast.25, f32[512,512]{1,0:T(8,128)} %get-tuple-element.27.signal, ...), custom_call_target="tpu_custom_call" | custom-call | flops 536870912 | bytes 2097152 | tf_op jit(solution)/shard_map/gate_and_project/pallas_call | solution.py:268
  153.8 3.8 %project_out.2 = (bf16[256,512]{1,0:T(8,128)(2,1)}, bf16[256,512]{1,0:T(8,128)(2,1)}, bf16[256,512]{1,0:T(8,128)(2,1)}, bf16[256,512]{1,0:T(8,128)(2,1)}) custom-call(s32[4]{0:T(128)} %pad_add_fusion.owners, bf16[256,512]{1,0:T(8,128)(2,1)} %get-tuple-element.29.g, bf16[512,4096]{1,0:T(8,128)(2,1)} %w3.7, bf16[512,4096]{1,0:T(8,128)(2,1)} %w3.7, ...), custom_call_target="tpu_custom_call" | custom-call | flops 536870912 | bytes 2097152 | tf_op jit(solution)/shard_map/project_out/pallas_call | solution.py:295
  157.6 3.3 %collective-permute-start.13 = (bf16[256,512]{1,0:T(8,128)(2,1)S(1)}, bf16[256,512]{1,0:T(8,128)(2,1)S(1)}, u32[]{:S(2)}, u32[]{:S(2)}) collective-permute-start(bf16[256,512]{1,0:T(8,128)(2,1)S(1)} %copy-done.21), channel_id=1, source_target_pairs={{0,6},{1,7},{2,0},{3,1},{4,2},{5,3},{6,4},{7,5},{8,14},{9,15},{10,... | collective-permute-start | bytes 786440 | tf_op jit(solution)/shard_map/ppermute | solution.py:133
  160.9 2.0 collective-permute-start.10
  162.9 4.1 %gate_and_project.3 = (bf16[256,512]{1,0:T(8,128)(2,1)}, bf16[256,512]{1,0:T(8,128)(2,1)}, bf16[256,512]{1,0:T(8,128)(2,1)}, bf16[256,512]{1,0:T(8,128)(2,1)}, bf16[256,512]{1,0:T(8,128)(2,1)}) custom-call(s32[4]{0:T(128)} %pad_add_fusion.1.owners, bf16[512,512]{1,0:T(8,128)(2,1)} %bitcast.26, f32[512,512]{1,0:T(8,128)} %get-tuple-element.27.signal, ...), custom_call_target="tpu_custom_call" | custom-call | flops 536870912 | bytes 2097152 | tf_op jit(solution)/shard_map/gate_and_project/pallas_call | solution.py:268
  167.0 3.8 %project_out.3 = (bf16[256,512]{1,0:T(8,128)(2,1)}, bf16[256,512]{1,0:T(8,128)(2,1)}, bf16[256,512]{1,0:T(8,128)(2,1)}, bf16[256,512]{1,0:T(8,128)(2,1)}) custom-call(s32[4]{0:T(128)} %pad_add_fusion.owners, bf16[256,512]{1,0:T(8,128)(2,1)} %get-tuple-element.38.g, bf16[512,4096]{1,0:T(8,128)(2,1)} %w3.7, bf16[512,4096]{1,0:T(8,128)(2,1)} %w3.7, ...), custom_call_target="tpu_custom_call" | custom-call | flops 536870912 | bytes 2097152 | tf_op jit(solution)/shard_map/project_out/pallas_call | solution.py:295
  171.1 2.1 %collective-permute-start.15 = (bf16[256,512]{1,0:T(8,128)(2,1)S(1)}, bf16[256,512]{1,0:T(8,128)(2,1)S(1)}, u32[]{:S(2)}, u32[]{:S(2)}) collective-permute-start(bf16[256,512]{1,0:T(8,128)(2,1)S(1)} %add_convert_fusion.6), channel_id=1, source_target_pairs={{0,2},{1,3},{2,4},{3,5},{4,6},{5,7},{6,0},{7,1},{8,10},{9,11},{10,... | collective-permute-start | bytes 786440 | tf_op jit(solution)/shard_map/ppermute | solution.py:133
  173.3 9.9 %collective-permute-done.21 = bf16[256,512]{1,0:T(8,128)(2,1)S(1)} collective-permute-done((bf16[256,512]{1,0:T(8,128)(2,1)S(1)}, bf16[256,512]{1,0:T(8,128)(2,1)S(1)}, u32[]{:S(2)}, u32[]{:S(2)}) %collective-permute-start.21) | collective-permute-done | bytes 262176 | tf_op jit(solution)/shard_map/ppermute | solution.py:133
  183.2 1.2 collective-permute-start.20
  184.5 1.8 collective-permute-start.12
  186.3 1.5 collective-permute-start.22
  187.9 0.9 collective-permute-start.16
  188.9 4.7 %collective-permute-done.20 = bf16[256,512]{1,0:T(8,128)(2,1)S(1)} collective-permute-done((bf16[256,512]{1,0:T(8,128)(2,1)S(1)}, bf16[256,512]{1,0:T(8,128)(2,1)S(1)}, u32[]{:S(2)}, u32[]{:S(2)}) %collective-permute-start.20) | collective-permute-done | bytes 262176 | tf_op jit(solution)/shard_map/ppermute | solution.py:133
  193.7 3.2 %collective-permute-start.19 = (bf16[256,512]{1,0:T(8,128)(2,1)S(1)}, bf16[256,512]{1,0:T(8,128)(2,1)S(1)}, u32[]{:S(2)}, u32[]{:S(2)}) collective-permute-start(bf16[256,512]{1,0:T(8,128)(2,1)S(1)} %add_convert_fusion.3), channel_id=1, source_target_pairs={{0,6},{1,7},{2,0},{3,1},{4,2},{5,3},{6,4},{7,5},{8,14},{9,15},{10,... | collective-permute-start | bytes 786440 | tf_op jit(solution)/shard_map/ppermute | solution.py:133
  197.0 0.9 collective-permute-start.23
  197.9 1.3 collective-permute-done.12
  199.4 3.2 %collective-permute-done.17 = bf16[256,512]{1,0:T(8,128)(2,1)S(1)} collective-permute-done((bf16[256,512]{1,0:T(8,128)(2,1)S(1)}, bf16[256,512]{1,0:T(8,128)(2,1)S(1)}, u32[]{:S(2)}, u32[]{:S(2)}) %collective-permute-start.17) | collective-permute-done | bytes 262176 | tf_op jit(solution)/shard_map/ppermute | solution.py:133
  202.6 2.4 %collective-permute-done.23 = bf16[256,512]{1,0:T(8,128)(2,1)S(1)} collective-permute-done((bf16[256,512]{1,0:T(8,128)(2,1)S(1)}, bf16[256,512]{1,0:T(8,128)(2,1)S(1)}, u32[]{:S(2)}, u32[]{:S(2)}) %collective-permute-start.23) | collective-permute-done | bytes 262176 | tf_op jit(solution)/shard_map/ppermute | solution.py:138
  205.1 0.8 pad_maximum_fusion
  (85 shorter events, 4.2 us)
Async XLA Ops:
  0.0 15.2 %collective-permute-start.2 = (bf16[512,512]{1,0:T(8,128)(2,1)}, bf16[512,512]{1,0:T(8,128)(2,1)S(1)}, u32[]{:S(2)}, u32[]{:S(2)}) collective-permute-start(bf16[512,512]{1,0:T(8,128)(2,1)} %refs_0_.1), channel_id=1, source_target_pairs={{0,1},{1,0},{2,3},{3,2},{4,5},{5,4},{6,7},{7,6},{8,9},{9,8},{10,11... | collective-permute-start | bytes 1572872 | tf_op jit(solution)/shard_map/ppermute | solution.py:138
  3.1 33.7 %collective-permute-start = (bf16[512,512]{1,0:T(8,128)(2,1)}, bf16[512,512]{1,0:T(8,128)(2,1)S(1)}, u32[]{:S(2)}, u32[]{:S(2)}) collective-permute-start(bf16[512,512]{1,0:T(8,128)(2,1)} %refs_0_.1), channel_id=1, source_target_pairs={{0,2},{1,3},{2,4},{3,5},{4,6},{5,7},{6,0},{7,1},{8,10},{9,11},{10,... | collective-permute-start | bytes 1572872 | tf_op jit(solution)/shard_map/ppermute | solution.py:133
  4.7 32.6 %collective-permute-start.1 = (bf16[512,512]{1,0:T(8,128)(2,1)}, bf16[512,512]{1,0:T(8,128)(2,1)S(1)}, u32[]{:S(2)}, u32[]{:S(2)}) collective-permute-start(bf16[512,512]{1,0:T(8,128)(2,1)} %refs_0_.1), channel_id=1, source_target_pairs={{0,6},{1,7},{2,0},{3,1},{4,2},{5,3},{6,4},{7,5},{8,14},{9,15},{10,... | collective-permute-start | bytes 1572872 | tf_op jit(solution)/shard_map/ppermute | solution.py:133
  15.2 21.6 %copy-start.5 = (bf16[512,512]{1,0:T(8,128)(2,1)}, bf16[512,512]{1,0:T(8,128)(2,1)S(1)}, u32[]{:S(2)}) copy-start(bf16[512,512]{1,0:T(8,128)(2,1)S(1)} %collective-permute-done.2.refs_3_) | copy-start | bytes 1572868
  15.2 67.9 %collective-permute-start.3 = (bf16[512,512]{1,0:T(8,128)(2,1)S(1)}, bf16[512,512]{1,0:T(8,128)(2,1)S(1)}, u32[]{:S(2)}, u32[]{:S(2)}) collective-permute-start(bf16[512,512]{1,0:T(8,128)(2,1)S(1)} %collective-permute-done.2.refs_3_), channel_id=1, source_target_pairs={{0,2},{1,3},{2,4},{3,5},{4,6},{5,7},{6,0},{7,1},{8,10},{9,11},{10,... | collective-permute-start | bytes 1572872 | tf_op jit(solution)/shard_map/ppermute | solution.py:133
  17.0 66.2 %collective-permute-start.4 = (bf16[512,512]{1,0:T(8,128)(2,1)S(1)}, bf16[512,512]{1,0:T(8,128)(2,1)S(1)}, u32[]{:S(2)}, u32[]{:S(2)}) collective-permute-start(bf16[512,512]{1,0:T(8,128)(2,1)S(1)} %collective-permute-done.2.refs_3_), channel_id=1, source_target_pairs={{0,6},{1,7},{2,0},{3,1},{4,2},{5,3},{6,4},{7,5},{8,14},{9,15},{10,... | collective-permute-start | bytes 1572872 | tf_op jit(solution)/shard_map/ppermute | solution.py:133
  19.2 21.1 %collective-permute-start.9 = (bf16[16,512]{1,0:T(8,128)(2,1)S(1)}, bf16[16,512]{1,0:T(8,128)(2,1)S(1)}, u32[]{:S(2)}, u32[]{:S(2)}) collective-permute-start(bf16[16,512]{1,0:T(8,128)(2,1)S(1)} %slice.19), channel_id=1, source_target_pairs={{0,8},{8,16},{16,24},{24,32},{32,40},{40,48},{48,56},{56,64},{64,7... | collective-permute-start | bytes 49160 | tf_op jit(solution)/shard_map/ppermute | solution.py:128
  22.7 87.9 %all-to-all-start.1 = ((bf16[16,32,512]{2,1,0:T(8,128)(2,1)}), bf16[16,32,512]{2,1,0:T(8,128)(2,1)S(1)}, u32[]{:S(2)}, u32[]{:S(2)}) async-start(bf16[16,32,512]{2,1,0:T(8,128)(2,1)} %bitcast.27), calls=%async_computation.1 | async-start | bytes 1048576 | tf_op jit(solution)/shard_map/all_to_all | solution.py:323
  36.8 46.3 %copy-start.2 = (bf16[512,512]{1,0:T(8,128)(2,1)}, bf16[512,512]{1,0:T(8,128)(2,1)S(1)}, u32[]{:S(2)}) copy-start(bf16[512,512]{1,0:T(8,128)(2,1)S(1)} %collective-permute-done.refs_1_) | copy-start | bytes 1572868
  36.9 58.1 %collective-permute-start.5 = (bf16[256,512]{1,0:T(8,128)(2,1)S(1)}, bf16[256,512]{1,0:T(8,128)(2,1)S(1)}, u32[]{:S(2)}, u32[]{:S(2)}) collective-permute-start(bf16[256,512]{1,0:T(8,128)(2,1)S(1)} %slice.20), channel_id=1, source_target_pairs={{0,2},{1,3},{2,4},{3,5},{4,6},{5,7},{6,0},{7,1},{8,10},{9,11},{10,... | collective-permute-start | bytes 786440 | tf_op jit(solution)/shard_map/ppermute | solution.py:133
  37.3 45.8 %copy-start.4 = (bf16[512,512]{1,0:T(8,128)(2,1)}, bf16[512,512]{1,0:T(8,128)(2,1)S(1)}, u32[]{:S(2)}) copy-start(bf16[512,512]{1,0:T(8,128)(2,1)S(1)} %collective-permute-done.1.refs_2_) | copy-start | bytes 1572868
  37.3 57.6 %collective-permute-start.6 = (bf16[256,512]{1,0:T(8,128)(2,1)S(1)}, bf16[256,512]{1,0:T(8,128)(2,1)S(1)}, u32[]{:S(2)}, u32[]{:S(2)}) collective-permute-start(bf16[256,512]{1,0:T(8,128)(2,1)S(1)} %slice.21), channel_id=1, source_target_pairs={{0,6},{1,7},{2,0},{3,1},{4,2},{5,3},{6,4},{7,5},{8,14},{9,15},{10,... | collective-permute-start | bytes 786440 | tf_op jit(solution)/shard_map/ppermute | solution.py:133
  83.1 11.8 %copy-start.1 = (bf16[512,512]{1,0:T(8,128)(2,1)}, bf16[512,512]{1,0:T(8,128)(2,1)S(1)}, u32[]{:S(2)}) copy-start(bf16[512,512]{1,0:T(8,128)(2,1)S(1)} %collective-permute-done.3.refs_1_) | copy-start | bytes 1572868
  83.2 21.5 %collective-permute-start.7 = (bf16[256,512]{1,0:T(8,128)(2,1)S(1)}, bf16[256,512]{1,0:T(8,128)(2,1)S(1)}, u32[]{:S(2)}, u32[]{:S(2)}) collective-permute-start(bf16[256,512]{1,0:T(8,128)(2,1)S(1)} %slice.22), channel_id=1, source_target_pairs={{0,2},{1,3},{2,4},{3,5},{4,6},{5,7},{6,0},{7,1},{8,10},{9,11},{10,... | collective-permute-start | bytes 786440 | tf_op jit(solution)/shard_map/ppermute | solution.py:133
  83.3 11.7 %copy-start.3 = (bf16[512,512]{1,0:T(8,128)(2,1)}, bf16[512,512]{1,0:T(8,128)(2,1)S(1)}, u32[]{:S(2)}) copy-start(bf16[512,512]{1,0:T(8,128)(2,1)S(1)} %collective-permute-done.4.refs_2_) | copy-start | bytes 1572868
  83.3 21.4 %collective-permute-start.8 = (bf16[256,512]{1,0:T(8,128)(2,1)S(1)}, bf16[256,512]{1,0:T(8,128)(2,1)S(1)}, u32[]{:S(2)}, u32[]{:S(2)}) collective-permute-start(bf16[256,512]{1,0:T(8,128)(2,1)S(1)} %slice.23), channel_id=1, source_target_pairs={{0,6},{1,7},{2,0},{3,1},{4,2},{5,3},{6,4},{7,5},{8,14},{9,15},{10,... | collective-permute-start | bytes 786440 | tf_op jit(solution)/shard_map/ppermute | solution.py:133
  104.7 0.8 copy-start.11
  110.6 5.6 %copy-start.6 = (bf16[16,32,512]{2,1,0:T(8,128)(2,1)}, bf16[16,32,512]{2,1,0:T(8,128)(2,1)S(1)}, u32[]{:S(2)}) copy-start(bf16[16,32,512]{2,1,0:T(8,128)(2,1)S(1)} %all-to-all-done.1) | copy-start | bytes 1572868
  110.6 16.5 %all-to-all-start = ((bf16[16,32,512]{2,1,0:T(8,128)(2,1)}), bf16[16,32,512]{2,1,0:T(8,128)(2,1)S(1)}, u32[]{:S(2)}, u32[]{:S(2)}) async-start(bf16[16,32,512]{2,1,0:T(8,128)(2,1)} %bitcast.29), calls=%async_computation | async-start | bytes 1048576 | tf_op jit(solution)/shard_map/all_to_all | solution.py:337
  127.0 0.8 copy-start.7
  133.9 14.4 %all-to-all-start.2 = ((bf16[16,32,512]{2,1,0:T(8,128)(2,1)}), bf16[16,32,512]{2,1,0:T(8,128)(2,1)S(1)}, u32[]{:S(2)}, u32[]{:S(2)}) async-start(bf16[16,32,512]{2,1,0:T(8,128)(2,1)} %bitcast.31), calls=%async_computation.2 | async-start | bytes 1048576 | tf_op jit(solution)/shard_map/all_to_all | solution.py:338
  148.3 0.8 copy-start
  153.2 17.8 %collective-permute-start.14 = (bf16[256,512]{1,0:T(8,128)(2,1)}, bf16[256,512]{1,0:T(8,128)(2,1)S(1)}, u32[]{:S(2)}, u32[]{:S(2)}) collective-permute-start(bf16[256,512]{1,0:T(8,128)(2,1)} %get-tuple-element.37), channel_id=1, source_target_pairs={{0,2},{1,3},{2,4},{3,5},{4,6},{5,7},{6,0},{7,1},{8,10},{9,11},{10,... | collective-permute-start | bytes 786440 | tf_op jit(solution)/shard_map/ppermute | solution.py:133
  153.8 3.8 %copy-start.21 = (bf16[256,512]{1,0:T(8,128)(2,1)S(1)}, bf16[256,512]{1,0:T(8,128)(2,1)}, u32[]{:S(2)}) copy-start(bf16[256,512]{1,0:T(8,128)(2,1)} %get-tuple-element.35) | copy-start | bytes 786436
  157.6 13.5 %collective-permute-start.11 = (bf16[256,512]{1,0:T(8,128)(2,1)}, bf16[256,512]{1,0:T(8,128)(2,1)S(1)}, u32[]{:S(2)}, u32[]{:S(2)}) collective-permute-start(bf16[256,512]{1,0:T(8,128)(2,1)} %get-tuple-element.33), channel_id=1, source_target_pairs={{0,2},{1,3},{2,4},{3,5},{4,6},{5,7},{6,0},{7,1},{8,10},{9,11},{10,... | collective-permute-start | bytes 786440 | tf_op jit(solution)/shard_map/ppermute | solution.py:133
  157.6 26.8 %collective-permute-start.13 = (bf16[256,512]{1,0:T(8,128)(2,1)S(1)}, bf16[256,512]{1,0:T(8,128)(2,1)S(1)}, u32[]{:S(2)}, u32[]{:S(2)}) collective-permute-start(bf16[256,512]{1,0:T(8,128)(2,1)S(1)} %copy-done.21), channel_id=1, source_target_pairs={{0,6},{1,7},{2,0},{3,1},{4,2},{5,3},{6,4},{7,5},{8,14},{9,15},{10,... | collective-permute-start | bytes 786440 | tf_op jit(solution)/shard_map/ppermute | solution.py:133
  160.9 36.0 %collective-permute-start.10 = (bf16[256,512]{1,0:T(8,128)(2,1)}, bf16[256,512]{1,0:T(8,128)(2,1)S(1)}, u32[]{:S(2)}, u32[]{:S(2)}) collective-permute-start(bf16[256,512]{1,0:T(8,128)(2,1)} %get-tuple-element.31), channel_id=1, source_target_pairs={{0,6},{1,7},{2,0},{3,1},{4,2},{5,3},{6,4},{7,5},{8,14},{9,15},{10,... | collective-permute-start | bytes 786440 | tf_op jit(solution)/shard_map/ppermute | solution.py:133
  167.0 4.0 %copy-start.23 = (bf16[256,512]{1,0:T(8,128)(2,1)S(1)}, bf16[256,512]{1,0:T(8,128)(2,1)}, u32[]{:S(2)}) copy-start(bf16[256,512]{1,0:T(8,128)(2,1)} %get-tuple-element.46) | copy-start | bytes 786436
  167.0 4.1 %copy-start.15 = (bf16[256,512]{1,0:T(8,128)(2,1)S(1)}, bf16[256,512]{1,0:T(8,128)(2,1)}, u32[]{:S(2)}) copy-start(bf16[256,512]{1,0:T(8,128)(2,1)} %get-tuple-element.36) | copy-start | bytes 786436
  167.0 6.2 %copy-start.16 = (bf16[256,512]{1,0:T(8,128)(2,1)S(1)}, bf16[256,512]{1,0:T(8,128)(2,1)}, u32[]{:S(2)}) copy-start(bf16[256,512]{1,0:T(8,128)(2,1)} %get-tuple-element.32) | copy-start | bytes 786436
  167.0 16.2 %copy-start.22 = (bf16[256,512]{1,0:T(8,128)(2,1)S(1)}, bf16[256,512]{1,0:T(8,128)(2,1)}, u32[]{:S(2)}) copy-start(bf16[256,512]{1,0:T(8,128)(2,1)} %get-tuple-element.44) | copy-start | bytes 786436
  167.0 17.4 %copy-start.17 = (bf16[256,512]{1,0:T(8,128)(2,1)S(1)}, bf16[256,512]{1,0:T(8,128)(2,1)}, u32[]{:S(2)}) copy-start(bf16[256,512]{1,0:T(8,128)(2,1)} %get-tuple-element.45) | copy-start | bytes 786436
  167.0 20.8 %copy-start.18 = (bf16[256,512]{1,0:T(8,128)(2,1)S(1)}, bf16[256,512]{1,0:T(8,128)(2,1)}, u32[]{:S(2)}) copy-start(bf16[256,512]{1,0:T(8,128)(2,1)} %get-tuple-element.34) | copy-start | bytes 786436
  170.8 18.0 %copy-start.14 = (bf16[256,512]{1,0:T(8,128)(2,1)S(1)}, bf16[256,512]{1,0:T(8,128)(2,1)}, u32[]{:S(2)}) copy-start(bf16[256,512]{1,0:T(8,128)(2,1)} %get-tuple-element.41) | copy-start | bytes 786436
  170.8 22.8 %copy-start.20 = (bf16[256,512]{1,0:T(8,128)(2,1)S(1)}, bf16[256,512]{1,0:T(8,128)(2,1)}, u32[]{:S(2)}) copy-start(bf16[256,512]{1,0:T(8,128)(2,1)} %get-tuple-element.40) | copy-start | bytes 786436
  170.8 26.1 %copy-start.19 = (bf16[256,512]{1,0:T(8,128)(2,1)S(1)}, bf16[256,512]{1,0:T(8,128)(2,1)}, u32[]{:S(2)}) copy-start(bf16[256,512]{1,0:T(8,128)(2,1)} %get-tuple-element.43) | copy-start | bytes 786436
  170.8 28.4 %copy-start.12 = (bf16[256,512]{1,0:T(8,128)(2,1)S(1)}, bf16[256,512]{1,0:T(8,128)(2,1)}, u32[]{:S(2)}) copy-start(bf16[256,512]{1,0:T(8,128)(2,1)} %get-tuple-element.30) | copy-start | bytes 786436
  170.8 17.1 %collective-permute-start.18 = (bf16[256,512]{1,0:T(8,128)(2,1)}, bf16[256,512]{1,0:T(8,128)(2,1)S(1)}, u32[]{:S(2)}, u32[]{:S(2)}) collective-permute-start(bf16[256,512]{1,0:T(8,128)(2,1)} %get-tuple-element.42), channel_id=1, source_target_pairs={{0,6},{1,7},{2,0},{3,1},{4,2},{5,3},{6,4},{7,5},{8,14},{9,15},{10,... | collective-permute-start | bytes 786440 | tf_op jit(solution)/shard_map/ppermute | solution.py:133
  171.0 12.2 %collective-permute-start.21 = (bf16[256,512]{1,0:T(8,128)(2,1)S(1)}, bf16[256,512]{1,0:T(8,128)(2,1)S(1)}, u32[]{:S(2)}, u32[]{:S(2)}) collective-permute-start(bf16[256,512]{1,0:T(8,128)(2,1)S(1)} %copy-done.23), channel_id=1, source_target_pairs={{0,6},{1,7},{2,0},{3,1},{4,2},{5,3},{6,4},{7,5},{8,14},{9,15},{10,... | collective-permute-start | bytes 786440 | tf_op jit(solution)/shard_map/ppermute | solution.py:133
  171.1 33.9 %copy-start.13 = (bf16[256,512]{1,0:T(8,128)(2,1)S(1)}, bf16[256,512]{1,0:T(8,128)(2,1)}, u32[]{:S(2)}) copy-start(bf16[256,512]{1,0:T(8,128)(2,1)} %get-tuple-element.39) | copy-start | bytes 786436
  171.1 15.2 %collective-permute-start.15 = (bf16[256,512]{1,0:T(8,128)(2,1)S(1)}, bf16[256,512]{1,0:T(8,128)(2,1)S(1)}, u32[]{:S(2)}, u32[]{:S(2)}) collective-permute-start(bf16[256,512]{1,0:T(8,128)(2,1)S(1)} %add_convert_fusion.6), channel_id=1, source_target_pairs={{0,2},{1,3},{2,4},{3,5},{4,6},{5,7},{6,0},{7,1},{8,10},{9,11},{10,... | collective-permute-start | bytes 786440 | tf_op jit(solution)/shard_map/ppermute | solution.py:133
  183.2 10.5 %collective-permute-start.20 = (bf16[256,512]{1,0:T(8,128)(2,1)S(1)}, bf16[256,512]{1,0:T(8,128)(2,1)S(1)}, u32[]{:S(2)}, u32[]{:S(2)}) collective-permute-start(bf16[256,512]{1,0:T(8,128)(2,1)S(1)} %copy-done.22), channel_id=1, source_target_pairs={{0,2},{1,3},{2,4},{3,5},{4,6},{5,7},{6,0},{7,1},{8,10},{9,11},{10,... | collective-permute-start | bytes 786440 | tf_op jit(solution)/shard_map/ppermute | solution.py:133
  184.5 14.8 %collective-permute-start.12 = (bf16[256,512]{1,0:T(8,128)(2,1)S(1)}, bf16[256,512]{1,0:T(8,128)(2,1)S(1)}, u32[]{:S(2)}, u32[]{:S(2)}) collective-permute-start(bf16[256,512]{1,0:T(8,128)(2,1)S(1)} %add_convert_fusion.7), channel_id=1, source_target_pairs={{0,2},{1,3},{2,4},{3,5},{4,6},{5,7},{6,0},{7,1},{8,10},{9,11},{10,... | collective-permute-start | bytes 786440 | tf_op jit(solution)/shard_map/ppermute | solution.py:133
  186.3 7.4 %collective-permute-start.22 = (bf16[256,512]{1,0:T(8,128)(2,1)S(1)}, bf16[256,512]{1,0:T(8,128)(2,1)S(1)}, u32[]{:S(2)}, u32[]{:S(2)}) collective-permute-start(bf16[256,512]{1,0:T(8,128)(2,1)S(1)} %add_convert_fusion.2), channel_id=1, source_target_pairs={{0,6},{1,7},{2,0},{3,1},{4,2},{5,3},{6,4},{7,5},{8,14},{9,15},{10,... | collective-permute-start | bytes 786440 | tf_op jit(solution)/shard_map/ppermute | solution.py:133
  187.9 11.3 %collective-permute-start.16 = (bf16[256,512]{1,0:T(8,128)(2,1)S(1)}, bf16[256,512]{1,0:T(8,128)(2,1)S(1)}, u32[]{:S(2)}, u32[]{:S(2)}) collective-permute-start(bf16[256,512]{1,0:T(8,128)(2,1)S(1)} %add_convert_fusion.5), channel_id=1, source_target_pairs={{0,1},{1,0},{2,3},{3,2},{4,5},{5,4},{6,7},{7,6},{8,9},{9,8},{10,11... | collective-permute-start | bytes 786440 | tf_op jit(solution)/shard_map/ppermute | solution.py:138
  193.6 8.9 %collective-permute-start.17 = (bf16[256,512]{1,0:T(8,128)(2,1)S(1)}, bf16[256,512]{1,0:T(8,128)(2,1)S(1)}, u32[]{:S(2)}, u32[]{:S(2)}) collective-permute-start(bf16[256,512]{1,0:T(8,128)(2,1)S(1)} %copy-done.20), channel_id=1, source_target_pairs={{0,2},{1,3},{2,4},{3,5},{4,6},{5,7},{6,0},{7,1},{8,10},{9,11},{10,... | collective-permute-start | bytes 786440 | tf_op jit(solution)/shard_map/ppermute | solution.py:133
  193.7 8.9 %collective-permute-start.19 = (bf16[256,512]{1,0:T(8,128)(2,1)S(1)}, bf16[256,512]{1,0:T(8,128)(2,1)S(1)}, u32[]{:S(2)}, u32[]{:S(2)}) collective-permute-start(bf16[256,512]{1,0:T(8,128)(2,1)S(1)} %add_convert_fusion.3), channel_id=1, source_target_pairs={{0,6},{1,7},{2,0},{3,1},{4,2},{5,3},{6,4},{7,5},{8,14},{9,15},{10,... | collective-permute-start | bytes 786440 | tf_op jit(solution)/shard_map/ppermute | solution.py:133
  197.0 8.0 %collective-permute-start.23 = (bf16[256,512]{1,0:T(8,128)(2,1)S(1)}, bf16[256,512]{1,0:T(8,128)(2,1)S(1)}, u32[]{:S(2)}, u32[]{:S(2)}) collective-permute-start(bf16[256,512]{1,0:T(8,128)(2,1)S(1)} %add_convert_fusion.1), channel_id=1, source_target_pairs={{0,1},{1,0},{2,3},{3,2},{4,5},{5,4},{6,7},{7,6},{8,9},{9,8},{10,11... | collective-permute-start | bytes 786440 | tf_op jit(solution)/shard_map/ppermute | solution.py:138
  (3 other events, 2.1 us)

commit v2 on v1

--- a/solution.py
+++ b/solution.py
@@ -90,7 +90,9 @@
 def whole():
     return pl.BlockSpec(memory_space=pltpu.VMEM)
 
-VM = 56 * 1024 * 1024
+def params(mib):
+    return pltpu.CompilerParams(vmem_limit_bytes=mib * 1024 * 1024)
+
 
 def filter_spectrum(x, tables, seqs):
     rows = x.shape[1]
@@ -101,7 +103,7 @@
         out_shape=jax.ShapeDtypeStruct((chans * K1, 256), jnp.float32),
         in_specs=[whole()] * 4, out_specs=whole(),
         scratch_shapes=[pltpu.VMEM((x.shape[1] // 128, x.shape[0], 128), jnp.float32)],
-        compiler_params=pltpu.CompilerParams(vmem_limit_bytes=VM),
+        compiler_params=params(16),
         name="filter_spectrum",
         cost_estimate=pl.CostEstimate(flops=4_000_000_000, bytes_accessed=4_000_000, transcendentals=0),
     )(x, first, tw, forward)
@@ -116,7 +118,7 @@
         out_shape=jax.ShapeDtypeStruct(x.shape, jnp.bfloat16),
         in_specs=[whole()] * 7, out_specs=whole(),
         scratch_shapes=[pltpu.VMEM((x.shape[1] // 128, x.shape[0], 128), jnp.float32)] * 2,
-        compiler_params=pltpu.CompilerParams(vmem_limit_bytes=VM),
+        compiler_params=params(16),
         name="convolve",
         cost_estimate=pl.CostEstimate(flops=5_000_000_000, bytes_accessed=4_000_000, transcendentals=0),
     )(x, spec, first, tw, forward, backward, last)
@@ -138,8 +140,10 @@
     return lax.ppermute(array, "chan", [(i, i ^ 1) for i in range(count)])
 
 
-def params(**more):
-    return pltpu.CompilerParams(vmem_limit_bytes=VM, **more)
+def following_far(array):
+    seqs, count = lax.axis_size("seq"), lax.axis_size("chan")
+    pairs = [(s * count + c, (s + 1) * count + (((c + 4) % count) ^ 1)) for s in range(seqs - 1) for c in range(count)]
+    return lax.ppermute(array, ("seq", "chan"), pairs)
 
 
 def transpose_kernel(x_ref, out):
@@ -151,27 +155,9 @@
         transpose_kernel,
         out_shape=jax.ShapeDtypeStruct(x.shape[::-1], jnp.bfloat16),
         in_specs=[whole()], out_specs=whole(),
-        compiler_params=params(), name="transposed",
+        compiler_params=params(8), name="transposed",
         cost_estimate=pl.CostEstimate(flops=0, bytes_accessed=6 * x.size, transcendentals=0),
     )(x)
-
-
-def halo_kernel(x_ref, w_ref, out):
-    out[0] = jnp.dot(x_ref[...], w_ref[0], preferred_element_type=jnp.float32).astype(jnp.bfloat16)
-
-
-def halo_projection(halo, weight):
-    branches, model, width = weight.shape
-    rows = halo.shape[0]
-    return pl.pallas_call(
-        halo_kernel,
-        grid=(branches,),
-        out_shape=jax.ShapeDtypeStruct((branches, rows, width), jnp.bfloat16),
-        in_specs=[pl.BlockSpec((rows, model), lambda j: (0, 0)), pl.BlockSpec((1, model, width), lambda j: (j, 0, 0))],
-        out_specs=pl.BlockSpec((1, rows, width), lambda j: (j, 0, 0)),
-        compiler_params=params(), name="halo_projection",
-        cost_estimate=pl.CostEstimate(flops=2 * rows * weight.size, bytes_accessed=2 * weight.size, transcendentals=0),
-    )(halo, weight)
 
 
 def round_kernel(pieces, has_acc, owners, *refs):
@@ -201,19 +187,21 @@
         functools.partial(round_kernel, [len(b) for b in blocks], acc is not None),
         out_shape=jax.ShapeDtypeStruct((branches, rows, width), jnp.float32),
         grid_spec=pltpu.PrefetchScalarGridSpec(num_scalar_prefetch=1, grid=(branches,), in_specs=specs, out_specs=acc_spec),
-        compiler_params=params(), name="project_round",
+        compiler_params=params(20), name="project_round",
         cost_estimate=pl.CostEstimate(flops=2 * len(blocks) * rows * depth * branches * width, bytes_accessed=2 * len(blocks) * depth * branches * width, transcendentals=0),
     )(owners, *args)
 
 
-def signal_kernel(owners, acc, lo, hi, weight, halo, taps, signal_t, signal, gate_out):
+def signal_kernel(owners, acc, lo, hi, weight, halo, halo_acc, taps, signal_t, signal, gate_out):
     rows = acc.shape[1]
     block = jnp.concatenate([lo[...], hi[...]], axis=0)
     short = []
     for j in range(3):
         proj = acc[j] + jnp.dot(block, weight[j], preferred_element_type=jnp.float32)
         proj = proj.astype(jnp.bfloat16).astype(jnp.float32)
-        ext = jnp.concatenate([halo[j].astype(jnp.float32)[8:], proj], axis=0)
+        before = halo_acc[j] + jnp.dot(halo[...], weight[j], preferred_element_type=jnp.float32)
+        before = before.astype(jnp.bfloat16).astype(jnp.float32)
+        ext = jnp.concatenate([before[8:], proj], axis=0)
         short.append(taps[0, j:j + 1] * ext[6:6 + rows] + taps[1, j:j + 1] * ext[7:7 + rows] + taps[2, j:j + 1] * proj)
     sig = short[2] * short[1]
     gate_out[...] = short[0]
@@ -221,13 +209,14 @@
     signal_t[...] = sig.T.astype(jnp.bfloat16)
 
 
-def signal_of(acc, lo, hi, owners, weight, halo, taps):
+def signal_of(acc, lo, hi, owners, weight, halo, halo_acc, taps):
     branches, _, width = weight.shape
     rows = acc.shape[1]
     depth = lo.shape[1]
     cols = 256
     col = lambda c, o: (0, c)
     cube = lambda c, o: (0, 0, c)
+    fixed = lambda c, o: (0, 0)
     return pl.pallas_call(
         signal_kernel,
         out_shape=(
@@ -239,71 +228,72 @@
             num_scalar_prefetch=1, grid=(width // cols,),
             in_specs=[
                 pl.BlockSpec((branches, rows, cols), cube),
-                pl.BlockSpec(lo.shape, lambda c, o: (0, 0)),
-                pl.BlockSpec(hi.shape, lambda c, o: (0, 0)),
+                pl.BlockSpec(lo.shape, fixed),
+                pl.BlockSpec(hi.shape, fixed),
                 pl.BlockSpec((branches, depth, cols), lambda c, o: (0, o[0], c)),
-                pl.BlockSpec((branches, halo.shape[1], cols), cube),
+                pl.BlockSpec(halo.shape, fixed),
+                pl.BlockSpec((branches, halo_acc.shape[1], cols), cube),
                 pl.BlockSpec((3, branches, cols), cube),
             ],
             out_specs=[pl.BlockSpec((cols, rows), lambda c, o: (c, 0)), pl.BlockSpec((rows, cols), col), pl.BlockSpec((rows, cols), col)],
         ),
-        compiler_params=params(), name="signal_of",
-    )(owners, acc, lo, hi, weight, halo, taps)
-
-
-def gate_kernel(owners, conv, signal, gate_out, skip, w0, w1, w2, w3, gated, o0, o1, o2, o3):
+        compiler_params=params(20), name="signal_of",
+        cost_estimate=pl.CostEstimate(flops=2 * rows * depth * branches * width, bytes_accessed=16 * rows * width, transcendentals=0),
+    )(owners, acc, lo, hi, weight, halo, halo_acc, taps)
+
+
+def fetch(owners, k, weight, held, sems):
+    cols = held.shape[2]
+    start = pl.multiple_of(owners[k] * cols, cols)
+    return pltpu.make_async_copy(weight.at[:, pl.ds(start, cols)], held.at[k], sems.at[k])
+
+
+def gate_kernel(owners, conv, signal, gate_out, skip, weight, gated, out, held, sems):
+    copy = fetch(owners, 0, weight, held, sems)
+    copy.start()
     total = conv[...].astype(jnp.float32).T + skip[...] * signal[...]
     g = (total * gate_out[...]).astype(jnp.bfloat16)
     gated[...] = g
-    for w, o in ((w0, o0), (w1, o1), (w2, o2), (w3, o3)):
-        o[...] = jnp.dot(g, w[...], preferred_element_type=jnp.float32).astype(jnp.bfloat16)
-
-
-def gate_and_project(part, parts, conv, signal, gate_out, skip, owners, weight):
+    copy.wait()
+    out[...] = jnp.dot(g, held[0], preferred_element_type=jnp.float32).astype(jnp.bfloat16)
+
+
+def gate_and_project(conv, signal, gate_out, skip, owners, weight, cols):
     width, rows = conv.shape
-    cols = weight.shape[1] // 8
-    rows //= parts
-    row = lambda i, o: (part, 0)
-    out = pl.BlockSpec((rows, cols), lambda i, o: (0, 0))
+    smem = pl.BlockSpec(memory_space=pltpu.SMEM)
     return pl.pallas_call(
         gate_kernel,
-        out_shape=(jax.ShapeDtypeStruct((rows, width), jnp.bfloat16),) + (jax.ShapeDtypeStruct((rows, cols), jnp.bfloat16),) * 4,
-        grid_spec=pltpu.PrefetchScalarGridSpec(
-            num_scalar_prefetch=1, grid=(1,),
-            in_specs=[
-                pl.BlockSpec((width, rows), lambda i, o: (0, part)),
-                pl.BlockSpec((rows, width), row),
-                pl.BlockSpec((rows, width), row),
-                pl.BlockSpec((1, width), lambda i, o: (0, 0)),
-            ] + [pl.BlockSpec((width, cols), lambda i, o, k=k: (0, o[k])) for k in range(4)],
-            out_specs=[pl.BlockSpec((rows, width), lambda i, o: (0, 0))] + [out] * 4,
-        ),
-        compiler_params=params(), name="gate_and_project",
-        cost_estimate=pl.CostEstimate(flops=8 * rows * width * cols, bytes_accessed=8 * width * cols, transcendentals=0),
-    )(owners, conv, signal, gate_out, skip, weight, weight, weight, weight)
-
-
-def out_kernel(owners, g, w0, w1, w2, w3, o0, o1, o2, o3):
-    for w, o in ((w0, o0), (w1, o1), (w2, o2), (w3, o3)):
-        o[...] = jnp.dot(g[...], w[...], preferred_element_type=jnp.float32).astype(jnp.bfloat16)
-
-
-def project_out(gated, owners, weight):
+        out_shape=(jax.ShapeDtypeStruct((rows, width), jnp.bfloat16), jax.ShapeDtypeStruct((rows, cols), jnp.bfloat16)),
+        in_specs=[smem] + [whole()] * 4 + [pl.BlockSpec(memory_space=pl.ANY)],
+        out_specs=[whole()] * 2,
+        scratch_shapes=[pltpu.VMEM((1, width, cols), jnp.bfloat16), pltpu.SemaphoreType.DMA((1,))],
+        compiler_params=params(16), name="gate_and_project",
+        cost_estimate=pl.CostEstimate(flops=2 * rows * width * cols, bytes_accessed=12 * rows * width, transcendentals=0),
+    )(owners, conv, signal, gate_out, skip, weight)
+
+
+def out_kernel(count, owners, g, weight, *refs):
+    outs, (held, sems) = refs[:count], refs[count:]
+    copies = [fetch(owners, k, weight, held, sems) for k in range(count)]
+    for copy in copies:
+        copy.start()
+    for k in range(count):
+        copies[k].wait()
+        outs[k][...] = jnp.dot(g[...], held[k], preferred_element_type=jnp.float32).astype(jnp.bfloat16)
+
+
+def project_out(gated, owners, weight, cols):
     rows, width = gated.shape
-    cols = weight.shape[1] // 8
-    out = pl.BlockSpec((rows, cols), lambda i, o: (0, 0))
-    return pl.pallas_call(
-        out_kernel,
-        out_shape=(jax.ShapeDtypeStruct((rows, cols), jnp.bfloat16),) * 4,
-        grid_spec=pltpu.PrefetchScalarGridSpec(
-            num_scalar_prefetch=1, grid=(1,),
-            in_specs=[pl.BlockSpec((rows, width), lambda i, o: (0, 0))]
-            + [pl.BlockSpec((width, cols), lambda i, o, k=k: (0, o[k])) for k in range(4)],
-            out_specs=[out] * 4,
-        ),
-        compiler_params=params(), name="project_out",
-        cost_estimate=pl.CostEstimate(flops=8 * rows * width * cols, bytes_accessed=8 * width * cols, transcendentals=0),
-    )(owners, gated, weight, weight, weight, weight)
+    count = owners.shape[0]
+    return pl.pallas_call(
+        functools.partial(out_kernel, count),
+        out_shape=(jax.ShapeDtypeStruct((rows, cols), jnp.bfloat16),) * count,
+        in_specs=[pl.BlockSpec(memory_space=pltpu.SMEM), whole(), pl.BlockSpec(memory_space=pl.ANY)],
+        out_specs=[whole()] * count,
+        scratch_shapes=[pltpu.VMEM((count, width, cols), jnp.bfloat16), pltpu.SemaphoreType.DMA((count,))],
+        compiler_params=params(16), name="project_out",
+        cost_estimate=pl.CostEstimate(flops=2 * count * rows * width * cols, bytes_accessed=4 * count * width * cols, transcendentals=0),
+    )(owners, gated, weight)
 
 
 def added(*terms):
@@ -311,51 +301,43 @@
 
 
 def shards(tables, tokens, in_weight, short_weight, long_filter, skip_gain, out_weight):
-    seqs = lax.axis_size("seq")
     count = lax.axis_size("chan")
     rows, width = tokens.shape
     half = rows // 2
+    cols = out_weight.shape[1] // count
     me = lax.axis_index("chan")
     at = lambda dy, dx: jnp.bitwise_xor((me + 2 * dy) % count, dx).astype(jnp.int32)
     ids = lambda *pairs: jnp.stack([at(dy, dx) for dy, dx in pairs])
     weight = jnp.transpose(in_weight, (1, 0, 2))
-
+    seqs = lax.axis_size("seq")
+
+    below, above, side = ring(tokens, 1), ring(tokens, -1), cross(tokens)
     fil = lax.all_to_all(transposed(long_filter), "seq", 0, 0, tiled=True)
-    below, above, side = ring(tokens, 1), ring(tokens, -1), cross(tokens)
-    side_below, side_above = ring(side, 1), ring(side, -1)
-    far_lo, far_hi = ring(below[:half], 1), ring(above[half:], -1)
-    side_far_lo, side_far_hi = ring(side_below[:half], 1), ring(side_above[half:], -1)
-    halo = lax.all_gather(shifted(tokens[rows - 16:], "seq", 1), "chan", axis=1, tiled=True)
+    halo = following_far(tokens[rows - 16:])
+    side_below, side_above, far = ring(side, 1), cross(above), ring(above, -1)
+    far_lo, far_hi = ring(side_below[:half], 1), ring(side_above[half:], -1)
 
     spec = filter_spectrum(fil, tables, seqs)
-    acc = project_round(None, [[tokens]], ids((0, 0)), weight)
-    halo = halo_projection(halo, weight)
-    acc = project_round(acc, [[below], [above], [side]], ids((-1, 0), (1, 0), (0, 1)), weight)
-    acc = project_round(acc, [[side_below], [side_above], [far_lo, far_hi]], ids((-1, 1), (1, 1), (2, 0)), weight)
-    signal_t, signal, gate_out = signal_of(acc, side_far_lo, side_far_hi, ids((2, 1)), weight, halo, short_weight)
+    acc = project_round(None, [[tokens], [below], [above], [side]], ids((0, 0), (-1, 0), (1, 0), (0, 1)), weight)
+    acc = project_round(acc, [[side_below], [side_above], [far]], ids((-1, 1), (1, 1), (2, 0)), weight)
+    halo_acc = shifted(acc[:, rows - 16:], "seq", 1)
+    signal_t, signal, gate_out = signal_of(acc, far_lo, far_hi, ids((2, 1)), weight, halo, halo_acc, short_weight)
 
     conv = convolve(lax.all_to_all(signal_t, "seq", 0, 0, tiled=True), spec, tables, seqs)
     conv = lax.all_to_all(conv, "seq", 0, 0, tiled=True)
 
     skip = skip_gain.reshape(1, width)
-    near = ids((2, 0), (1, 0), (-1, 0), (0, 0))
-    wide = ids((2, 1), (1, 1), (-1, 1), (0, 1))
-    g_lo, *lo = gate_and_project(0, 2, conv, signal, gate_out, skip, wide, out_weight)
-    g_hi, *hi = gate_and_project(1, 2, conv, signal, gate_out, skip, wide, out_weight)
-
-    def reduced(lo, hi):
-        far_lo, up_lo, down_lo, own_lo = lo
-        far_hi, up_hi, down_hi, own_hi = hi
-        from_lo, from_hi = ring(far_lo, 1), ring(far_hi, -1)
-        here_hi, here_lo = ring(up_hi, 1), ring(down_lo, -1)
-        sum_lo = ring(added(up_lo, from_lo), 1)
-        sum_hi = ring(added(down_hi, from_hi), -1)
-        return (own_lo, here_lo, sum_lo), (own_hi, here_hi, sum_hi)
-
-    wide_lo, wide_hi = reduced(lo, hi)
-    wide_lo, wide_hi = cross(added(*wide_lo)), cross(added(*wide_hi))
-    near_lo, near_hi = reduced(project_out(g_lo, near, out_weight), project_out(g_hi, near, out_weight))
-    return jnp.concatenate([added(*near_lo, wide_lo), added(*near_hi, wide_hi)], axis=0)
+    gated, far_side = gate_and_project(conv, signal, gate_out, skip, ids((2, 1)), out_weight, cols)
+    to_lo, to_hi = ring(far_side[:half], -1), ring(far_side[half:], 1)
+    down_side, up_side, far = project_out(gated, ids((-1, 1), (1, 1), (2, 0)), out_weight, cols)
+    far = ring(far, 1)
+    up, down, side, own = project_out(gated, ids((1, 0), (-1, 0), (0, 1), (0, 0)), out_weight, cols)
+    down = ring(down, -1)
+    down_side = ring(jnp.concatenate([added(down_side[:half], to_lo), down_side[half:]], axis=0), -1)
+    up_side = cross(jnp.concatenate([up_side[:half], added(up_side[half:], to_hi)], axis=0))
+    side = cross(added(side, down_side))
+    up = ring(added(up, far, up_side), 1)
+    return added(own, down, side, up)
 
 
 def solution(mesh):

time: 207 us -> 145 us (0.70)
  Pallas kernels: 61.2 us -> 24.7 us
  blocking collectives: 36.4 us -> 13.5 us
  local copies, waits for them, and re-layouts: 4.62 us -> 19.6 us
  waiting for transfers between devices: 47.1 us -> 35.6 us
  starting transfers between devices: 52.2 us -> 48.6 us
  other arithmetic: 4.03 us -> 1.84 us
    all_gather x1 -> x0, blocking collectives: 36.4 us -> none  [shards(): lax.all_gather(shifted(tokens[rows - 16:], 'seq', 1), 'chan', axis=1, til...]
    ppermute x20 -> x12, starting transfers between devices: 28.5 us -> 14.8 us  [ring(): lax.ppermute(array, 'chan', [(i, (i + 2 * by) % count) for i in range(cou...]
    all_to_all x0 -> x1, blocking collectives: none -> 13.5 us  [shards(): conv = lax.all_to_all(conv, 'seq', 0, 0, tiled=True)]
    pallas_call x3 -> x2, Pallas kernels: 21.1 us -> 7.84 us  [project_round(): pl.pallas_call(functools.partial(round_kernel, [len(b) for b in blocks],...]
    unnamed x48 -> x40, local copies, waits for them, and re-layouts: 3.83 us -> 16.8 us
    all_to_all x1 -> x0, waiting for transfers between devices: 10.2 us -> none  [shards(): conv = lax.all_to_all(conv, 'seq', 0, 0, tiled=True)]
    pallas_call x3 -> x2, Pallas kernels: 14.1 us -> 4.8 us  [project_out(): pl.pallas_call(functools.partial(out_kernel, count), out_shape=(jax.Shape...]
    pallas_call x2 -> x1, Pallas kernels: 8.12 us -> 0.86 us  [gate_and_project(): pl.pallas_call(gate_kernel, out_shape=(jax.ShapeDtypeStruct((rows, width)...]
  transfers between devices with their start and end apart: 27 -> 20, of which waited for: 8 -> 11; matrix products, arithmetic and copies ran while one was open for 2% -> 2% of each run, Pallas kernels for 25% -> 14%
where the time goes in v2:
time: 145 us; the launch traced here: 144 us
  starting transfers between devices  48.6 us (34%)
  waiting for transfers between devices  35.6 us (25%)
  Pallas kernels  24.7 us (17%)
  local copies, waits for them, and re-layouts  19.6 us (14%)
  blocking collectives  13.5 us (9%)
  other arithmetic  1.84 us (1%)
    unnamed x40, local copies, waits for them, and re-layouts  16.8 us
    ppermute x12, waiting for transfers between devices, ring(): lax.ppermute(array, 'chan', [(i, (i + 2 * by) % count) for i in range(cou...  14.8 us
    ppermute x12, starting transfers between devices, ring(): lax.ppermute(array, 'chan', [(i, (i + 2 * by) % count) for i in range(cou...  14.8 us
    ppermute x4, waiting for transfers between devices, cross(): return lax.ppermute(array, 'chan', [(i, i ^ 1) for i in range(count)])  13.8 us
    all_to_all x1, blocking collectives, shards(): conv = lax.all_to_all(conv, 'seq', 0, 0, tiled=True)  13.5 us
    ppermute x4, starting transfers between devices, cross(): return lax.ppermute(array, 'chan', [(i, i ^ 1) for i in range(count)])  11.9 us
    all_to_all x1, starting transfers between devices, shards(): lax.all_to_all(signal_t, 'seq', 0, 0, tiled=True)  8.43 us
    pallas_call x2, Pallas kernels, project_round(): pl.pallas_call(functools.partial(round_kernel, [len(b) for b in blocks],...  7.84 us
  transfers between devices with their start and end apart: 20, of which 11 were waited for; matrix products, arithmetic and copies ran while one was open for 2% of the time, Pallas kernels for 14%

profile of v2, /device:TPU:0, one launch (start us, length us, event | category | flops | bytes accessed | tf_op | source)
XLA Modules:
  0.0 144.1 jit_solution(8559682666776823595)
XLA Ops:
  0.0 3.1 %collective-permute-start.1 = (bf16[512,512]{1,0:T(8,128)(2,1)}, bf16[512,512]{1,0:T(8,128)(2,1)S(1)}, u32[]{:S(2)}, u32[]{:S(2)}) collective-permute-start(bf16[512,512]{1,0:T(8,128)(2,1)} %refs_0_.1), channel_id=1, source_target_pairs={{0,6},{1,7},{2,0},{3,1},{4,2},{5,3},{6,4},{7,5},{8,14},{9,15},{10,... | collective-permute-start | bytes 1572872 | tf_op jit(solution)/shard_map/ppermute | solution.py:135
  3.1 3.0 %collective-permute-start.2 = (bf16[512,512]{1,0:T(8,128)(2,1)}, bf16[512,512]{1,0:T(8,128)(2,1)S(1)}, u32[]{:S(2)}, u32[]{:S(2)}) collective-permute-start(bf16[512,512]{1,0:T(8,128)(2,1)} %refs_0_.1), channel_id=1, source_target_pairs={{0,1},{1,0},{2,3},{3,2},{4,5},{5,4},{6,7},{7,6},{8,9},{9,8},{10,11... | collective-permute-start | bytes 1572872 | tf_op jit(solution)/shard_map/ppermute | solution.py:140
  6.1 1.2 copy-done.8
  7.4 1.0 transposed.1
  8.4 5.5 %all-to-all-start.1 = ((bf16[16,32,512]{2,1,0:T(8,128)(2,1)}), bf16[16,32,512]{2,1,0:T(8,128)(2,1)}, u32[]{:S(2)}, u32[]{:S(2)}) async-start(bf16[16,32,512]{2,1,0:T(8,128)(2,1)} %bitcast.11), calls=%async_computation.1 | async-start | bytes 1048576 | tf_op jit(solution)/shard_map/all_to_all | solution.py:315
  13.9 0.7 collective-permute-done.1.refs_2_
  14.6 3.0 %collective-permute-start.4 = (bf16[512,512]{1,0:T(8,128)(2,1)S(1)}, bf16[512,512]{1,0:T(8,128)(2,1)S(1)}, u32[]{:S(2)}, u32[]{:S(2)}) collective-permute-start(bf16[512,512]{1,0:T(8,128)(2,1)S(1)} %collective-permute-done.1.refs_2_), channel_id=1, source_target_pairs={{0,1},{1,0},{2,3},{3,2},{4,5},{5,4},{6,7},{7,6},{8,9},{9,8},{10,11... | collective-permute-start | bytes 1572872 | tf_op jit(solution)/shard_map/ppermute | solution.py:140
  17.6 3.6 %collective-permute-start.5 = (bf16[512,512]{1,0:T(8,128)(2,1)S(1)}, bf16[512,512]{1,0:T(8,128)(2,1)S(1)}, u32[]{:S(2)}, u32[]{:S(2)}) collective-permute-start(bf16[512,512]{1,0:T(8,128)(2,1)S(1)} %collective-permute-done.1.refs_2_), channel_id=1, source_target_pairs={{0,6},{1,7},{2,0},{3,1},{4,2},{5,3},{6,4},{7,5},{8,14},{9,15},{10,... | collective-permute-start | bytes 1572872 | tf_op jit(solution)/shard_map/ppermute | solution.py:135
  21.4 4.6 %copy-done = bf16[4096,3,512]{2,0,1:T(8,128)(2,1)S(1)} copy-done((bf16[4096,3,512]{2,0,1:T(8,128)(2,1)S(1)}, bf16[4096,3,512]{2,0,1:T(8,128)(2,1)}, u32[]{:S(2)}) %copy-start) | copy-done | bytes 12582936
  26.0 1.0 copy-done.9
  27.0 4.3 %project_round.2.refs_0_ = f32[3,512,512]{2,1,0:T(8,128)S(1)} custom-call(s32[4]{0:T(128)S(1)} %pad_add_fusion.2.owners, bf16[512,512]{1,0:T(8,128)(2,1)S(1)} %copy-done.9, bf16[512,512]{1,0:T(8,128)(2,1)S(1)} %collective-permute-done.refs_1_, bf16[512,512]{1,0:T(8,128)(2,1)S(1)} %collective-permute-done.1.refs_2_, ...), custom_call_target="tpu_custom_call" | custom-call | flops 3221225472 | bytes 6291456 | tf_op jit(solution)/shard_map/project_round/pallas_call | solution.py:186
  31.3 3.7 %collective-permute-done.4.refs_2_ = bf16[512,512]{1,0:T(8,128)(2,1)S(1)} collective-permute-done((bf16[512,512]{1,0:T(8,128)(2,1)S(1)}, bf16[512,512]{1,0:T(8,128)(2,1)S(1)}, u32[]{:S(2)}, u32[]{:S(2)}) %collective-permute-start.4) | collective-permute-done | bytes 524320 | tf_op jit(solution)/shard_map/ppermute | solution.py:140
  35.1 0.7 slice.41
  35.8 2.4 %collective-permute-start.7 = (bf16[256,512]{1,0:T(8,128)(2,1)}, bf16[256,512]{1,0:T(8,128)(2,1)S(1)}, u32[]{:S(2)}, u32[]{:S(2)}) collective-permute-start(bf16[256,512]{1,0:T(8,128)(2,1)} %slice.41), channel_id=1, source_target_pairs={{0,6},{1,7},{2,0},{3,1},{4,2},{5,3},{6,4},{7,5},{8,14},{9,15},{10,... | collective-permute-start | bytes 786440 | tf_op jit(solution)/shard_map/ppermute | solution.py:135
  38.2 0.7 slice.40
  38.9 3.5 %project_round.3.acc = f32[3,512,512]{2,1,0:T(8,128)S(1)} custom-call(s32[3]{0:T(128)S(1)} %pad_add_fusion.1.owners, f32[3,512,512]{2,1,0:T(8,128)S(1)} %project_round.2.refs_0_, bf16[512,512]{1,0:T(8,128)(2,1)S(1)} %collective-permute-done.3.refs_1_, bf16[512,512]{1,0:T(8,128)(2,1)S(1)} %collective-permute-done.4.refs_2_, ...), custom_call_target="tpu_custom_call" | custom-call | flops 2415919104 | bytes 4718592 | tf_op jit(solution)/shard_map/project_round/pallas_call | solution.py:186
  42.5 0.6 slice.42
  43.1 1.5 %collective-permute-start.9 = (f32[3,16,512]{2,1,0:T(8,128)}, f32[3,16,512]{2,1,0:T(8,128)S(1)}, u32[]{:S(2)}, u32[]{:S(2)}) collective-permute-start(f32[3,16,512]{2,1,0:T(8,128)} %slice.42), channel_id=1, source_target_pairs={{0,8},{8,16},{16,24},{24,32},{32,40},{40,48},{48,56},{56,64},{64,7... | collective-permute-start | bytes 294920 | tf_op jit(solution)/shard_map/ppermute | solution.py:130
  45.3 6.6 %collective-permute-start.8 = (bf16[16,512]{1,0:T(8,128)(2,1)}, bf16[16,512]{1,0:T(8,128)(2,1)S(1)}, u32[]{:S(2)}, u32[]{:S(2)}) collective-permute-start(bf16[16,512]{1,0:T(8,128)(2,1)} %slice.32), channel_id=1, source_target_pairs={{0,13},{1,12},{2,15},{3,14},{4,9},{5,8},{6,11},{7,10},{8,21},{9,20... | collective-permute-start | bytes 49160 | tf_op jit(solution)/shard_map/ppermute | solution.py:146
  51.8 1.6 %collective-permute-done.8.halo = bf16[16,512]{1,0:T(8,128)(2,1)S(1)} collective-permute-done((bf16[16,512]{1,0:T(8,128)(2,1)}, bf16[16,512]{1,0:T(8,128)(2,1)S(1)}, u32[]{:S(2)}, u32[]{:S(2)}) %collective-permute-start.8) | collective-permute-done | bytes 16416 | tf_op jit(solution)/shard_map/ppermute | solution.py:146
  53.5 4.6 %copy-done.2 = bf16[4096,3,512]{2,0,1:T(8,128)(2,1)S(1)} copy-done((bf16[4096,3,512]{2,0,1:T(8,128)(2,1)S(1)}, bf16[4096,3,512]{2,0,1:T(8,128)(2,1)}, u32[]{:S(2)}) %copy-start.2) | copy-done | bytes 12582936
  58.1 3.7 %signal_of.1 = (bf16[512,512]{1,0:T(8,128)(2,1)S(1)}, f32[512,512]{1,0:T(8,128)S(1)}, f32[512,512]{1,0:T(8,128)S(1)}) custom-call(s32[1]{0:T(128)} %bitcast.4.owners, f32[3,512,512]{2,1,0:T(8,128)S(1)} %project_round.3.acc, bf16[256,512]{1,0:T(8,128)(2,1)} %collective-permute-done.6.lo, bf16[256,512]{1,0:T(8,128)(2,1)S(1)} %collective-permute-done.7.hi, ...), custom_call_target="tpu_custom_call" | custom-call | flops 805306368 | bytes 4194304 | tf_op jit(solution)/shard_map/signal_of/pallas_call | solution.py:220
  61.8 1.0 copy-done.4
  62.8 1.0 copy-done.6
  63.8 0.8 copy-done.10
  64.6 8.4 %all-to-all-start = ((bf16[16,32,512]{2,1,0:T(8,128)(2,1)}), bf16[16,32,512]{2,1,0:T(8,128)(2,1)S(1)}, u32[]{:S(2)}, u32[]{:S(2)}) async-start(bf16[16,32,512]{2,1,0:T(8,128)(2,1)} %bitcast.25), calls=%async_computation | async-start | bytes 1048576 | tf_op jit(solution)/shard_map/all_to_all | solution.py:326
  73.1 0.9 copy-done.13
  74.0 0.9 copy-done.16
  74.8 0.8 copy-done.18
  75.6 3.0 %filter_spectrum.1.h_ref = f32[2304,256]{1,0:T(8,128)S(1)} custom-call(bf16[512,512]{1,0:T(8,128)(2,1)} %bitcast.12.x_ref, bf16[144,64]{1,0:T(8,128)(2,1)S(1)} %copy-done.18, f32[2,72,128]{2,1,0:T(8,128)S(1)} %copy-done.16, bf16[256,256]{1,0:T(8,128)(2,1)S(1)} %copy-done.13), custom_call_target="tpu_custom_call" | custom-call | flops 4000000000 | bytes 4000000 | tf_op jit(solution)/shard_map/filter_spectrum/pallas_call | solution.py:101
  78.6 5.3 %all-to-all-done = bf16[16,32,512]{2,1,0:T(8,128)(2,1)S(1)} async-done(((bf16[16,32,512]{2,1,0:T(8,128)(2,1)}), bf16[16,32,512]{2,1,0:T(8,128)(2,1)S(1)}, u32[]{:S(2)}, u32[]{:S(2)}) %all-to-all-start) | async-done | bytes 524320 | tf_op jit(solution)/shard_map/all_to_all | solution.py:326
  84.0 3.4 %convolve.1 = bf16[512,512]{1,0:T(8,128)(2,1)S(1)} custom-call(bf16[512,512]{1,0:T(8,128)(2,1)S(1)} %bitcast.26, f32[2304,256]{1,0:T(8,128)S(1)} %filter_spectrum.1.h_ref, bf16[144,64]{1,0:T(8,128)(2,1)S(1)} %copy-done.18, f32[2,72,128]{2,1,0:T(8,128)S(1)} %copy-done.17, bf16[256,256]{1,0:T(8,128)(2,1)S(1)} %copy-done.14, bf16[256,256]{1,0:T(8,128)(2,1)S(1)} %copy-done.15, ...), custom_call_target="tpu_custom_call" | custom-call | flops 5000000000 | bytes 4000000 | tf_op jit(solution)/shard_map/convolve/pallas_call | solution.py:116
  87.4 13.5 %all_to_all.33 = bf16[16,32,512]{2,1,0:T(8,128)(2,1)S(1)} all-to-all(bf16[16,32,512]{2,1,0:T(8,128)(2,1)S(1)} %bitcast.27), channel_id=1, replica_groups=mesh['seq'=16,'chan'=8] {'seq'}, dimensions={0} | all-to-all | bytes 1048576 | tf_op jit(solution)/shard_map/all_to_all | solution.py:327
  100.9 0.9 gate_and_project.1
  101.8 2.0 %collective-permute-start.11 = (bf16[256,512]{1,0:T(8,128)(2,1)S(1)}, bf16[256,512]{1,0:T(8,128)(2,1)S(1)}, u32[]{:S(2)}, u32[]{:S(2)}) collective-permute-start(bf16[256,512]{1,0:T(8,128)(2,1)S(1)} %get-tuple-element.29), channel_id=1, source_target_pairs={{0,6},{1,7},{2,0},{3,1},{4,2},{5,3},{6,4},{7,5},{8,14},{9,15},{10,... | collective-permute-start | bytes 786440 | tf_op jit(solution)/shard_map/ppermute | solution.py:135
  103.9 2.1 %project_out.3 = (bf16[512,512]{1,0:T(8,128)(2,1)S(1)}, bf16[512,512]{1,0:T(8,128)(2,1)S(1)}, bf16[512,512]{1,0:T(8,128)(2,1)S(1)}) custom-call(s32[3]{0:T(128)S(1)} %pad_add_fusion.1.owners, bf16[512,512]{1,0:T(8,128)(2,1)S(1)} %get-tuple-element.20.g, bf16[512,4096]{1,0:T(8,128)(2,1)S(1)} %copy-done.3), custom_call_target="tpu_custom_call" | custom-call | flops 805306368 | bytes 3145728 | tf_op jit(solution)/shard_map/project_out/pallas_call | solution.py:288
  106.3 3.2 %collective-permute-done.11 = bf16[256,512]{1,0:T(8,128)(2,1)S(1)} collective-permute-done((bf16[256,512]{1,0:T(8,128)(2,1)S(1)}, bf16[256,512]{1,0:T(8,128)(2,1)S(1)}, u32[]{:S(2)}, u32[]{:S(2)}) %collective-permute-start.11) | collective-permute-done | bytes 262176 | tf_op jit(solution)/shard_map/ppermute | solution.py:135
  109.6 3.2 %collective-permute-start.12 = (bf16[512,512]{1,0:T(8,128)(2,1)S(1)}, bf16[512,512]{1,0:T(8,128)(2,1)S(1)}, u32[]{:S(2)}, u32[]{:S(2)}) collective-permute-start(bf16[512,512]{1,0:T(8,128)(2,1)S(1)} %pad_maximum_fusion), channel_id=1, source_target_pairs={{0,6},{1,7},{2,0},{3,1},{4,2},{5,3},{6,4},{7,5},{8,14},{9,15},{10,... | collective-permute-start | bytes 1572872 | tf_op jit(solution)/shard_map/ppermute | solution.py:135
  112.8 3.7 %collective-permute-done.15 = bf16[256,512]{1,0:T(8,128)(2,1)S(1)} collective-permute-done((bf16[256,512]{1,0:T(8,128)(2,1)S(1)}, bf16[256,512]{1,0:T(8,128)(2,1)S(1)}, u32[]{:S(2)}, u32[]{:S(2)}) %collective-permute-start.15) | collective-permute-done | bytes 262176 | tf_op jit(solution)/shard_map/ppermute | solution.py:135
  116.7 3.0 %collective-permute-start.16 = (bf16[512,512]{1,0:T(8,128)(2,1)S(1)}, bf16[512,512]{1,0:T(8,128)(2,1)S(1)}, u32[]{:S(2)}, u32[]{:S(2)}) collective-permute-start(bf16[512,512]{1,0:T(8,128)(2,1)S(1)} %pad_maximum_fusion.1), channel_id=1, source_target_pairs={{0,1},{1,0},{2,3},{3,2},{4,5},{5,4},{6,7},{7,6},{8,9},{9,8},{10,11... | collective-permute-start | bytes 1572872 | tf_op jit(solution)/shard_map/ppermute | solution.py:140
  119.7 2.7 %project_out.2 = (bf16[512,512]{1,0:T(8,128)(2,1)S(1)}, bf16[512,512]{1,0:T(8,128)(2,1)S(1)}, bf16[512,512]{1,0:T(8,128)(2,1)S(1)}, bf16[512,512]{1,0:T(8,128)(2,1)S(1)}) custom-call(s32[4]{0:T(128)S(1)} %pad_add_fusion.owners, bf16[512,512]{1,0:T(8,128)(2,1)S(1)} %get-tuple-element.20.g, bf16[512,4096]{1,0:T(8,128)(2,1)S(1)} %copy-done.3), custom_call_target="tpu_custom_call" | custom-call | flops 1073741824 | bytes 4194304 | tf_op jit(solution)/shard_map/project_out/pallas_call | solution.py:288
  122.5 2.7 %collective-permute-done.12 = bf16[512,512]{1,0:T(8,128)(2,1)S(1)} collective-permute-done((bf16[512,512]{1,0:T(8,128)(2,1)S(1)}, bf16[512,512]{1,0:T(8,128)(2,1)S(1)}, u32[]{:S(2)}, u32[]{:S(2)}) %collective-permute-start.12) | collective-permute-done | bytes 524320 | tf_op jit(solution)/shard_map/ppermute | solution.py:135
  125.3 2.8 %collective-permute-start.13 = (bf16[512,512]{1,0:T(8,128)(2,1)S(1)}, bf16[512,512]{1,0:T(8,128)(2,1)S(1)}, u32[]{:S(2)}, u32[]{:S(2)}) collective-permute-start(bf16[512,512]{1,0:T(8,128)(2,1)S(1)} %add_convert_fusion.2), channel_id=1, source_target_pairs={{0,1},{1,0},{2,3},{3,2},{4,5},{5,4},{6,7},{7,6},{8,9},{9,8},{10,11... | collective-permute-start | bytes 1572872 | tf_op jit(solution)/shard_map/ppermute | solution.py:140
  128.1 4.3 %collective-permute-done.16 = bf16[512,512]{1,0:T(8,128)(2,1)S(1)} collective-permute-done((bf16[512,512]{1,0:T(8,128)(2,1)S(1)}, bf16[512,512]{1,0:T(8,128)(2,1)S(1)}, u32[]{:S(2)}, u32[]{:S(2)}) %collective-permute-start.16) | collective-permute-done | bytes 524320 | tf_op jit(solution)/shard_map/ppermute | solution.py:140
  132.7 1.1 collective-permute-done.10
  133.8 5.9 %collective-permute-done.13 = bf16[512,512]{1,0:T(8,128)(2,1)S(1)} collective-permute-done((bf16[512,512]{1,0:T(8,128)(2,1)S(1)}, bf16[512,512]{1,0:T(8,128)(2,1)S(1)}, u32[]{:S(2)}, u32[]{:S(2)}) %collective-permute-start.13) | collective-permute-done | bytes 524320 | tf_op jit(solution)/shard_map/ppermute | solution.py:140
  139.7 3.4 %collective-permute-done.17 = bf16[512,512]{1,0:T(8,128)(2,1)S(1)} collective-permute-done((bf16[512,512]{1,0:T(8,128)(2,1)S(1)}, bf16[512,512]{1,0:T(8,128)(2,1)S(1)}, u32[]{:S(2)}, u32[]{:S(2)}) %collective-permute-start.17) | collective-permute-done | bytes 524320 | tf_op jit(solution)/shard_map/ppermute | solution.py:135
  143.1 1.1 add_convert_fusion
  (59 shorter events, 1.9 us)
Async XLA Ops:
  0.0 14.6 %collective-permute-start.1 = (bf16[512,512]{1,0:T(8,128)(2,1)}, bf16[512,512]{1,0:T(8,128)(2,1)S(1)}, u32[]{:S(2)}, u32[]{:S(2)}) collective-permute-start(bf16[512,512]{1,0:T(8,128)(2,1)} %refs_0_.1), channel_id=1, source_target_pairs={{0,6},{1,7},{2,0},{3,1},{4,2},{5,3},{6,4},{7,5},{8,14},{9,15},{10,... | collective-permute-start | bytes 1572872 | tf_op jit(solution)/shard_map/ppermute | solution.py:135
  3.1 18.1 %collective-permute-start.2 = (bf16[512,512]{1,0:T(8,128)(2,1)}, bf16[512,512]{1,0:T(8,128)(2,1)S(1)}, u32[]{:S(2)}, u32[]{:S(2)}) collective-permute-start(bf16[512,512]{1,0:T(8,128)(2,1)} %refs_0_.1), channel_id=1, source_target_pairs={{0,1},{1,0},{2,3},{3,2},{4,5},{5,4},{6,7},{7,6},{8,9},{9,8},{10,11... | collective-permute-start | bytes 1572872 | tf_op jit(solution)/shard_map/ppermute | solution.py:140
  6.1 15.2 %collective-permute-start = (bf16[512,512]{1,0:T(8,128)(2,1)}, bf16[512,512]{1,0:T(8,128)(2,1)S(1)}, u32[]{:S(2)}, u32[]{:S(2)}) collective-permute-start(bf16[512,512]{1,0:T(8,128)(2,1)} %refs_0_.1), channel_id=1, source_target_pairs={{0,2},{1,3},{2,4},{3,5},{4,6},{5,7},{6,0},{7,1},{8,10},{9,11},{10,... | collective-permute-start | bytes 1572872 | tf_op jit(solution)/shard_map/ppermute | solution.py:135
  6.1 1.2 copy-start.8
  8.4 56.2 %all-to-all-start.1 = ((bf16[16,32,512]{2,1,0:T(8,128)(2,1)}), bf16[16,32,512]{2,1,0:T(8,128)(2,1)}, u32[]{:S(2)}, u32[]{:S(2)}) async-start(bf16[16,32,512]{2,1,0:T(8,128)(2,1)} %bitcast.11), calls=%async_computation.1 | async-start | bytes 1048576 | tf_op jit(solution)/shard_map/all_to_all | solution.py:315
  14.6 20.5 %collective-permute-start.4 = (bf16[512,512]{1,0:T(8,128)(2,1)S(1)}, bf16[512,512]{1,0:T(8,128)(2,1)S(1)}, u32[]{:S(2)}, u32[]{:S(2)}) collective-permute-start(bf16[512,512]{1,0:T(8,128)(2,1)S(1)} %collective-permute-done.1.refs_2_), channel_id=1, source_target_pairs={{0,1},{1,0},{2,3},{3,2},{4,5},{5,4},{6,7},{7,6},{8,9},{9,8},{10,11... | collective-permute-start | bytes 1572872 | tf_op jit(solution)/shard_map/ppermute | solution.py:140
  17.6 21.3 %collective-permute-start.5 = (bf16[512,512]{1,0:T(8,128)(2,1)S(1)}, bf16[512,512]{1,0:T(8,128)(2,1)S(1)}, u32[]{:S(2)}, u32[]{:S(2)}) collective-permute-start(bf16[512,512]{1,0:T(8,128)(2,1)S(1)} %collective-permute-done.1.refs_2_), channel_id=1, source_target_pairs={{0,6},{1,7},{2,0},{3,1},{4,2},{5,3},{6,4},{7,5},{8,14},{9,15},{10,... | collective-permute-start | bytes 1572872 | tf_op jit(solution)/shard_map/ppermute | solution.py:135
  21.2 17.0 %collective-permute-start.3 = (bf16[512,512]{1,0:T(8,128)(2,1)S(1)}, bf16[512,512]{1,0:T(8,128)(2,1)S(1)}, u32[]{:S(2)}, u32[]{:S(2)}) collective-permute-start(bf16[512,512]{1,0:T(8,128)(2,1)S(1)} %collective-permute-done.2.refs_3_), channel_id=1, source_target_pairs={{0,2},{1,3},{2,4},{3,5},{4,6},{5,7},{6,0},{7,1},{8,10},{9,11},{10,... | collective-permute-start | bytes 1572872 | tf_op jit(solution)/shard_map/ppermute | solution.py:135
  21.4 4.6 %copy-start = (bf16[4096,3,512]{2,0,1:T(8,128)(2,1)S(1)}, bf16[4096,3,512]{2,0,1:T(8,128)(2,1)}, u32[]{:S(2)}) copy-start(bf16[4096,3,512]{2,0,1:T(8,128)(2,1)} %param.12) | copy-start | bytes 37748740
  26.0 1.0 copy-start.9
  27.0 11.9 %copy-start.1 = (bf16[4096,3,512]{2,0,1:T(8,128)(2,1)S(1)}, bf16[4096,3,512]{2,0,1:T(8,128)(2,1)}, u32[]{:S(2)}) copy-start(bf16[4096,3,512]{2,0,1:T(8,128)(2,1)} %param.12) | copy-start | bytes 37748740
  35.8 17.7 %collective-permute-start.7 = (bf16[256,512]{1,0:T(8,128)(2,1)}, bf16[256,512]{1,0:T(8,128)(2,1)S(1)}, u32[]{:S(2)}, u32[]{:S(2)}) collective-permute-start(bf16[256,512]{1,0:T(8,128)(2,1)} %slice.41), channel_id=1, source_target_pairs={{0,6},{1,7},{2,0},{3,1},{4,2},{5,3},{6,4},{7,5},{8,14},{9,15},{10,... | collective-permute-start | bytes 786440 | tf_op jit(solution)/shard_map/ppermute | solution.py:135
  38.9 14.6 %copy-start.11 = (f32[3,3,512]{2,1,0:T(4,128)S(1)}, f32[3,3,512]{2,1,0:T(4,128)}, u32[]{:S(2)}) copy-start(f32[3,3,512]{2,1,0:T(4,128)} %taps.1) | copy-start | bytes 55300
  38.9 14.6 %collective-permute-start.6 = (bf16[256,512]{1,0:T(8,128)(2,1)}, bf16[256,512]{1,0:T(8,128)(2,1)}, u32[]{:S(2)}, u32[]{:S(2)}) collective-permute-start(bf16[256,512]{1,0:T(8,128)(2,1)} %slice.40), channel_id=1, source_target_pairs={{0,2},{1,3},{2,4},{3,5},{4,6},{5,7},{6,0},{7,1},{8,10},{9,11},{10,... | collective-permute-start | bytes 786440 | tf_op jit(solution)/shard_map/ppermute | solution.py:135
  43.1 10.4 %collective-permute-start.9 = (f32[3,16,512]{2,1,0:T(8,128)}, f32[3,16,512]{2,1,0:T(8,128)S(1)}, u32[]{:S(2)}, u32[]{:S(2)}) collective-permute-start(f32[3,16,512]{2,1,0:T(8,128)} %slice.42), channel_id=1, source_target_pairs={{0,8},{8,16},{16,24},{24,32},{32,40},{40,48},{48,56},{56,64},{64,7... | collective-permute-start | bytes 294920 | tf_op jit(solution)/shard_map/ppermute | solution.py:130
  45.3 8.2 %collective-permute-start.8 = (bf16[16,512]{1,0:T(8,128)(2,1)}, bf16[16,512]{1,0:T(8,128)(2,1)S(1)}, u32[]{:S(2)}, u32[]{:S(2)}) collective-permute-start(bf16[16,512]{1,0:T(8,128)(2,1)} %slice.32), channel_id=1, source_target_pairs={{0,13},{1,12},{2,15},{3,14},{4,9},{5,8},{6,11},{7,10},{8,21},{9,20... | collective-permute-start | bytes 49160 | tf_op jit(solution)/shard_map/ppermute | solution.py:146
  53.5 4.6 %copy-start.2 = (bf16[4096,3,512]{2,0,1:T(8,128)(2,1)S(1)}, bf16[4096,3,512]{2,0,1:T(8,128)(2,1)}, u32[]{:S(2)}) copy-start(bf16[4096,3,512]{2,0,1:T(8,128)(2,1)} %param.12) | copy-start | bytes 37748740
  61.8 1.0 copy-start.4
  62.8 1.0 copy-start.6
  63.8 0.8 copy-start.10
  64.6 19.3 %all-to-all-start = ((bf16[16,32,512]{2,1,0:T(8,128)(2,1)}), bf16[16,32,512]{2,1,0:T(8,128)(2,1)S(1)}, u32[]{:S(2)}, u32[]{:S(2)}) async-start(bf16[16,32,512]{2,1,0:T(8,128)(2,1)} %bitcast.25), calls=%async_computation | async-start | bytes 1048576 | tf_op jit(solution)/shard_map/all_to_all | solution.py:326
  73.1 0.9 copy-start.13
  74.0 0.9 copy-start.16
  74.8 0.8 copy-start.18
  75.6 8.3 %copy-start.14 = (bf16[256,256]{1,0:T(8,128)(2,1)S(1)}, bf16[256,256]{1,0:T(8,128)(2,1)}, u32[]{:S(2)}) copy-start(bf16[256,256]{1,0:T(8,128)(2,1)} %constant.73.clone.forward) | copy-start | bytes 393220
  75.6 8.3 %copy-start.15 = (bf16[256,256]{1,0:T(8,128)(2,1)S(1)}, bf16[256,256]{1,0:T(8,128)(2,1)}, u32[]{:S(2)}) copy-start(bf16[256,256]{1,0:T(8,128)(2,1)} %constant.74.clone.backward) | copy-start | bytes 393220
  75.6 8.3 %copy-start.17 = (f32[2,72,128]{2,1,0:T(8,128)S(1)}, f32[2,72,128]{2,1,0:T(8,128)}, u32[]{:S(2)}) copy-start(f32[2,72,128]{2,1,0:T(8,128)} %constant.72.clone.tw) | copy-start | bytes 221188
  75.6 8.3 %copy-start.19 = (bf16[64,144]{1,0:T(8,128)(2,1)S(1)}, bf16[64,144]{1,0:T(8,128)(2,1)}, u32[]{:S(2)}) copy-start(bf16[64,144]{1,0:T(8,128)(2,1)} %constant.75.clone.last) | copy-start | bytes 55300
  83.9 16.9 %copy-start.3 = (bf16[512,4096]{1,0:T(8,128)(2,1)S(1)}, bf16[512,4096]{1,0:T(8,128)(2,1)}, u32[]{:S(2)}) copy-start(bf16[512,4096]{1,0:T(8,128)(2,1)} %weight.5) | copy-start | bytes 12582916
  84.0 16.9 %copy-start.5 = (f32[512,512]{1,0:T(8,128)S(1)}, f32[512,512]{1,0:T(8,128)}, u32[]{:S(2)}) copy-start(f32[512,512]{1,0:T(8,128)} %copy-done.4) | copy-start | bytes 3145732
  84.0 16.9 %copy-start.7 = (f32[512,512]{1,0:T(8,128)S(1)}, f32[512,512]{1,0:T(8,128)}, u32[]{:S(2)}) copy-start(f32[512,512]{1,0:T(8,128)} %copy-done.6) | copy-start | bytes 3145732
  84.0 16.9 %copy-start.12 = (f32[512]{0:T(512)S(1)}, f32[512]{0:T(512)}, u32[]{:S(2)}) copy-start(f32[512]{0:T(512)} %param.15) | copy-start | bytes 6148
  101.8 7.6 %collective-permute-start.11 = (bf16[256,512]{1,0:T(8,128)(2,1)S(1)}, bf16[256,512]{1,0:T(8,128)(2,1)S(1)}, u32[]{:S(2)}, u32[]{:S(2)}) collective-permute-start(bf16[256,512]{1,0:T(8,128)(2,1)S(1)} %get-tuple-element.29), channel_id=1, source_target_pairs={{0,6},{1,7},{2,0},{3,1},{4,2},{5,3},{6,4},{7,5},{8,14},{9,15},{10,... | collective-permute-start | bytes 786440 | tf_op jit(solution)/shard_map/ppermute | solution.py:135
  106.0 10.5 %collective-permute-start.15 = (bf16[256,512]{1,0:T(8,128)(2,1)S(1)}, bf16[256,512]{1,0:T(8,128)(2,1)S(1)}, u32[]{:S(2)}, u32[]{:S(2)}) collective-permute-start(bf16[256,512]{1,0:T(8,128)(2,1)S(1)} %get-tuple-element.30), channel_id=1, source_target_pairs={{0,2},{1,3},{2,4},{3,5},{4,6},{5,7},{6,0},{7,1},{8,10},{9,11},{10,... | collective-permute-start | bytes 786440 | tf_op jit(solution)/shard_map/ppermute | solution.py:135
  106.2 22.0 %collective-permute-start.14 = (bf16[512,512]{1,0:T(8,128)(2,1)S(1)}, bf16[512,512]{1,0:T(8,128)(2,1)S(1)}, u32[]{:S(2)}, u32[]{:S(2)}) collective-permute-start(bf16[512,512]{1,0:T(8,128)(2,1)S(1)} %get-tuple-element.27), channel_id=1, source_target_pairs={{0,2},{1,3},{2,4},{3,5},{4,6},{5,7},{6,0},{7,1},{8,10},{9,11},{10,... | collective-permute-start | bytes 1572872 | tf_op jit(solution)/shard_map/ppermute | solution.py:135
  109.6 15.6 %collective-permute-start.12 = (bf16[512,512]{1,0:T(8,128)(2,1)S(1)}, bf16[512,512]{1,0:T(8,128)(2,1)S(1)}, u32[]{:S(2)}, u32[]{:S(2)}) collective-permute-start(bf16[512,512]{1,0:T(8,128)(2,1)S(1)} %pad_maximum_fusion), channel_id=1, source_target_pairs={{0,6},{1,7},{2,0},{3,1},{4,2},{5,3},{6,4},{7,5},{8,14},{9,15},{10,... | collective-permute-start | bytes 1572872 | tf_op jit(solution)/shard_map/ppermute | solution.py:135
  116.7 15.7 %collective-permute-start.16 = (bf16[512,512]{1,0:T(8,128)(2,1)S(1)}, bf16[512,512]{1,0:T(8,128)(2,1)S(1)}, u32[]{:S(2)}, u32[]{:S(2)}) collective-permute-start(bf16[512,512]{1,0:T(8,128)(2,1)S(1)} %pad_maximum_fusion.1), channel_id=1, source_target_pairs={{0,1},{1,0},{2,3},{3,2},{4,5},{5,4},{6,7},{7,6},{8,9},{9,8},{10,11... | collective-permute-start | bytes 1572872 | tf_op jit(solution)/shard_map/ppermute | solution.py:140
  122.4 11.4 %collective-permute-start.10 = (bf16[512,512]{1,0:T(8,128)(2,1)S(1)}, bf16[512,512]{1,0:T(8,128)(2,1)S(1)}, u32[]{:S(2)}, u32[]{:S(2)}) collective-permute-start(bf16[512,512]{1,0:T(8,128)(2,1)S(1)} %get-tuple-element.22), channel_id=1, source_target_pairs={{0,6},{1,7},{2,0},{3,1},{4,2},{5,3},{6,4},{7,5},{8,14},{9,15},{10,... | collective-permute-start | bytes 1572872 | tf_op jit(solution)/shard_map/ppermute | solution.py:135
  125.3 14.3 %collective-permute-start.13 = (bf16[512,512]{1,0:T(8,128)(2,1)S(1)}, bf16[512,512]{1,0:T(8,128)(2,1)S(1)}, u32[]{:S(2)}, u32[]{:S(2)}) collective-permute-start(bf16[512,512]{1,0:T(8,128)(2,1)S(1)} %add_convert_fusion.2), channel_id=1, source_target_pairs={{0,1},{1,0},{2,3},{3,2},{4,5},{5,4},{6,7},{7,6},{8,9},{9,8},{10,11... | collective-permute-start | bytes 1572872 | tf_op jit(solution)/shard_map/ppermute | solution.py:140
  132.6 10.5 %collective-permute-start.17 = (bf16[512,512]{1,0:T(8,128)(2,1)S(1)}, bf16[512,512]{1,0:T(8,128)(2,1)S(1)}, u32[]{:S(2)}, u32[]{:S(2)}) collective-permute-start(bf16[512,512]{1,0:T(8,128)(2,1)S(1)} %add_convert_fusion.1), channel_id=1, source_target_pairs={{0,2},{1,3},{2,4},{3,5},{4,6},{5,7},{6,0},{7,1},{8,10},{9,11},{10,... | collective-permute-start | bytes 1572872 | tf_op jit(solution)/shard_map/ppermute | solution.py:135

commit v3 on v2

v3 whole, which is shorter than its diff:
```python
import functools

import numpy as np
import jax
import jax.numpy as jnp
import ml_dtypes
from jax import lax
from jax.experimental import pallas as pl
from jax.experimental.pallas import tpu as pltpu
from jax.sharding import PartitionSpec as P

K1 = 72
GROUP = 8


def fourier_tables(seqs, rows):
    total = 2 * seqs * rows
    fine = 128
    coarse = total // fine
    half = coarse // 2
    per = rows // fine
    n1 = (np.arange(seqs)[None, :] * per + np.arange(per)[:, None]).reshape(-1)
    k1 = np.arange(half + 1)
    ang = 2 * np.pi * ((k1[:, None] * n1[None, :]) % coarse) / coarse
    pad = ((0, K1 - half - 1), (0, 0))
    first = np.concatenate([np.pad(np.cos(ang), pad), np.pad(-np.sin(ang), pad)])
    weight = np.where((k1 == 0) | (k1 == half), 1.0, 2.0)[:, None]
    last = np.concatenate([np.pad(weight * np.cos(ang), pad), np.pad(-weight * np.sin(ang), pad)]).T
    n2 = np.arange(fine)
    tw = 2 * np.pi * (k1[:, None] * n2[None, :]) / total
    tw_cos, tw_sin = np.pad(np.cos(tw), pad), np.pad(np.sin(tw), pad)
    ang2 = 2 * np.pi * ((n2[:, None] * n2[None, :]) % fine) / fine
    c, s = np.cos(ang2), np.sin(ang2)
    forward = np.block([[c, -s], [s, c]])
    backward = np.block([[c, s], [-s, c]])
    bf = ml_dtypes.bfloat16
    twiddle = np.stack([tw_cos, tw_sin]).astype(np.float32)
    return first.astype(bf), twiddle, forward.astype(bf), backward.astype(bf), last.astype(bf)


def spectrum_of(xs, base, seqs, chans, first, tw, forward):
    cols = []
    for i in range(GROUP):
        cols.append(jnp.concatenate([xs[p, pl.ds(base + i, seqs, stride=chans), :] for p in range(xs.shape[0])], axis=0))
    x = jnp.concatenate(cols, axis=1).astype(jnp.bfloat16)
    s = jnp.dot(first[...], x, preferred_element_type=jnp.float32)
    tc, ts = tw[0], tw[1]
    z = []
    for i in range(GROUP):
        re, im = s[:K1, i * 128:(i + 1) * 128], s[K1:, i * 128:(i + 1) * 128]
        z.append(jnp.concatenate([re * tc + im * ts, im * tc - re * ts], axis=1))
    z = jnp.concatenate(z, axis=0).astype(jnp.bfloat16)
    return jnp.dot(z, forward[...], preferred_element_type=jnp.float32)


def filter_kernel(seqs, chans, x_ref, first, tw, forward, out, xs, held, sems):
    for p in range(xs.shape[0]):
        xs[p] = x_ref[:, p * 128:(p + 1) * 128].astype(jnp.float32)

    @pl.loop(0, chans // GROUP)
    def _(g):
        held[g] = spectrum_of(xs, g * GROUP, seqs, chans, first, tw, forward).astype(jnp.bfloat16)
        pltpu.make_async_copy(held.at[g], out.at[g], sems.at[g]).start()

    @pl.loop(0, chans // GROUP)
    def _(g):
        pltpu.make_async_copy(held.at[g], out.at[g], sems.at[g]).wait()


def conv_kernel(seqs, chans, scale, x_ref, h_ref, first, tw, forward, backward, last, out, xs, ys, held, sems):
    for g in range(chans // GROUP):
        pltpu.make_async_copy(h_ref.at[g], held.at[g], sems.at[g]).start()
    for p in range(xs.shape[0]):
        xs[p] = x_ref[:, p * 128:(p + 1) * 128].astype(jnp.float32)

    @pl.loop(0, chans // GROUP)
    def _(g):
        q = spectrum_of(xs, g * GROUP, seqs, chans, first, tw, forward)
        pltpu.make_async_copy(h_ref.at[g], held.at[g], sems.at[g]).wait()
        h = held[g].astype(jnp.float32)
        qr, qi, hr, hi = q[:, :128], q[:, 128:], h[:, :128], h[:, 128:]
        p = jnp.concatenate([qr * hr - qi * hi, qr * hi + qi * hr], axis=1).astype(jnp.bfloat16)
        u = jnp.dot(p, backward[...], preferred_element_type=jnp.float32)
        tc, ts = tw[0] * scale, tw[1] * scale
        v = []
        for i in range(GROUP):
            re, im = u[i * K1:(i + 1) * K1, :128], u[i * K1:(i + 1) * K1, 128:]
            v.append(jnp.concatenate([re * tc - im * ts, im * tc + re * ts], axis=0))
        v = jnp.concatenate(v, axis=1).astype(jnp.bfloat16)
        y = jnp.dot(last[...], v, preferred_element_type=jnp.float32)
        for i in range(GROUP):
            yi = y[:, i * 128:(i + 1) * 128]
            for p in range(ys.shape[0]):
                ys[p, pl.ds(g * GROUP + i, seqs, stride=chans), :] = yi[p * seqs:(p + 1) * seqs]

    for p in range(ys.shape[0]):
        out[:, p * 128:(p + 1) * 128] = ys[p].astype(jnp.bfloat16)


def whole():
    return pl.BlockSpec(memory_space=pltpu.VMEM)

def params(mib):
    return pltpu.CompilerParams(vmem_limit_bytes=mib * 1024 * 1024)


def filter_spectrum(x, tables, seqs):
    chans = x.shape[0] // seqs
    first, tw, forward, _, _ = tables
    shape = (chans // GROUP, GROUP * K1, 256)
    return pl.pallas_call(
        functools.partial(filter_kernel, seqs, chans),
        out_shape=pltpu.HBM(shape, jnp.bfloat16),
        in_specs=[whole()] * 4, out_specs=in_hbm(),
        scratch_shapes=[
            pltpu.VMEM((x.shape[1] // 128, x.shape[0], 128), jnp.float32),
            pltpu.VMEM(shape, jnp.bfloat16),
            pltpu.SemaphoreType.DMA(shape[:1]),
        ],
        compiler_params=params(10),
        name="filter_spectrum",
        cost_estimate=pl.CostEstimate(flops=4_000_000_000, bytes_accessed=4_000_000, transcendentals=0),
    )(x, first, tw, forward)


def convolve(x, spec, tables, seqs):
    rows = x.shape[1]
    chans = x.shape[0] // seqs
    first, tw, forward, backward, last = tables
    return pl.pallas_call(
        functools.partial(conv_kernel, seqs, chans, 1.0 / (2 * seqs * rows)),
        out_shape=jax.ShapeDtypeStruct(x.shape, jnp.bfloat16),
        in_specs=[whole(), in_hbm()] + [whole()] * 5, out_specs=whole(),
        scratch_shapes=[pltpu.VMEM((x.shape[1] // 128, x.shape[0], 128), jnp.float32)] * 2
        + [pltpu.VMEM(spec.shape, spec.dtype), pltpu.SemaphoreType.DMA(spec.shape[:1])],
        compiler_params=params(12),
        name="convolve",
        cost_estimate=pl.CostEstimate(flops=5_000_000_000, bytes_accessed=4_000_000, transcendentals=0),
    )(x, from_hbm(spec), first, tw, forward, backward, last)


def shifted(array, axis, by):
    count = lax.axis_size(axis)
    pairs = [(i, i + by) for i in range(count) if 0 <= i + by < count]
    return lax.ppermute(array, axis, pairs)


def ring(array, by):
    count = lax.axis_size("chan")
    return lax.ppermute(array, "chan", [(i, (i + 2 * by) % count) for i in range(count)])


def cross(array):
    count = lax.axis_size("chan")
    return lax.ppermute(array, "chan", [(i, i ^ 1) for i in range(count)])


def following(array):
    seqs, count = lax.axis_size("seq"), lax.axis_size("chan")
    pairs = [(s * count + c, (s + 1) * count + (c - 2) % count) for s in range(seqs - 1) for c in range(count)]
    return lax.ppermute(array, ("seq", "chan"), pairs)


def transpose_kernel(x_ref, out):
    out[...] = x_ref[...].T.astype(jnp.bfloat16)


def transposed(x):
    return pl.pallas_call(
        transpose_kernel,
        out_shape=jax.ShapeDtypeStruct(x.shape[::-1], jnp.bfloat16),
        in_specs=[whole()], out_specs=whole(),
        compiler_params=params(8), name="transposed",
        cost_estimate=pl.CostEstimate(flops=0, bytes_accessed=6 * x.size, transcendentals=0),
    )(x)


def owner(dy, dx):
    count = lax.axis_size("chan")
    return jnp.bitwise_xor(lax.rem(lax.axis_index("chan") + 2 * (dy % (count // 2)), count), dx)


def from_hbm(array):
    return pltpu.with_memory_space_constraint(array, pltpu.HBM)


def in_hbm():
    return pl.BlockSpec(memory_space=pltpu.HBM)


def in_vmem(array):
    return pltpu.with_memory_space_constraint(array, pltpu.VMEM)


def rows_of(weight, j, place, depth):
    start = pl.multiple_of(owner(*place) * depth, depth)
    return weight[j, pl.ds(start, depth), :]


def round_kernel(places, has_acc, tail, *refs):
    refs = list(refs)
    acc = refs.pop(0) if has_acc else None
    blocks = [refs.pop(0) for _ in places]
    weight, out, *tail_out = refs
    for j in range(out.shape[0]):
        total = acc[j] if has_acc else None
        for block, place in zip(blocks, places):
            term = jnp.dot(block[...], rows_of(weight, j, place, block.shape[1]), preferred_element_type=jnp.float32)
            total = term if total is None else total + term
        out[j] = total
        if tail:
            tail_out[0][j] = total[total.shape[0] - tail:]


def project_round(acc, blocks, places, weight, tail=0):
    branches, _, width = weight.shape
    rows, depth = blocks[0].shape
    count = len(blocks)
    args = ([acc] if acc is not None else []) + blocks
    return pl.pallas_call(
        functools.partial(round_kernel, places, acc is not None, tail),
        out_shape=[jax.ShapeDtypeStruct((branches, n, width), jnp.float32) for n in ((rows, tail) if tail else (rows,))],
        in_specs=[whole()] * (len(args) + 1),
        out_specs=[whole()] * (2 if tail else 1),
        compiler_params=params(10), name="project_round",
        cost_estimate=pl.CostEstimate(flops=2 * count * rows * depth * branches * width, bytes_accessed=2 * count * depth * branches * width, transcendentals=0),
    )(*args, in_vmem(weight))


def signal_kernel(place, acc, lo, hi, halo, halo_acc, weight, taps, signal_t, signal, gate_out, sig_t, sig, gate, out_sems):
    branches, rows, width = acc.shape
    lead = halo.shape[0]
    block = jnp.concatenate([lo[...], hi[...]], axis=0)
    cols = 256
    outs = []
    for c in range(0, width, cols):
        short = []
        for j in range(branches):
            w = rows_of(weight, j, place, block.shape[1])[:, c:c + cols]
            here = acc[j, :, c:c + cols] + jnp.dot(block, w, preferred_element_type=jnp.float32)
            before = halo_acc[j, :, c:c + cols] + jnp.dot(halo[...], w, preferred_element_type=jnp.float32)
            here, before = [p.astype(jnp.bfloat16).astype(jnp.float32) for p in (here, before)]
            ext = jnp.concatenate([before, here], axis=0)
            tap = [taps[k, j:j + 1, c:c + cols] for k in range(3)]
            short.append(tap[0] * ext[lead - 2:lead - 2 + rows] + tap[1] * ext[lead - 1:lead - 1 + rows] + tap[2] * here)
        s = short[2] * short[1]
        k = c // cols
        sig_t[c:c + cols, :] = s.T.astype(jnp.bfloat16)
        sig[k] = s
        gate[k] = short[0]
        pairs = ((sig_t.at[c:c + cols, :], signal_t.at[c:c + cols, :]), (sig.at[k], signal.at[:, c:c + cols]), (gate.at[k], gate_out.at[:, c:c + cols]))
        for i, (src, dst) in enumerate(pairs):
            outs.append(pltpu.make_async_copy(src, dst, out_sems.at[i, k]))
            outs[-1].start()
    for copy in outs:
        copy.wait()


def signal_of(acc, lo, hi, halo, halo_acc, place, weight, taps):
    branches, rows, width = acc.shape
    depth = lo.shape[1]
    parts = width // 256
    return pl.pallas_call(
        functools.partial(signal_kernel, place),
        out_shape=[pltpu.HBM((width, rows), jnp.bfloat16)] + [pltpu.HBM((rows, width), jnp.float32)] * 2,
        in_specs=[whole()] * 7,
        out_specs=[in_hbm()] * 3,
        scratch_shapes=[
            pltpu.VMEM((width, rows), jnp.bfloat16),
            pltpu.VMEM((parts, rows, 256), jnp.float32),
            pltpu.VMEM((parts, rows, 256), jnp.float32),
            pltpu.SemaphoreType.DMA((3, parts)),
        ],
        compiler_params=params(12), name="signal_of",
        cost_estimate=pl.CostEstimate(flops=2 * rows * depth * branches * width, bytes_accessed=16 * rows * width, transcendentals=0),
    )(acc, lo, hi, halo, halo_acc, in_vmem(weight), taps)


def fetch_columns(weight, at, held, sem):
    cols = held.shape[1]
    start = pl.multiple_of(at * cols, cols)
    return pltpu.make_async_copy(weight.at[:, pl.ds(start, cols)], held, sem)


def gate_kernel(places, conv, signal, gate_out, skip, weight, gated, *refs):
    outs, (held, sems) = refs[:-2], refs[-2:]
    copies = [fetch_columns(weight, owner(*p), held.at[k], sems.at[k]) for k, p in enumerate(places)]
    for copy in copies:
        copy.start()
    total = conv[...].astype(jnp.float32).T + skip[...] * signal[...]
    g = (total * gate_out[...]).astype(jnp.bfloat16)
    gated[...] = g
    half = outs[0].shape[0]
    for k in range(len(places)):
        copies[k].wait()
        outs[2 * k][...] = jnp.dot(g[:half], held[k], preferred_element_type=jnp.float32).astype(jnp.bfloat16)
        outs[2 * k + 1][...] = jnp.dot(g[half:], held[k], preferred_element_type=jnp.float32).astype(jnp.bfloat16)


def gate_and_project(conv, signal, gate_out, skip, places, weight, cols):
    width, rows = conv.shape
    count = len(places)
    return pl.pallas_call(
        functools.partial(gate_kernel, places),
        out_shape=[jax.ShapeDtypeStruct((rows, width), jnp.bfloat16)] + [jax.ShapeDtypeStruct((rows // 2, cols), jnp.bfloat16)] * (2 * count),
        in_specs=[whole()] * 4 + [in_hbm()],
        out_specs=[whole()] * (1 + 2 * count),
        scratch_shapes=[pltpu.VMEM((count, width, cols), jnp.bfloat16), pltpu.SemaphoreType.DMA((count,))],
        compiler_params=params(10), name="gate_and_project",
        cost_estimate=pl.CostEstimate(flops=2 * count * rows * width * cols, bytes_accessed=12 * rows * width, transcendentals=0),
    )(conv, signal, gate_out, skip, weight)


def out_kernel(places, pieces, g, weight, *refs):
    count = len(places)
    outs, (held, sems) = list(refs[:sum(pieces)]), refs[sum(pieces):]
    copies = [fetch_columns(weight, owner(*p), held.at[k], sems.at[k]) for k, p in enumerate(places)]
    for copy in copies:
        copy.start()
    for k in range(count):
        copies[k].wait()
        for p in range(pieces[k]):
            out = outs.pop(0)
            part = out.shape[0]
            out[...] = jnp.dot(g[p * part:(p + 1) * part], held[k], preferred_element_type=jnp.float32).astype(jnp.bfloat16)


def project_out(gated, places, pieces, weight, cols):
    rows, width = gated.shape
    count = len(places)
    return pl.pallas_call(
        functools.partial(out_kernel, places, pieces),
        out_shape=[jax.ShapeDtypeStruct((rows // n, cols), jnp.bfloat16) for n in pieces for _ in range(n)],
        in_specs=[whole(), in_hbm()],
        out_specs=[whole()] * sum(pieces),
        scratch_shapes=[pltpu.VMEM((count, width, cols), jnp.bfloat16), pltpu.SemaphoreType.DMA((count,))],
        compiler_params=params(10), name="project_out",
        cost_estimate=pl.CostEstimate(flops=2 * count * rows * width * cols, bytes_accessed=4 * count * width * cols, transcendentals=0),
    )(gated, weight)


def added(*terms):
    return sum(t.astype(jnp.float32) for t in terms).astype(jnp.bfloat16)


def shards(tables, tokens, in_weight, short_weight, long_filter, skip_gain, out_weight):
    count = lax.axis_size("chan")
    seqs = lax.axis_size("seq")
    rows, width = tokens.shape
    half = rows // 2
    cols = out_weight.shape[1] // count
    weight = jnp.transpose(in_weight, (1, 0, 2))
    together = lax.optimization_barrier

    above, side, below = ring(tokens, -1), cross(tokens), ring(tokens, 1)
    above, side, below, fil = together((above, side, below, transposed(long_filter)))
    far, side_above, side_below = ring(above, -1), cross(above), ring(side, 1)
    fil = lax.all_to_all(fil, "seq", 0, 0, tiled=True)
    acc, = project_round(None, [tokens, below, above, side], [(0, 0), (-1, 0), (1, 0), (0, 1)], weight)
    far, side_above, side_below, acc = together((far, side_above, side_below, acc))
    far_hi, far_lo = ring(side_above[half:], -1), ring(side_below[:half], 1)
    halo = following(side_above[rows - 16:])
    acc, tail = project_round(acc, [side_below, side_above, far], [(-1, 1), (1, 1), (2, 0)], weight, 16)
    halo_acc = shifted(tail, "seq", 1)
    signal_t, signal, gate_out = signal_of(acc, far_lo, far_hi, halo, halo_acc, (2, 1), weight, short_weight)
    spec = filter_spectrum(fil, tables, seqs)

    conv = convolve(lax.all_to_all(signal_t, "seq", 0, 0, tiled=True), spec, tables, seqs)
    conv = lax.all_to_all(conv, "seq", 0, 0, tiled=True)

    skip = skip_gain.reshape(1, width)
    gated, far_side_lo, far_side_hi, up_side_lo, up_side_hi = gate_and_project(conv, signal, gate_out, skip, [(2, 1), (1, 1)], out_weight, cols)
    to_hi, to_lo, up_side_lo = ring(far_side_hi, 1), ring(far_side_lo, -1), cross(up_side_lo)
    down_side, far = project_out(gated, [(-1, 1), (2, 0)], (1, 1), out_weight, cols)
    up, down, side, own = project_out(gated, [(1, 0), (-1, 0), (0, 1), (0, 0)], (1, 1, 1, 1), out_weight, cols)
    to_hi, to_lo, far, up_side_lo = together((to_hi, to_lo, far, up_side_lo))
    down_side = ring(jnp.concatenate([added(down_side[:half], to_lo), down_side[half:]], axis=0), -1)
    up_side_hi = cross(added(up_side_hi, to_hi))
    far = ring(far, 1)
    down_side, down = together((down_side, down))
    side = cross(added(side, down_side))
    up = added(up, far, jnp.concatenate([up_side_lo, up_side_hi], axis=0))
    up, down = ring(up, 1), ring(down, -1)
    return added(own, down, side, up)


def solution(mesh):
    in_specs = (
        P("seq", "chan"),
        P(None, None, "chan"),
        P(None, None, "chan"),
        P("seq", "chan"),
        P("chan"),
        P("chan", None),
    )
    def run(*args):
        seqs = mesh.shape["seq"]
        tables = tuple(jnp.asarray(t) for t in fourier_tables(seqs, args[0].shape[0] // seqs))
        body = functools.partial(shards, tables)
        return jax.shard_map(body, mesh=mesh, in_specs=in_specs, out_specs=P("seq", "chan"), check_vma=False)(*args)
    return run
```

time: 145 us -> 135 us (0.931)
  local copies, waits for them, and re-layouts: 19.6 us -> 6.96 us
  waiting for transfers between devices: 35.6 us -> 42.1 us
  starting transfers between devices: 48.6 us -> 46.2 us
  Pallas kernels: 24.7 us -> 23.2 us
    unnamed x40 -> x28, local copies, waits for them, and re-layouts: 16.8 us -> 6.9 us
    ppermute x12, waiting for transfers between devices: 14.8 us -> 19.7 us  [ring(): lax.ppermute(array, 'chan', [(i, (i + 2 * by) % count) for i in range(cou...]
    all_to_all x1, starting transfers between devices: 8.43 us -> 4.97 us  [shards(): lax.all_to_all(signal_t, 'seq', 0, 0, tiled=True)]
    slice x6 -> x3, local copies, waits for them, and re-layouts: 2.75 us -> 0.04 us  [the longest x2 0.04 us: shards(): far_hi, far_lo = (ring(side_above[half:], -1), ring(side_below[:half], 1))]
    pallas_call x7, Pallas kernels: 20.2 us -> 17.5 us  [the longest x2 6 us: project_round(): pl.pallas_call(functools.partial(round_kernel, places, acc is not None, t...]
    all_to_all x1, waiting for transfers between devices: 5.29 us -> 7.06 us  [shards(): lax.all_to_all(signal_t, 'seq', 0, 0, tiled=True)]
    ppermute x4 -> x5, starting transfers between devices: 11.9 us -> 12.7 us  [cross(): return lax.ppermute(array, 'chan', [(i, i ^ 1) for i in range(count)])]
    ppermute x4 -> x5, waiting for transfers between devices: 13.8 us -> 13.9 us  [cross(): return lax.ppermute(array, 'chan', [(i, i ^ 1) for i in range(count)])]
  transfers between devices with their start and end apart: 20 -> 21, of which waited for: 11 -> 11; matrix products, arithmetic and copies ran while one was open for 2% -> 0% of each run, Pallas kernels for 14% -> 13%
where the time goes in v3:
time: 135 us; the launch traced here: 134 us
  starting transfers between devices  46.2 us (34%)
  waiting for transfers between devices  42.1 us (31%)
  Pallas kernels  23.2 us (17%)
  blocking collectives  13.5 us (10%)
  local copies, waits for them, and re-layouts  6.96 us (5%)
  other arithmetic  1.57 us (1%)
    ppermute x12, waiting for transfers between devices, ring(): lax.ppermute(array, 'chan', [(i, (i + 2 * by) % count) for i in range(cou...  19.7 us
    ppermute x12, starting transfers between devices, ring(): lax.ppermute(array, 'chan', [(i, (i + 2 * by) % count) for i in range(cou...  14.5 us
    ppermute x5, waiting for transfers between devices, cross(): return lax.ppermute(array, 'chan', [(i, i ^ 1) for i in range(count)])  13.9 us
    all_to_all x1, blocking collectives, shards(): conv = lax.all_to_all(conv, 'seq', 0, 0, tiled=True)  13.5 us
    ppermute x5, starting transfers between devices, cross(): return lax.ppermute(array, 'chan', [(i, i ^ 1) for i in range(count)])  12.7 us
    all_to_all x1, waiting for transfers between devices, shards(): lax.all_to_all(signal_t, 'seq', 0, 0, tiled=True)  7.06 us
    unnamed x28, local copies, waits for them, and re-layouts  6.9 us
    all_to_all x1, starting transfers between devices, shards(): fil = lax.all_to_all(fil, 'seq', 0, 0, tiled=True)  6.33 us
  transfers between devices with their start and end apart: 21, of which 11 were waited for; matrix products, arithmetic and copies ran while one was open for 0% of the time, Pallas kernels for 13%

profile of v3, /device:TPU:0, one launch (start us, length us, event | category | flops | bytes accessed | tf_op | source)
XLA Modules:
  0.0 133.9 jit_solution(11322951227560531405)
XLA Ops:
  0.0 3.1 %collective-permute-start = (bf16[512,512]{1,0:T(8,128)(2,1)}, bf16[512,512]{1,0:T(8,128)(2,1)S(1)}, u32[]{:S(2)}, u32[]{:S(2)}) collective-permute-start(bf16[512,512]{1,0:T(8,128)(2,1)} %refs_0_.1), channel_id=1, source_target_pairs={{0,6},{1,7},{2,0},{3,1},{4,2},{5,3},{6,4},{7,5},{8,14},{9,15},{10,... | collective-permute-start | bytes 1572872 | tf_op jit(solution)/shard_map/ppermute | solution.py:150
  3.1 3.0 %collective-permute-start.1 = (bf16[512,512]{1,0:T(8,128)(2,1)}, bf16[512,512]{1,0:T(8,128)(2,1)S(1)}, u32[]{:S(2)}, u32[]{:S(2)}) collective-permute-start(bf16[512,512]{1,0:T(8,128)(2,1)} %refs_0_.1), channel_id=1, source_target_pairs={{0,1},{1,0},{2,3},{3,2},{4,5},{5,4},{6,7},{7,6},{8,9},{9,8},{10,11... | collective-permute-start | bytes 1572872 | tf_op jit(solution)/shard_map/ppermute | solution.py:155
  6.1 1.2 copy-done.5
  7.4 1.0 transposed.1
  8.3 6.3 %collective-permute-done.refs_2_ = bf16[512,512]{1,0:T(8,128)(2,1)S(1)} collective-permute-done((bf16[512,512]{1,0:T(8,128)(2,1)}, bf16[512,512]{1,0:T(8,128)(2,1)S(1)}, u32[]{:S(2)}, u32[]{:S(2)}) %collective-permute-start) | collective-permute-done | bytes 524320 | tf_op jit(solution)/shard_map/ppermute | solution.py:150
  14.6 3.6 %collective-permute-done.1.refs_3_ = bf16[512,512]{1,0:T(8,128)(2,1)S(1)} collective-permute-done((bf16[512,512]{1,0:T(8,128)(2,1)}, bf16[512,512]{1,0:T(8,128)(2,1)S(1)}, u32[]{:S(2)}, u32[]{:S(2)}) %collective-permute-start.1) | collective-permute-done | bytes 524320 | tf_op jit(solution)/shard_map/ppermute | solution.py:155
  18.2 2.5 %collective-permute-done.2.refs_1_ = bf16[512,512]{1,0:T(8,128)(2,1)S(1)} collective-permute-done((bf16[512,512]{1,0:T(8,128)(2,1)}, bf16[512,512]{1,0:T(8,128)(2,1)S(1)}, u32[]{:S(2)}, u32[]{:S(2)}) %collective-permute-start.2) | collective-permute-done | bytes 524320 | tf_op jit(solution)/shard_map/ppermute | solution.py:150
  20.7 1.3 collective-permute-start.4
  22.0 1.3 collective-permute-start.5
  23.3 6.3 %all-to-all-start.1 = ((bf16[16,32,512]{2,1,0:T(8,128)(2,1)}), bf16[16,32,512]{2,1,0:T(8,128)(2,1)}, u32[]{:S(2)}, u32[]{:S(2)}) async-start(bf16[16,32,512]{2,1,0:T(8,128)(2,1)} %bitcast.3), calls=%async_computation.1 | async-start | bytes 1048576 | tf_op jit(solution)/shard_map/all_to_all | solution.py:358
  29.6 4.6 %copy-done = bf16[4096,3,512]{2,0,1:T(8,128)(2,1)S(1)} copy-done((bf16[4096,3,512]{2,0,1:T(8,128)(2,1)S(1)}, bf16[4096,3,512]{2,0,1:T(8,128)(2,1)}, u32[]{:S(2)}) %copy-start) | copy-done | bytes 12582936
  34.2 1.0 copy-done.6
  35.2 3.4 %project_round.2.refs_0_ = f32[3,512,512]{2,1,0:T(8,128)S(1)} custom-call(bf16[512,512]{1,0:T(8,128)(2,1)S(1)} %copy-done.6, bf16[512,512]{1,0:T(8,128)(2,1)S(1)} %collective-permute-done.2.refs_1_, bf16[512,512]{1,0:T(8,128)(2,1)S(1)} %collective-permute-done.refs_2_, bf16[512,512]{1,0:T(8,128)(2,1)S(1)} %collective-permute-done.1.refs_3_, ...), custom_call_target="tpu_custom_call" | custom-call | flops 3221225472 | bytes 6291456 | tf_op jit(solution)/shard_map/project_round/pallas_call | solution.py:220
  38.7 1.3 collective-permute-start.7
  40.0 0.9 collective-permute-start.6
  40.9 2.6 %project_round.3 = (f32[3,512,512]{2,1,0:T(8,128)S(1)}, f32[3,16,512]{2,1,0:T(8,128)S(1)}) custom-call(f32[3,512,512]{2,1,0:T(8,128)S(1)} %project_round.2.refs_0_, bf16[512,512]{1,0:T(8,128)(2,1)S(1)} %collective-permute-done.5.refs_1_, bf16[512,512]{1,0:T(8,128)(2,1)S(1)} %collective-permute-done.4.refs_2_, ...), custom_call_target="tpu_custom_call" | custom-call | flops 2415919104 | bytes 4718592 | tf_op jit(solution)/shard_map/project_round/pallas_call | solution.py:220
  43.5 1.7 %collective-permute-start.9 = (f32[3,16,512]{2,1,0:T(8,128)S(1)}, f32[3,16,512]{2,1,0:T(8,128)S(1)}, u32[]{:S(2)}, u32[]{:S(2)}) collective-permute-start(f32[3,16,512]{2,1,0:T(8,128)S(1)} %get-tuple-element.43), channel_id=1, source_target_pairs={{0,8},{8,16},{16,24},{24,32},{32,40},{40,48},{48,56},{56,64},{64,7... | collective-permute-start | bytes 294920 | tf_op jit(solution)/shard_map/ppermute | solution.py:145
  45.2 6.1 %collective-permute-start.8 = (bf16[16,512]{1,0:T(8,128)(2,1)S(1)}, bf16[16,512]{1,0:T(8,128)(2,1)S(1)}, u32[]{:S(2)}, u32[]{:S(2)}) collective-permute-start(bf16[16,512]{1,0:T(8,128)(2,1)S(1)} %slice.17), channel_id=1, source_target_pairs={{0,14},{1,15},{2,8},{3,9},{4,10},{5,11},{6,12},{7,13},{8,22},{9,23... | collective-permute-start | bytes 49160 | tf_op jit(solution)/shard_map/ppermute | solution.py:161
  51.3 1.4 %collective-permute-done.8.halo = bf16[16,512]{1,0:T(8,128)(2,1)S(1)} collective-permute-done((bf16[16,512]{1,0:T(8,128)(2,1)S(1)}, bf16[16,512]{1,0:T(8,128)(2,1)S(1)}, u32[]{:S(2)}, u32[]{:S(2)}) %collective-permute-start.8) | collective-permute-done | bytes 16416 | tf_op jit(solution)/shard_map/ppermute | solution.py:161
  52.8 3.2 %signal_of.1 = (bf16[512,512]{1,0:T(8,128)(2,1)}, f32[512,512]{1,0:T(8,128)}, f32[512,512]{1,0:T(8,128)}) custom-call(f32[3,512,512]{2,1,0:T(8,128)S(1)} %get-tuple-element.42.acc, bf16[256,512]{1,0:T(8,128)(2,1)S(1)} %collective-permute-done.6.lo, bf16[256,512]{1,0:T(8,128)(2,1)S(1)} %collective-permute-done.7.hi, ...), custom_call_target="tpu_custom_call" | custom-call | flops 805306368 | bytes 4194304 | tf_op jit(solution)/shard_map/signal_of/pallas_call | solution.py:263
  56.1 5.0 %all-to-all-start = ((bf16[16,32,512]{2,1,0:T(8,128)(2,1)}), bf16[16,32,512]{2,1,0:T(8,128)(2,1)S(1)}, u32[]{:S(2)}, u32[]{:S(2)}) async-start(bf16[16,32,512]{2,1,0:T(8,128)(2,1)} %bitcast.15), calls=%async_computation | async-start | bytes 1048576 | tf_op jit(solution)/shard_map/all_to_all | solution.py:368
  61.1 3.7 %filter_spectrum.1.h_ref = bf16[4,576,256]{2,1,0:T(8,128)(2,1)} custom-call(bf16[512,512]{1,0:T(8,128)(2,1)} %bitcast.4.x_ref, bf16[144,64]{1,0:T(8,128)(2,1)S(1)} %copy-done.12, f32[2,72,128]{2,1,0:T(8,128)S(1)} %copy-done.11, bf16[256,256]{1,0:T(8,128)(2,1)S(1)} %copy-done.9), custom_call_target="tpu_custom_call" | custom-call | flops 4000000000 | bytes 4000000 | tf_op jit(solution)/shard_map/filter_spectrum/pallas_call | solution.py:111
  64.8 7.1 %all-to-all-done = bf16[16,32,512]{2,1,0:T(8,128)(2,1)S(1)} async-done(((bf16[16,32,512]{2,1,0:T(8,128)(2,1)}), bf16[16,32,512]{2,1,0:T(8,128)(2,1)S(1)}, u32[]{:S(2)}, u32[]{:S(2)}) %all-to-all-start) | async-done | bytes 524320 | tf_op jit(solution)/shard_map/all_to_all | solution.py:368
  71.9 4.7 %convolve.1 = bf16[512,512]{1,0:T(8,128)(2,1)S(1)} custom-call(bf16[512,512]{1,0:T(8,128)(2,1)S(1)} %bitcast.12, bf16[4,576,256]{2,1,0:T(8,128)(2,1)} %filter_spectrum.1.h_ref, bf16[144,64]{1,0:T(8,128)(2,1)S(1)} %copy-done.12, f32[2,72,128]{2,1,0:T(8,128)S(1)} %copy-done.11, bf16[256,256]{1,0:T(8,128)(2,1)S(1)} %copy-done.9, ...), custom_call_target="tpu_custom_call" | custom-call | flops 5000000000 | bytes 4000000 | tf_op jit(solution)/shard_map/convolve/pallas_call | solution.py:130
  76.6 13.5 %all_to_all.33 = bf16[16,32,512]{2,1,0:T(8,128)(2,1)S(1)} all-to-all(bf16[16,32,512]{2,1,0:T(8,128)(2,1)S(1)} %bitcast.13), channel_id=1, replica_groups=mesh['seq'=16,'chan'=8] {'seq'}, dimensions={0} | all-to-all | bytes 1048576 | tf_op jit(solution)/shard_map/all_to_all | solution.py:369
  90.2 1.4 %gate_and_project.1 = (bf16[512,512]{1,0:T(8,128)(2,1)S(1)}, bf16[256,512]{1,0:T(8,128)(2,1)S(1)}, bf16[256,512]{1,0:T(8,128)(2,1)S(1)}, bf16[256,512]{1,0:T(8,128)(2,1)S(1)}, bf16[256,512]{1,0:T(8,128)(2,1)S(1)}) custom-call(bf16[512,512]{1,0:T(8,128)(2,1)S(1)} %bitcast.11, f32[512,512]{1,0:T(8,128)S(1)} %copy-done.3, f32[512,512]{1,0:T(8,128)S(1)} %copy-done.4, ...), custom_call_target="tpu_custom_call" | custom-call | flops 536870912 | bytes 3145728 | tf_op jit(solution)/shard_map/gate_and_project/pallas_call | solution.py:303
  91.6 0.1 collective-permute-start.10
  91.6 3.2 %collective-permute-start.11 = (bf16[256,512]{1,0:T(8,128)(2,1)S(1)}, bf16[256,512]{1,0:T(8,128)(2,1)S(1)}, u32[]{:S(2)}, u32[]{:S(2)}) collective-permute-start(bf16[256,512]{1,0:T(8,128)(2,1)S(1)} %get-tuple-element.52), channel_id=1, source_target_pairs={{0,6},{1,7},{2,0},{3,1},{4,2},{5,3},{6,4},{7,5},{8,14},{9,15},{10,... | collective-permute-start | bytes 786440 | tf_op jit(solution)/shard_map/ppermute | solution.py:150
  94.9 2.7 %collective-permute-start.12 = (bf16[256,512]{1,0:T(8,128)(2,1)S(1)}, bf16[256,512]{1,0:T(8,128)(2,1)S(1)}, u32[]{:S(2)}, u32[]{:S(2)}) collective-permute-start(bf16[256,512]{1,0:T(8,128)(2,1)S(1)} %get-tuple-element.54), channel_id=1, source_target_pairs={{0,1},{1,0},{2,3},{3,2},{4,5},{5,4},{6,7},{7,6},{8,9},{9,8},{10,11... | collective-permute-start | bytes 786440 | tf_op jit(solution)/shard_map/ppermute | solution.py:155
  97.6 1.1 project_out.3
  98.7 1.7 %collective-permute-done.10 = bf16[256,512]{1,0:T(8,128)(2,1)S(1)} collective-permute-done((bf16[256,512]{1,0:T(8,128)(2,1)S(1)}, bf16[256,512]{1,0:T(8,128)(2,1)S(1)}, u32[]{:S(2)}, u32[]{:S(2)}) %collective-permute-start.10) | collective-permute-done | bytes 262176 | tf_op jit(solution)/shard_map/ppermute | solution.py:150
  100.4 3.2 %collective-permute-done.12 = bf16[256,512]{1,0:T(8,128)(2,1)S(1)} collective-permute-done((bf16[256,512]{1,0:T(8,128)(2,1)S(1)}, bf16[256,512]{1,0:T(8,128)(2,1)S(1)}, u32[]{:S(2)}, u32[]{:S(2)}) %collective-permute-start.12) | collective-permute-done | bytes 262176 | tf_op jit(solution)/shard_map/ppermute | solution.py:155
  103.6 0.1 add_convert_fusion.4
  103.8 1.6 %collective-permute-start.13 = (bf16[512,512]{1,0:T(8,128)(2,1)S(1)}, bf16[512,512]{1,0:T(8,128)(2,1)S(1)}, u32[]{:S(2)}, u32[]{:S(2)}) collective-permute-start(bf16[512,512]{1,0:T(8,128)(2,1)S(1)} %pad_maximum_fusion), channel_id=1, source_target_pairs={{0,6},{1,7},{2,0},{3,1},{4,2},{5,3},{6,4},{7,5},{8,14},{9,15},{10,... | collective-permute-start | bytes 1572872 | tf_op jit(solution)/shard_map/ppermute | solution.py:150
  105.3 0.5 collective-permute-start.16
  105.8 2.1 %project_out.2 = (bf16[512,512]{1,0:T(8,128)(2,1)S(1)}, bf16[512,512]{1,0:T(8,128)(2,1)S(1)}, bf16[512,512]{1,0:T(8,128)(2,1)S(1)}, bf16[512,512]{1,0:T(8,128)(2,1)S(1)}) custom-call(bf16[512,512]{1,0:T(8,128)(2,1)S(1)} %get-tuple-element.48.g, bf16[512,4096]{1,0:T(8,128)(2,1)S(1)} %copy-done.2), custom_call_target="tpu_custom_call" | custom-call | flops 1073741824 | bytes 4194304 | tf_op jit(solution)/shard_map/project_out/pallas_call | solution.py:331
  108.0 0.1 add_convert_fusion.3
  108.0 2.8 %collective-permute-start.17 = (bf16[256,512]{1,0:T(8,128)(2,1)S(1)}, bf16[256,512]{1,0:T(8,128)(2,1)S(1)}, u32[]{:S(2)}, u32[]{:S(2)}) collective-permute-start(bf16[256,512]{1,0:T(8,128)(2,1)S(1)} %add_convert_fusion.3), channel_id=1, source_target_pairs={{0,1},{1,0},{2,3},{3,2},{4,5},{5,4},{6,7},{7,6},{8,9},{9,8},{10,11... | collective-permute-start | bytes 786440 | tf_op jit(solution)/shard_map/ppermute | solution.py:155
  110.9 4.9 %collective-permute-done.13 = bf16[512,512]{1,0:T(8,128)(2,1)S(1)} collective-permute-done((bf16[512,512]{1,0:T(8,128)(2,1)S(1)}, bf16[512,512]{1,0:T(8,128)(2,1)S(1)}, u32[]{:S(2)}, u32[]{:S(2)}) %collective-permute-start.13) | collective-permute-done | bytes 524320 | tf_op jit(solution)/shard_map/ppermute | solution.py:150
  115.8 0.1 add_convert_fusion.2
  115.9 2.8 %collective-permute-start.15 = (bf16[512,512]{1,0:T(8,128)(2,1)S(1)}, bf16[512,512]{1,0:T(8,128)(2,1)S(1)}, u32[]{:S(2)}, u32[]{:S(2)}) collective-permute-start(bf16[512,512]{1,0:T(8,128)(2,1)S(1)} %add_convert_fusion.2), channel_id=1, source_target_pairs={{0,1},{1,0},{2,3},{3,2},{4,5},{5,4},{6,7},{7,6},{8,9},{9,8},{10,11... | collective-permute-start | bytes 1572872 | tf_op jit(solution)/shard_map/ppermute | solution.py:155
  118.7 2.4 %collective-permute-start.14 = (bf16[512,512]{1,0:T(8,128)(2,1)S(1)}, bf16[512,512]{1,0:T(8,128)(2,1)S(1)}, u32[]{:S(2)}, u32[]{:S(2)}) collective-permute-start(bf16[512,512]{1,0:T(8,128)(2,1)S(1)} %get-tuple-element.57), channel_id=1, source_target_pairs={{0,6},{1,7},{2,0},{3,1},{4,2},{5,3},{6,4},{7,5},{8,14},{9,15},{10,... | collective-permute-start | bytes 1572872 | tf_op jit(solution)/shard_map/ppermute | solution.py:150
  121.2 0.2 add_convert_fusion.1
  121.4 0.1 collective-permute-start.18
  121.4 7.1 %collective-permute-done.15 = bf16[512,512]{1,0:T(8,128)(2,1)S(1)} collective-permute-done((bf16[512,512]{1,0:T(8,128)(2,1)S(1)}, bf16[512,512]{1,0:T(8,128)(2,1)S(1)}, u32[]{:S(2)}, u32[]{:S(2)}) %collective-permute-start.15) | collective-permute-done | bytes 524320 | tf_op jit(solution)/shard_map/ppermute | solution.py:155
  128.5 0.9 collective-permute-done.14
  129.5 3.4 %collective-permute-done.18 = bf16[512,512]{1,0:T(8,128)(2,1)S(1)} collective-permute-done((bf16[512,512]{1,0:T(8,128)(2,1)S(1)}, bf16[512,512]{1,0:T(8,128)(2,1)S(1)}, u32[]{:S(2)}, u32[]{:S(2)}) %collective-permute-start.18) | collective-permute-done | bytes 524320 | tf_op jit(solution)/shard_map/ppermute | solution.py:150
  132.9 1.1 add_convert_fusion
  (42 shorter events, 0.2 us)
Async XLA Ops:
  0.0 14.6 %collective-permute-start = (bf16[512,512]{1,0:T(8,128)(2,1)}, bf16[512,512]{1,0:T(8,128)(2,1)S(1)}, u32[]{:S(2)}, u32[]{:S(2)}) collective-permute-start(bf16[512,512]{1,0:T(8,128)(2,1)} %refs_0_.1), channel_id=1, source_target_pairs={{0,6},{1,7},{2,0},{3,1},{4,2},{5,3},{6,4},{7,5},{8,14},{9,15},{10,... | collective-permute-start | bytes 1572872 | tf_op jit(solution)/shard_map/ppermute | solution.py:150
  3.1 15.1 %collective-permute-start.1 = (bf16[512,512]{1,0:T(8,128)(2,1)}, bf16[512,512]{1,0:T(8,128)(2,1)S(1)}, u32[]{:S(2)}, u32[]{:S(2)}) collective-permute-start(bf16[512,512]{1,0:T(8,128)(2,1)} %refs_0_.1), channel_id=1, source_target_pairs={{0,1},{1,0},{2,3},{3,2},{4,5},{5,4},{6,7},{7,6},{8,9},{9,8},{10,11... | collective-permute-start | bytes 1572872 | tf_op jit(solution)/shard_map/ppermute | solution.py:155
  6.1 14.5 %collective-permute-start.2 = (bf16[512,512]{1,0:T(8,128)(2,1)}, bf16[512,512]{1,0:T(8,128)(2,1)S(1)}, u32[]{:S(2)}, u32[]{:S(2)}) collective-permute-start(bf16[512,512]{1,0:T(8,128)(2,1)} %refs_0_.1), channel_id=1, source_target_pairs={{0,2},{1,3},{2,4},{3,5},{4,6},{5,7},{6,0},{7,1},{8,10},{9,11},{10,... | collective-permute-start | bytes 1572872 | tf_op jit(solution)/shard_map/ppermute | solution.py:150
  6.1 1.2 copy-start.5
  20.6 18.0 %collective-permute-start.3 = (bf16[512,512]{1,0:T(8,128)(2,1)S(1)}, bf16[512,512]{1,0:T(8,128)(2,1)S(1)}, u32[]{:S(2)}, u32[]{:S(2)}) collective-permute-start(bf16[512,512]{1,0:T(8,128)(2,1)S(1)} %collective-permute-done.refs_2_), channel_id=1, source_target_pairs={{0,6},{1,7},{2,0},{3,1},{4,2},{5,3},{6,4},{7,5},{8,14},{9,15},{10,... | collective-permute-start | bytes 1572872 | tf_op jit(solution)/shard_map/ppermute | solution.py:150
  20.7 18.0 %collective-permute-start.4 = (bf16[512,512]{1,0:T(8,128)(2,1)S(1)}, bf16[512,512]{1,0:T(8,128)(2,1)S(1)}, u32[]{:S(2)}, u32[]{:S(2)}) collective-permute-start(bf16[512,512]{1,0:T(8,128)(2,1)S(1)} %collective-permute-done.refs_2_), channel_id=1, source_target_pairs={{0,1},{1,0},{2,3},{3,2},{4,5},{5,4},{6,7},{7,6},{8,9},{9,8},{10,11... | collective-permute-start | bytes 1572872 | tf_op jit(solution)/shard_map/ppermute | solution.py:155
  22.0 16.7 %collective-permute-start.5 = (bf16[512,512]{1,0:T(8,128)(2,1)S(1)}, bf16[512,512]{1,0:T(8,128)(2,1)S(1)}, u32[]{:S(2)}, u32[]{:S(2)}) collective-permute-start(bf16[512,512]{1,0:T(8,128)(2,1)S(1)} %collective-permute-done.1.refs_3_), channel_id=1, source_target_pairs={{0,2},{1,3},{2,4},{3,5},{4,6},{5,7},{6,0},{7,1},{8,10},{9,11},{10,... | collective-permute-start | bytes 1572872 | tf_op jit(solution)/shard_map/ppermute | solution.py:150
  23.3 32.8 %all-to-all-start.1 = ((bf16[16,32,512]{2,1,0:T(8,128)(2,1)}), bf16[16,32,512]{2,1,0:T(8,128)(2,1)}, u32[]{:S(2)}, u32[]{:S(2)}) async-start(bf16[16,32,512]{2,1,0:T(8,128)(2,1)} %bitcast.3), calls=%async_computation.1 | async-start | bytes 1048576 | tf_op jit(solution)/shard_map/all_to_all | solution.py:358
  29.6 4.6 %copy-start = (bf16[4096,3,512]{2,0,1:T(8,128)(2,1)S(1)}, bf16[4096,3,512]{2,0,1:T(8,128)(2,1)}, u32[]{:S(2)}) copy-start(bf16[4096,3,512]{2,0,1:T(8,128)(2,1)} %param.12) | copy-start | bytes 37748740
  34.2 1.0 copy-start.6
  35.2 5.7 %copy-start.1 = (bf16[4096,3,512]{2,0,1:T(8,128)(2,1)S(1)}, bf16[4096,3,512]{2,0,1:T(8,128)(2,1)}, u32[]{:S(2)}) copy-start(bf16[4096,3,512]{2,0,1:T(8,128)(2,1)} %param.12) | copy-start | bytes 37748740
  38.7 14.1 %collective-permute-start.7 = (bf16[256,512]{1,0:T(8,128)(2,1)S(1)}, bf16[256,512]{1,0:T(8,128)(2,1)S(1)}, u32[]{:S(2)}, u32[]{:S(2)}) collective-permute-start(bf16[256,512]{1,0:T(8,128)(2,1)S(1)} %slice.16), channel_id=1, source_target_pairs={{0,6},{1,7},{2,0},{3,1},{4,2},{5,3},{6,4},{7,5},{8,14},{9,15},{10,... | collective-permute-start | bytes 786440 | tf_op jit(solution)/shard_map/ppermute | solution.py:150
  40.0 12.8 %copy-start.7 = (f32[3,3,512]{2,1,0:T(4,128)S(1)}, f32[3,3,512]{2,1,0:T(4,128)}, u32[]{:S(2)}) copy-start(f32[3,3,512]{2,1,0:T(4,128)} %taps.1) | copy-start | bytes 55300
  40.0 12.8 %collective-permute-start.6 = (bf16[256,512]{1,0:T(8,128)(2,1)S(1)}, bf16[256,512]{1,0:T(8,128)(2,1)S(1)}, u32[]{:S(2)}, u32[]{:S(2)}) collective-permute-start(bf16[256,512]{1,0:T(8,128)(2,1)S(1)} %slice.15), channel_id=1, source_target_pairs={{0,2},{1,3},{2,4},{3,5},{4,6},{5,7},{6,0},{7,1},{8,10},{9,11},{10,... | collective-permute-start | bytes 786440 | tf_op jit(solution)/shard_map/ppermute | solution.py:150
  43.5 9.3 %collective-permute-start.9 = (f32[3,16,512]{2,1,0:T(8,128)S(1)}, f32[3,16,512]{2,1,0:T(8,128)S(1)}, u32[]{:S(2)}, u32[]{:S(2)}) collective-permute-start(f32[3,16,512]{2,1,0:T(8,128)S(1)} %get-tuple-element.43), channel_id=1, source_target_pairs={{0,8},{8,16},{16,24},{24,32},{32,40},{40,48},{48,56},{56,64},{64,7... | collective-permute-start | bytes 294920 | tf_op jit(solution)/shard_map/ppermute | solution.py:145
  45.2 7.6 %collective-permute-start.8 = (bf16[16,512]{1,0:T(8,128)(2,1)S(1)}, bf16[16,512]{1,0:T(8,128)(2,1)S(1)}, u32[]{:S(2)}, u32[]{:S(2)}) collective-permute-start(bf16[16,512]{1,0:T(8,128)(2,1)S(1)} %slice.17), channel_id=1, source_target_pairs={{0,14},{1,15},{2,8},{3,9},{4,10},{5,11},{6,12},{7,13},{8,22},{9,23... | collective-permute-start | bytes 49160 | tf_op jit(solution)/shard_map/ppermute | solution.py:161
  52.8 8.3 %copy-start.9 = (bf16[256,256]{1,0:T(8,128)(2,1)S(1)}, bf16[256,256]{1,0:T(8,128)(2,1)}, u32[]{:S(2)}) copy-start(bf16[256,256]{1,0:T(8,128)(2,1)} %constant.12.clone.forward) | copy-start | bytes 393220
  52.8 8.3 %copy-start.11 = (f32[2,72,128]{2,1,0:T(8,128)S(1)}, f32[2,72,128]{2,1,0:T(8,128)}, u32[]{:S(2)}) copy-start(f32[2,72,128]{2,1,0:T(8,128)} %constant.11.clone.tw) | copy-start | bytes 221188
  52.8 8.3 %copy-start.12 = (bf16[144,64]{1,0:T(8,128)(2,1)S(1)}, bf16[144,64]{1,0:T(8,128)(2,1)}, u32[]{:S(2)}) copy-start(bf16[144,64]{1,0:T(8,128)(2,1)} %constant.10.clone.first) | copy-start | bytes 55300
  56.1 15.8 %all-to-all-start = ((bf16[16,32,512]{2,1,0:T(8,128)(2,1)}), bf16[16,32,512]{2,1,0:T(8,128)(2,1)S(1)}, u32[]{:S(2)}, u32[]{:S(2)}) async-start(bf16[16,32,512]{2,1,0:T(8,128)(2,1)} %bitcast.15), calls=%async_computation | async-start | bytes 1048576 | tf_op jit(solution)/shard_map/all_to_all | solution.py:368
  61.1 10.8 %copy-start.10 = (bf16[256,256]{1,0:T(8,128)(2,1)S(1)}, bf16[256,256]{1,0:T(8,128)(2,1)}, u32[]{:S(2)}) copy-start(bf16[256,256]{1,0:T(8,128)(2,1)} %constant.13.clone.backward) | copy-start | bytes 393220
  61.1 10.8 %copy-start.13 = (bf16[64,144]{1,0:T(8,128)(2,1)S(1)}, bf16[64,144]{1,0:T(8,128)(2,1)}, u32[]{:S(2)}) copy-start(bf16[64,144]{1,0:T(8,128)(2,1)} %constant.14.clone.last) | copy-start | bytes 55300
  71.9 18.2 %copy-start.2 = (bf16[512,4096]{1,0:T(8,128)(2,1)S(1)}, bf16[512,4096]{1,0:T(8,128)(2,1)}, u32[]{:S(2)}) copy-start(bf16[512,4096]{1,0:T(8,128)(2,1)} %weight.5) | copy-start | bytes 12582916
  71.9 18.2 %copy-start.3 = (f32[512,512]{1,0:T(8,128)S(1)}, f32[512,512]{1,0:T(8,128)}, u32[]{:S(2)}) copy-start(f32[512,512]{1,0:T(8,128)} %get-tuple-element.46.signal) | copy-start | bytes 3145732
  71.9 18.2 %copy-start.4 = (f32[512,512]{1,0:T(8,128)S(1)}, f32[512,512]{1,0:T(8,128)}, u32[]{:S(2)}) copy-start(f32[512,512]{1,0:T(8,128)} %get-tuple-element.47.gate_out) | copy-start | bytes 3145732
  71.9 18.2 %copy-start.8 = (f32[512]{0:T(512)S(1)}, f32[512]{0:T(512)}, u32[]{:S(2)}) copy-start(f32[512]{0:T(512)} %param.15) | copy-start | bytes 6148
  91.6 8.9 %collective-permute-start.10 = (bf16[256,512]{1,0:T(8,128)(2,1)S(1)}, bf16[256,512]{1,0:T(8,128)(2,1)S(1)}, u32[]{:S(2)}, u32[]{:S(2)}) collective-permute-start(bf16[256,512]{1,0:T(8,128)(2,1)S(1)} %get-tuple-element.51), channel_id=1, source_target_pairs={{0,2},{1,3},{2,4},{3,5},{4,6},{5,7},{6,0},{7,1},{8,10},{9,11},{10,... | collective-permute-start | bytes 786440 | tf_op jit(solution)/shard_map/ppermute | solution.py:150
  91.6 8.8 %collective-permute-start.11 = (bf16[256,512]{1,0:T(8,128)(2,1)S(1)}, bf16[256,512]{1,0:T(8,128)(2,1)S(1)}, u32[]{:S(2)}, u32[]{:S(2)}) collective-permute-start(bf16[256,512]{1,0:T(8,128)(2,1)S(1)} %get-tuple-element.52), channel_id=1, source_target_pairs={{0,6},{1,7},{2,0},{3,1},{4,2},{5,3},{6,4},{7,5},{8,14},{9,15},{10,... | collective-permute-start | bytes 786440 | tf_op jit(solution)/shard_map/ppermute | solution.py:150
  94.9 8.8 %collective-permute-start.12 = (bf16[256,512]{1,0:T(8,128)(2,1)S(1)}, bf16[256,512]{1,0:T(8,128)(2,1)S(1)}, u32[]{:S(2)}, u32[]{:S(2)}) collective-permute-start(bf16[256,512]{1,0:T(8,128)(2,1)S(1)} %get-tuple-element.54), channel_id=1, source_target_pairs={{0,1},{1,0},{2,3},{3,2},{4,5},{5,4},{6,7},{7,6},{8,9},{9,8},{10,11... | collective-permute-start | bytes 786440 | tf_op jit(solution)/shard_map/ppermute | solution.py:155
  103.8 12.0 %collective-permute-start.13 = (bf16[512,512]{1,0:T(8,128)(2,1)S(1)}, bf16[512,512]{1,0:T(8,128)(2,1)S(1)}, u32[]{:S(2)}, u32[]{:S(2)}) collective-permute-start(bf16[512,512]{1,0:T(8,128)(2,1)S(1)} %pad_maximum_fusion), channel_id=1, source_target_pairs={{0,6},{1,7},{2,0},{3,1},{4,2},{5,3},{6,4},{7,5},{8,14},{9,15},{10,... | collective-permute-start | bytes 1572872 | tf_op jit(solution)/shard_map/ppermute | solution.py:150
  105.3 15.9 %collective-permute-start.16 = (bf16[512,512]{1,0:T(8,128)(2,1)S(1)}, bf16[512,512]{1,0:T(8,128)(2,1)S(1)}, u32[]{:S(2)}, u32[]{:S(2)}) collective-permute-start(bf16[512,512]{1,0:T(8,128)(2,1)S(1)} %get-tuple-element.61), channel_id=1, source_target_pairs={{0,2},{1,3},{2,4},{3,5},{4,6},{5,7},{6,0},{7,1},{8,10},{9,11},{10,... | collective-permute-start | bytes 1572872 | tf_op jit(solution)/shard_map/ppermute | solution.py:150
  108.0 13.1 %collective-permute-start.17 = (bf16[256,512]{1,0:T(8,128)(2,1)S(1)}, bf16[256,512]{1,0:T(8,128)(2,1)S(1)}, u32[]{:S(2)}, u32[]{:S(2)}) collective-permute-start(bf16[256,512]{1,0:T(8,128)(2,1)S(1)} %add_convert_fusion.3), channel_id=1, source_target_pairs={{0,1},{1,0},{2,3},{3,2},{4,5},{5,4},{6,7},{7,6},{8,9},{9,8},{10,11... | collective-permute-start | bytes 786440 | tf_op jit(solution)/shard_map/ppermute | solution.py:155
  115.9 12.6 %collective-permute-start.15 = (bf16[512,512]{1,0:T(8,128)(2,1)S(1)}, bf16[512,512]{1,0:T(8,128)(2,1)S(1)}, u32[]{:S(2)}, u32[]{:S(2)}) collective-permute-start(bf16[512,512]{1,0:T(8,128)(2,1)S(1)} %add_convert_fusion.2), channel_id=1, source_target_pairs={{0,1},{1,0},{2,3},{3,2},{4,5},{5,4},{6,7},{7,6},{8,9},{9,8},{10,11... | collective-permute-start | bytes 1572872 | tf_op jit(solution)/shard_map/ppermute | solution.py:155
  118.7 10.8 %collective-permute-start.14 = (bf16[512,512]{1,0:T(8,128)(2,1)S(1)}, bf16[512,512]{1,0:T(8,128)(2,1)S(1)}, u32[]{:S(2)}, u32[]{:S(2)}) collective-permute-start(bf16[512,512]{1,0:T(8,128)(2,1)S(1)} %get-tuple-element.57), channel_id=1, source_target_pairs={{0,6},{1,7},{2,0},{3,1},{4,2},{5,3},{6,4},{7,5},{8,14},{9,15},{10,... | collective-permute-start | bytes 1572872 | tf_op jit(solution)/shard_map/ppermute | solution.py:150
  121.4 11.5 %collective-permute-start.18 = (bf16[512,512]{1,0:T(8,128)(2,1)S(1)}, bf16[512,512]{1,0:T(8,128)(2,1)S(1)}, u32[]{:S(2)}, u32[]{:S(2)}) collective-permute-start(bf16[512,512]{1,0:T(8,128)(2,1)S(1)} %add_convert_fusion.1), channel_id=1, source_target_pairs={{0,2},{1,3},{2,4},{3,5},{4,6},{5,7},{6,0},{7,1},{8,10},{9,11},{10,... | collective-permute-start | bytes 1572872 | tf_op jit(solution)/shard_map/ppermute | solution.py:150

commit v4 on v3

--- a/solution.py
+++ b/solution.py
@@ -10,7 +10,7 @@
 from jax.sharding import PartitionSpec as P
 
 K1 = 72
-GROUP = 8
+GROUP = 16
 
 
 def fourier_tables(seqs, rows):
@@ -155,9 +155,9 @@
     return lax.ppermute(array, "chan", [(i, i ^ 1) for i in range(count)])
 
 
-def following(array):
+def following_far(array):
     seqs, count = lax.axis_size("seq"), lax.axis_size("chan")
-    pairs = [(s * count + c, (s + 1) * count + (c - 2) % count) for s in range(seqs - 1) for c in range(count)]
+    pairs = [(s * count + c, (s + 1) * count + (((c + 4) % count) ^ 1)) for s in range(seqs - 1) for c in range(count)]
     return lax.ppermute(array, ("seq", "chan"), pairs)
 
 
@@ -225,6 +225,43 @@
         compiler_params=params(10), name="project_round",
         cost_estimate=pl.CostEstimate(flops=2 * count * rows * depth * branches * width, bytes_accessed=2 * count * depth * branches * width, transcendentals=0),
     )(*args, in_vmem(weight))
+
+
+def fetch_rows(weight, j, at, held, sem):
+    depth = held.shape[0]
+    start = pl.multiple_of(at * depth, depth)
+    return pltpu.make_async_copy(weight.at[j, pl.ds(start, depth)], held, sem)
+
+
+def first_kernel(places, *refs):
+    blocks, (weight, out, held, sems) = refs[:-4], refs[-4:]
+    branches = out.shape[0]
+    copies = [[fetch_rows(weight, j, owner(*p), held.at[j, k], sems.at[j, k]) for k, p in enumerate(places)] for j in range(branches)]
+    for row in copies:
+        for copy in row:
+            copy.start()
+    for j in range(branches):
+        total = None
+        for k in range(len(places)):
+            copies[j][k].wait()
+            term = jnp.dot(blocks[k][...], held[j, k], preferred_element_type=jnp.float32)
+            total = term if total is None else total + term
+        out[j] = total
+
+
+def first_round(blocks, places, weight):
+    branches, _, width = weight.shape
+    rows, depth = blocks[0].shape
+    count = len(blocks)
+    return pl.pallas_call(
+        functools.partial(first_kernel, places),
+        out_shape=jax.ShapeDtypeStruct((branches, rows, width), jnp.float32),
+        in_specs=[whole()] * count + [in_hbm()],
+        out_specs=whole(),
+        scratch_shapes=[pltpu.VMEM((branches, count, depth, width), jnp.bfloat16), pltpu.SemaphoreType.DMA((branches, count))],
+        compiler_params=params(10), name="first_round",
+        cost_estimate=pl.CostEstimate(flops=2 * count * rows * depth * branches * width, bytes_accessed=2 * count * depth * branches * width, transcendentals=0),
+    )(*blocks, from_hbm(weight))
 
 
 def signal_kernel(place, acc, lo, hi, halo, halo_acc, weight, taps, signal_t, signal, gate_out, sig_t, sig, gate, out_sems):
@@ -282,32 +319,30 @@
     return pltpu.make_async_copy(weight.at[:, pl.ds(start, cols)], held, sem)
 
 
-def gate_kernel(places, conv, signal, gate_out, skip, weight, gated, *refs):
-    outs, (held, sems) = refs[:-2], refs[-2:]
-    copies = [fetch_columns(weight, owner(*p), held.at[k], sems.at[k]) for k, p in enumerate(places)]
-    for copy in copies:
-        copy.start()
+def gate_kernel(place, conv, signal, gate_out, skip, weight, gated, *refs):
+    outs, (held, sem) = refs[:-2], refs[-2:]
+    copy = fetch_columns(weight, owner(*place), held, sem)
+    copy.start()
     total = conv[...].astype(jnp.float32).T + skip[...] * signal[...]
     g = (total * gate_out[...]).astype(jnp.bfloat16)
     gated[...] = g
-    half = outs[0].shape[0]
-    for k in range(len(places)):
-        copies[k].wait()
-        outs[2 * k][...] = jnp.dot(g[:half], held[k], preferred_element_type=jnp.float32).astype(jnp.bfloat16)
-        outs[2 * k + 1][...] = jnp.dot(g[half:], held[k], preferred_element_type=jnp.float32).astype(jnp.bfloat16)
-
-
-def gate_and_project(conv, signal, gate_out, skip, places, weight, cols):
-    width, rows = conv.shape
-    count = len(places)
-    return pl.pallas_call(
-        functools.partial(gate_kernel, places),
-        out_shape=[jax.ShapeDtypeStruct((rows, width), jnp.bfloat16)] + [jax.ShapeDtypeStruct((rows // 2, cols), jnp.bfloat16)] * (2 * count),
+    copy.wait()
+    at = 0
+    for out in outs:
+        out[...] = jnp.dot(g[at:at + out.shape[0]], held[...], preferred_element_type=jnp.float32).astype(jnp.bfloat16)
+        at += out.shape[0]
+
+
+def gate_and_project(conv, signal, gate_out, skip, place, pieces, weight, cols):
+    rows, width = signal.shape
+    return pl.pallas_call(
+        functools.partial(gate_kernel, place),
+        out_shape=[jax.ShapeDtypeStruct((rows, width), jnp.bfloat16)] + [jax.ShapeDtypeStruct((n, cols), jnp.bfloat16) for n in pieces],
         in_specs=[whole()] * 4 + [in_hbm()],
-        out_specs=[whole()] * (1 + 2 * count),
-        scratch_shapes=[pltpu.VMEM((count, width, cols), jnp.bfloat16), pltpu.SemaphoreType.DMA((count,))],
+        out_specs=[whole()] * (1 + len(pieces)),
+        scratch_shapes=[pltpu.VMEM((width, cols), jnp.bfloat16), pltpu.SemaphoreType.DMA],
         compiler_params=params(10), name="gate_and_project",
-        cost_estimate=pl.CostEstimate(flops=2 * count * rows * width * cols, bytes_accessed=12 * rows * width, transcendentals=0),
+        cost_estimate=pl.CostEstimate(flops=2 * rows * width * cols, bytes_accessed=12 * rows * width, transcendentals=0),
     )(conv, signal, gate_out, skip, weight)
 
 
@@ -339,6 +374,11 @@
     )(gated, weight)
 
 
+def thirds(rows):
+    tiles = rows // 16
+    return (tiles + 2) // 3 * 16, 2 * ((tiles + 2) // 3) * 16
+
+
 def added(*terms):
     return sum(t.astype(jnp.float32) for t in terms).astype(jnp.bfloat16)
 
@@ -353,13 +393,13 @@
     together = lax.optimization_barrier
 
     above, side, below = ring(tokens, -1), cross(tokens), ring(tokens, 1)
-    above, side, below, fil = together((above, side, below, transposed(long_filter)))
+    halo = following_far(tokens[rows - 16:])
+    above, side, below, halo, fil = together((above, side, below, halo, transposed(long_filter)))
     far, side_above, side_below = ring(above, -1), cross(above), ring(side, 1)
     fil = lax.all_to_all(fil, "seq", 0, 0, tiled=True)
-    acc, = project_round(None, [tokens, below, above, side], [(0, 0), (-1, 0), (1, 0), (0, 1)], weight)
+    acc = first_round([tokens, below, above, side], [(0, 0), (-1, 0), (1, 0), (0, 1)], weight)
     far, side_above, side_below, acc = together((far, side_above, side_below, acc))
     far_hi, far_lo = ring(side_above[half:], -1), ring(side_below[:half], 1)
-    halo = following(side_above[rows - 16:])
     acc, tail = project_round(acc, [side_below, side_above, far], [(-1, 1), (1, 1), (2, 0)], weight, 16)
     halo_acc = shifted(tail, "seq", 1)
     signal_t, signal, gate_out = signal_of(acc, far_lo, far_hi, halo, halo_acc, (2, 1), weight, short_weight)
@@ -369,17 +409,17 @@
     conv = lax.all_to_all(conv, "seq", 0, 0, tiled=True)
 
     skip = skip_gain.reshape(1, width)
-    gated, far_side_lo, far_side_hi, up_side_lo, up_side_hi = gate_and_project(conv, signal, gate_out, skip, [(2, 1), (1, 1)], out_weight, cols)
-    to_hi, to_lo, up_side_lo = ring(far_side_hi, 1), ring(far_side_lo, -1), cross(up_side_lo)
-    down_side, far = project_out(gated, [(-1, 1), (2, 0)], (1, 1), out_weight, cols)
+    one, two = thirds(rows)
+    gated, *pieces = gate_and_project(conv, signal, gate_out, skip, (2, 1), (one, two - one, rows - two), out_weight, cols)
+    to_down, to_up, to_far = ring(pieces[0], -1), ring(pieces[1], 1), cross(pieces[2])
+    up_side, down_side, far = project_out(gated, [(1, 1), (-1, 1), (2, 0)], (1, 1, 1), out_weight, cols)
     up, down, side, own = project_out(gated, [(1, 0), (-1, 0), (0, 1), (0, 0)], (1, 1, 1, 1), out_weight, cols)
-    to_hi, to_lo, far, up_side_lo = together((to_hi, to_lo, far, up_side_lo))
-    down_side = ring(jnp.concatenate([added(down_side[:half], to_lo), down_side[half:]], axis=0), -1)
-    up_side_hi = cross(added(up_side_hi, to_hi))
-    far = ring(far, 1)
+    down_side = ring(jnp.concatenate([added(down_side[:one], to_down), down_side[one:]], axis=0), -1)
+    up_side = cross(jnp.concatenate([up_side[:one], added(up_side[one:two], to_up), up_side[two:]], axis=0))
+    far = ring(jnp.concatenate([far[:two], added(far[two:], to_far)], axis=0), 1)
     down_side, down = together((down_side, down))
     side = cross(added(side, down_side))
-    up = added(up, far, jnp.concatenate([up_side_lo, up_side_hi], axis=0))
+    up = added(up, far, up_side)
     up, down = ring(up, 1), ring(down, -1)
     return added(own, down, side, up)
 

time: 135 us -> 129 us (0.956)
  local copies, waits for them, and re-layouts: 6.96 us -> 3.21 us
  starting transfers between devices: 46.2 us -> 43.3 us
  waiting for transfers between devices: 42.1 us -> 40.7 us
    pallas_call x1 -> x2, Pallas kernels: 1.39 us -> 6.53 us  [the longest x1 5.65 us: first_round(): pl.pallas_call(functools.partial(first_kernel, places), out_shape=jax.Sha...]
    ppermute x12, waiting for transfers between devices: 19.7 us -> 14.7 us  [ring(): lax.ppermute(array, 'chan', [(i, (i + 2 * by) % count) for i in range(cou...]
    ppermute x5, starting transfers between devices: 12.7 us -> 7.99 us  [cross(): return lax.ppermute(array, 'chan', [(i, i ^ 1) for i in range(count)])]
    unnamed x28 -> x26, local copies, waits for them, and re-layouts: 6.9 us -> 2.32 us
    ppermute x1, waiting for transfers between devices: 1.43 us -> 5.83 us  [following_far(): return lax.ppermute(array, ('seq', 'chan'), pairs)]
    ppermute x1, starting transfers between devices: 6.12 us -> 2.61 us  [following_far(): return lax.ppermute(array, ('seq', 'chan'), pairs)]
    pallas_call x2 -> x1, Pallas kernels: 6 us -> 2.6 us  [project_round(): pl.pallas_call(functools.partial(round_kernel, places, acc is not None, t...]
    all_to_all x1, starting transfers between devices: 4.97 us -> 8.27 us  [shards(): lax.all_to_all(signal_t, 'seq', 0, 0, tiled=True)]
  transfers between devices with their start and end apart: 21 -> 21, of which waited for: 11 -> 14; matrix products, arithmetic and copies ran while one was open for 0% -> 1% of each run, Pallas kernels for 13% -> 15%
where the time goes in v4:
time: 129 us; the launch traced here: 127 us
  starting transfers between devices  43.3 us (34%)
  waiting for transfers between devices  40.7 us (32%)
  Pallas kernels  24.2 us (19%)
  blocking collectives  13.5 us (10%)
  local copies, waits for them, and re-layouts  3.21 us (2%)
  other arithmetic  1.64 us (1%)
    ppermute x12, starting transfers between devices, ring(): lax.ppermute(array, 'chan', [(i, (i + 2 * by) % count) for i in range(cou...  16.7 us
    ppermute x12, waiting for transfers between devices, ring(): lax.ppermute(array, 'chan', [(i, (i + 2 * by) % count) for i in range(cou...  14.7 us
    all_to_all x1, blocking collectives, shards(): conv = lax.all_to_all(conv, 'seq', 0, 0, tiled=True)  13.5 us
    ppermute x5, waiting for transfers between devices, cross(): return lax.ppermute(array, 'chan', [(i, i ^ 1) for i in range(count)])  11.9 us
    all_to_all x1, starting transfers between devices, shards(): lax.all_to_all(signal_t, 'seq', 0, 0, tiled=True)  8.27 us
    ppermute x5, starting transfers between devices, cross(): return lax.ppermute(array, 'chan', [(i, i ^ 1) for i in range(count)])  7.99 us
    all_to_all x1, waiting for transfers between devices, shards(): lax.all_to_all(signal_t, 'seq', 0, 0, tiled=True)  7.38 us
    all_to_all x1, starting transfers between devices, shards(): fil = lax.all_to_all(fil, 'seq', 0, 0, tiled=True)  6.5 us
  transfers between devices with their start and end apart: 21, of which 14 were waited for; matrix products, arithmetic and copies ran while one was open for 1% of the time, Pallas kernels for 15%

profile of v4, /device:TPU:0, one launch (start us, length us, event | category | flops | bytes accessed | tf_op | source)
XLA Modules:
  0.0 127.0 jit_solution(946630635831492288)
XLA Ops:
  0.0 3.1 %collective-permute-start = (bf16[512,512]{1,0:T(8,128)(2,1)}, bf16[512,512]{1,0:T(8,128)(2,1)S(1)}, u32[]{:S(2)}, u32[]{:S(2)}) collective-permute-start(bf16[512,512]{1,0:T(8,128)(2,1)} %refs_0_.1), channel_id=1, source_target_pairs={{0,6},{1,7},{2,0},{3,1},{4,2},{5,3},{6,4},{7,5},{8,14},{9,15},{10,... | collective-permute-start | bytes 1572872 | tf_op jit(solution)/shard_map/ppermute | solution.py:150
  3.1 3.0 %collective-permute-start.1 = (bf16[512,512]{1,0:T(8,128)(2,1)}, bf16[512,512]{1,0:T(8,128)(2,1)S(1)}, u32[]{:S(2)}, u32[]{:S(2)}) collective-permute-start(bf16[512,512]{1,0:T(8,128)(2,1)} %refs_0_.1), channel_id=1, source_target_pairs={{0,1},{1,0},{2,3},{3,2},{4,5},{5,4},{6,7},{7,6},{8,9},{9,8},{10,11... | collective-permute-start | bytes 1572872 | tf_op jit(solution)/shard_map/ppermute | solution.py:155
  6.1 0.8 slice.30
  6.9 2.6 %collective-permute-start.3 = (bf16[16,512]{1,0:T(8,128)(2,1)S(1)}, bf16[16,512]{1,0:T(8,128)(2,1)S(1)}, u32[]{:S(2)}, u32[]{:S(2)}) collective-permute-start(bf16[16,512]{1,0:T(8,128)(2,1)S(1)} %slice.30), channel_id=1, source_target_pairs={{0,13},{1,12},{2,15},{3,14},{4,9},{5,8},{6,11},{7,10},{8,21},{9,20... | collective-permute-start | bytes 49160 | tf_op jit(solution)/shard_map/ppermute | solution.py:161
  9.5 1.2 copy-done.4
  10.8 1.0 transposed.1
  11.8 5.8 %collective-permute-done.3.halo = bf16[16,512]{1,0:T(8,128)(2,1)S(1)} collective-permute-done((bf16[16,512]{1,0:T(8,128)(2,1)S(1)}, bf16[16,512]{1,0:T(8,128)(2,1)S(1)}, u32[]{:S(2)}, u32[]{:S(2)}) %collective-permute-start.3) | collective-permute-done | bytes 16416 | tf_op jit(solution)/shard_map/ppermute | solution.py:161
  17.6 0.8 collective-permute-done.1.refs_3_
  18.4 2.6 %collective-permute-done.2.refs_1_ = bf16[512,512]{1,0:T(8,128)(2,1)S(1)} collective-permute-done((bf16[512,512]{1,0:T(8,128)(2,1)}, bf16[512,512]{1,0:T(8,128)(2,1)S(1)}, u32[]{:S(2)}, u32[]{:S(2)}) %collective-permute-start.2) | collective-permute-done | bytes 524320 | tf_op jit(solution)/shard_map/ppermute | solution.py:150
  21.0 1.1 collective-permute-start.5
  22.1 1.3 %collective-permute-start.6 = (bf16[512,512]{1,0:T(8,128)(2,1)S(1)}, bf16[512,512]{1,0:T(8,128)(2,1)S(1)}, u32[]{:S(2)}, u32[]{:S(2)}) collective-permute-start(bf16[512,512]{1,0:T(8,128)(2,1)S(1)} %collective-permute-done.1.refs_3_), channel_id=1, source_target_pairs={{0,2},{1,3},{2,4},{3,5},{4,6},{5,7},{6,0},{7,1},{8,10},{9,11},{10,... | collective-permute-start | bytes 1572872 | tf_op jit(solution)/shard_map/ppermute | solution.py:150
  23.4 6.5 %all-to-all-start.1 = ((bf16[16,32,512]{2,1,0:T(8,128)(2,1)}), bf16[16,32,512]{2,1,0:T(8,128)(2,1)}, u32[]{:S(2)}, u32[]{:S(2)}) async-start(bf16[16,32,512]{2,1,0:T(8,128)(2,1)} %bitcast.3), calls=%async_computation.1 | async-start | bytes 1048576 | tf_op jit(solution)/shard_map/all_to_all | solution.py:399
  29.9 1.0 copy-done.5
  31.0 5.6 %first_round.1.refs_0_ = f32[3,512,512]{2,1,0:T(8,128)S(1)} custom-call(bf16[512,512]{1,0:T(8,128)(2,1)S(1)} %copy-done.5, bf16[512,512]{1,0:T(8,128)(2,1)S(1)} %collective-permute-done.2.refs_1_, bf16[512,512]{1,0:T(8,128)(2,1)S(1)} %collective-permute-done.refs_2_, bf16[512,512]{1,0:T(8,128)(2,1)S(1)} %collective-permute-done.1.refs_3_, ...), custom_call_target="tpu_custom_call" | custom-call | flops 3221225472 | bytes 6291456 | tf_op jit(solution)/shard_map/first_round/pallas_call | solution.py:256
  36.7 0.4 collective-permute-done.6.refs_1_
  37.1 1.7 %collective-permute-start.7 = (bf16[256,512]{1,0:T(8,128)(2,1)S(1)}, bf16[256,512]{1,0:T(8,128)(2,1)S(1)}, u32[]{:S(2)}, u32[]{:S(2)}) collective-permute-start(bf16[256,512]{1,0:T(8,128)(2,1)S(1)} %slice.31), channel_id=1, source_target_pairs={{0,2},{1,3},{2,4},{3,5},{4,6},{5,7},{6,0},{7,1},{8,10},{9,11},{10,... | collective-permute-start | bytes 786440 | tf_op jit(solution)/shard_map/ppermute | solution.py:150
  38.8 1.7 %collective-permute-start.8 = (bf16[256,512]{1,0:T(8,128)(2,1)S(1)}, bf16[256,512]{1,0:T(8,128)(2,1)S(1)}, u32[]{:S(2)}, u32[]{:S(2)}) collective-permute-start(bf16[256,512]{1,0:T(8,128)(2,1)S(1)} %slice.32), channel_id=1, source_target_pairs={{0,6},{1,7},{2,0},{3,1},{4,2},{5,3},{6,4},{7,5},{8,14},{9,15},{10,... | collective-permute-start | bytes 786440 | tf_op jit(solution)/shard_map/ppermute | solution.py:150
  40.5 2.6 %project_round.1 = (f32[3,512,512]{2,1,0:T(8,128)S(1)}, f32[3,16,512]{2,1,0:T(8,128)S(1)}) custom-call(f32[3,512,512]{2,1,0:T(8,128)S(1)} %first_round.1.refs_0_, bf16[512,512]{1,0:T(8,128)(2,1)S(1)} %collective-permute-done.6.refs_1_, bf16[512,512]{1,0:T(8,128)(2,1)S(1)} %collective-permute-done.5.refs_2_, ...), custom_call_target="tpu_custom_call" | custom-call | flops 2415919104 | bytes 4718592 | tf_op jit(solution)/shard_map/project_round/pallas_call | solution.py:220
  43.1 1.3 %collective-permute-start.9 = (f32[3,16,512]{2,1,0:T(8,128)S(1)}, f32[3,16,512]{2,1,0:T(8,128)S(1)}, u32[]{:S(2)}, u32[]{:S(2)}) collective-permute-start(f32[3,16,512]{2,1,0:T(8,128)S(1)} %get-tuple-element.41), channel_id=1, source_target_pairs={{0,8},{8,16},{16,24},{24,32},{32,40},{40,48},{48,56},{56,64},{64,7... | collective-permute-start | bytes 294920 | tf_op jit(solution)/shard_map/ppermute | solution.py:145
  44.4 0.9 collective-permute-done.9.halo_acc
  45.4 1.2 collective-permute-done.7.lo
  46.6 3.2 %signal_of.1 = (bf16[512,512]{1,0:T(8,128)(2,1)}, f32[512,512]{1,0:T(8,128)}, f32[512,512]{1,0:T(8,128)}) custom-call(f32[3,512,512]{2,1,0:T(8,128)S(1)} %get-tuple-element.39.acc, bf16[256,512]{1,0:T(8,128)(2,1)S(1)} %collective-permute-done.7.lo, bf16[256,512]{1,0:T(8,128)(2,1)S(1)} %collective-permute-done.8.hi, ...), custom_call_target="tpu_custom_call" | custom-call | flops 805306368 | bytes 4194304 | tf_op jit(solution)/shard_map/signal_of/pallas_call | solution.py:300
  49.8 8.3 %all-to-all-start = ((bf16[16,32,512]{2,1,0:T(8,128)(2,1)}), bf16[16,32,512]{2,1,0:T(8,128)(2,1)S(1)}, u32[]{:S(2)}, u32[]{:S(2)}) async-start(bf16[16,32,512]{2,1,0:T(8,128)(2,1)} %bitcast.15), calls=%async_computation | async-start | bytes 1048576 | tf_op jit(solution)/shard_map/all_to_all | solution.py:408
  58.2 3.4 %filter_spectrum.1.h_ref = bf16[2,1152,256]{2,1,0:T(8,128)(2,1)} custom-call(bf16[512,512]{1,0:T(8,128)(2,1)} %bitcast.4.x_ref, bf16[144,64]{1,0:T(8,128)(2,1)S(1)} %copy-done.11, f32[2,72,128]{2,1,0:T(8,128)S(1)} %copy-done.10, bf16[256,256]{1,0:T(8,128)(2,1)S(1)} %copy-done.8), custom_call_target="tpu_custom_call" | custom-call | flops 4000000000 | bytes 4000000 | tf_op jit(solution)/shard_map/filter_spectrum/pallas_call | solution.py:111
  61.6 7.4 %all-to-all-done = bf16[16,32,512]{2,1,0:T(8,128)(2,1)S(1)} async-done(((bf16[16,32,512]{2,1,0:T(8,128)(2,1)}), bf16[16,32,512]{2,1,0:T(8,128)(2,1)S(1)}, u32[]{:S(2)}, u32[]{:S(2)}) %all-to-all-start) | async-done | bytes 524320 | tf_op jit(solution)/shard_map/all_to_all | solution.py:408
  69.0 3.7 %convolve.1 = bf16[512,512]{1,0:T(8,128)(2,1)S(1)} custom-call(bf16[512,512]{1,0:T(8,128)(2,1)S(1)} %bitcast.12, bf16[2,1152,256]{2,1,0:T(8,128)(2,1)} %filter_spectrum.1.h_ref, bf16[144,64]{1,0:T(8,128)(2,1)S(1)} %copy-done.11, f32[2,72,128]{2,1,0:T(8,128)S(1)} %copy-done.10, bf16[256,256]{1,0:T(8,128)(2,1)S(1)} %copy-done.8, ...), custom_call_target="tpu_custom_call" | custom-call | flops 5000000000 | bytes 4000000 | tf_op jit(solution)/shard_map/convolve/pallas_call | solution.py:130
  72.7 13.5 %all_to_all.33 = bf16[16,32,512]{2,1,0:T(8,128)(2,1)S(1)} all-to-all(bf16[16,32,512]{2,1,0:T(8,128)(2,1)S(1)} %bitcast.13), channel_id=1, replica_groups=mesh['seq'=16,'chan'=8] {'seq'}, dimensions={0} | all-to-all | bytes 1048576 | tf_op jit(solution)/shard_map/all_to_all | solution.py:409
  86.2 0.9 gate_and_project.1
  87.1 2.3 %collective-permute-start.14 = (bf16[160,512]{1,0:T(8,128)(2,1)S(1)}, bf16[160,512]{1,0:T(8,128)(2,1)S(1)}, u32[]{:S(2)}, u32[]{:S(2)}) collective-permute-start(bf16[160,512]{1,0:T(8,128)(2,1)S(1)} %get-tuple-element.56), channel_id=1, source_target_pairs={{0,1},{1,0},{2,3},{3,2},{4,5},{5,4},{6,7},{7,6},{8,9},{9,8},{10,11... | collective-permute-start | bytes 491528 | tf_op jit(solution)/shard_map/ppermute | solution.py:155
  89.5 1.6 %project_out.3 = (bf16[512,512]{1,0:T(8,128)(2,1)S(1)}, bf16[512,512]{1,0:T(8,128)(2,1)S(1)}, bf16[512,512]{1,0:T(8,128)(2,1)S(1)}) custom-call(bf16[512,512]{1,0:T(8,128)(2,1)S(1)} %get-tuple-element.46.g, bf16[512,4096]{1,0:T(8,128)(2,1)S(1)} %copy-done.1), custom_call_target="tpu_custom_call" | custom-call | flops 805306368 | bytes 3145728 | tf_op jit(solution)/shard_map/project_out/pallas_call | solution.py:366
  91.1 1.6 %collective-permute-start.10 = (bf16[176,512]{1,0:T(8,128)(2,1)S(1)}, bf16[176,512]{1,0:T(8,128)(2,1)S(1)}, u32[]{:S(2)}, u32[]{:S(2)}) collective-permute-start(bf16[176,512]{1,0:T(8,128)(2,1)S(1)} %get-tuple-element.49), channel_id=1, source_target_pairs={{0,6},{1,7},{2,0},{3,1},{4,2},{5,3},{6,4},{7,5},{8,14},{9,15},{10,... | collective-permute-start | bytes 540680 | tf_op jit(solution)/shard_map/ppermute | solution.py:150
  92.7 0.6 collective-permute-start.16
  93.3 0.8 collective-permute-done.14
  94.3 0.8 collective-permute-start.15
  95.1 1.6 %collective-permute-done.10 = bf16[176,512]{1,0:T(8,128)(2,1)S(1)} collective-permute-done((bf16[176,512]{1,0:T(8,128)(2,1)S(1)}, bf16[176,512]{1,0:T(8,128)(2,1)S(1)}, u32[]{:S(2)}, u32[]{:S(2)}) %collective-permute-start.10) | collective-permute-done | bytes 180256 | tf_op jit(solution)/shard_map/ppermute | solution.py:150
  96.8 2.8 %collective-permute-start.11 = (bf16[512,512]{1,0:T(8,128)(2,1)S(1)}, bf16[512,512]{1,0:T(8,128)(2,1)S(1)}, u32[]{:S(2)}, u32[]{:S(2)}) collective-permute-start(bf16[512,512]{1,0:T(8,128)(2,1)S(1)} %pad_maximum_fusion), channel_id=1, source_target_pairs={{0,6},{1,7},{2,0},{3,1},{4,2},{5,3},{6,4},{7,5},{8,14},{9,15},{10,... | collective-permute-start | bytes 1572872 | tf_op jit(solution)/shard_map/ppermute | solution.py:150
  99.6 1.9 %collective-permute-done.16 = bf16[176,512]{1,0:T(8,128)(2,1)S(1)} collective-permute-done((bf16[176,512]{1,0:T(8,128)(2,1)S(1)}, bf16[176,512]{1,0:T(8,128)(2,1)S(1)}, u32[]{:S(2)}, u32[]{:S(2)}) %collective-permute-start.16) | collective-permute-done | bytes 180256 | tf_op jit(solution)/shard_map/ppermute | solution.py:150
  101.6 0.1 collective-permute-start.17
  101.7 2.1 %project_out.2 = (bf16[512,512]{1,0:T(8,128)(2,1)S(1)}, bf16[512,512]{1,0:T(8,128)(2,1)S(1)}, bf16[512,512]{1,0:T(8,128)(2,1)S(1)}, bf16[512,512]{1,0:T(8,128)(2,1)S(1)}) custom-call(bf16[512,512]{1,0:T(8,128)(2,1)S(1)} %get-tuple-element.46.g, bf16[512,4096]{1,0:T(8,128)(2,1)S(1)} %copy-done.1), custom_call_target="tpu_custom_call" | custom-call | flops 1073741824 | bytes 4194304 | tf_op jit(solution)/shard_map/project_out/pallas_call | solution.py:366
  103.8 5.0 %collective-permute-done.11 = bf16[512,512]{1,0:T(8,128)(2,1)S(1)} collective-permute-done((bf16[512,512]{1,0:T(8,128)(2,1)S(1)}, bf16[512,512]{1,0:T(8,128)(2,1)S(1)}, u32[]{:S(2)}, u32[]{:S(2)}) %collective-permute-start.11) | collective-permute-done | bytes 524320 | tf_op jit(solution)/shard_map/ppermute | solution.py:150
  108.8 0.1 add_convert_fusion.2
  109.0 1.4 %collective-permute-start.13 = (bf16[512,512]{1,0:T(8,128)(2,1)S(1)}, bf16[512,512]{1,0:T(8,128)(2,1)S(1)}, u32[]{:S(2)}, u32[]{:S(2)}) collective-permute-start(bf16[512,512]{1,0:T(8,128)(2,1)S(1)} %add_convert_fusion.2), channel_id=1, source_target_pairs={{0,1},{1,0},{2,3},{3,2},{4,5},{5,4},{6,7},{7,6},{8,9},{9,8},{10,11... | collective-permute-start | bytes 1572872 | tf_op jit(solution)/shard_map/ppermute | solution.py:155
  110.4 3.0 %collective-permute-start.12 = (bf16[512,512]{1,0:T(8,128)(2,1)S(1)}, bf16[512,512]{1,0:T(8,128)(2,1)S(1)}, u32[]{:S(2)}, u32[]{:S(2)}) collective-permute-start(bf16[512,512]{1,0:T(8,128)(2,1)S(1)} %get-tuple-element.51), channel_id=1, source_target_pairs={{0,6},{1,7},{2,0},{3,1},{4,2},{5,3},{6,4},{7,5},{8,14},{9,15},{10,... | collective-permute-start | bytes 1572872 | tf_op jit(solution)/shard_map/ppermute | solution.py:150
  113.4 1.9 %collective-permute-done.17 = bf16[512,512]{1,0:T(8,128)(2,1)S(1)} collective-permute-done((bf16[512,512]{1,0:T(8,128)(2,1)S(1)}, bf16[512,512]{1,0:T(8,128)(2,1)S(1)}, u32[]{:S(2)}, u32[]{:S(2)}) %collective-permute-start.17) | collective-permute-done | bytes 524320 | tf_op jit(solution)/shard_map/ppermute | solution.py:155
  115.2 0.2 add_convert_fusion.1
  115.5 8.4 %collective-permute-done.13 = bf16[512,512]{1,0:T(8,128)(2,1)S(1)} collective-permute-done((bf16[512,512]{1,0:T(8,128)(2,1)S(1)}, bf16[512,512]{1,0:T(8,128)(2,1)S(1)}, u32[]{:S(2)}, u32[]{:S(2)}) %collective-permute-start.13) | collective-permute-done | bytes 524320 | tf_op jit(solution)/shard_map/ppermute | solution.py:155
  123.9 2.0 %collective-permute-done.18 = bf16[512,512]{1,0:T(8,128)(2,1)S(1)} collective-permute-done((bf16[512,512]{1,0:T(8,128)(2,1)S(1)}, bf16[512,512]{1,0:T(8,128)(2,1)S(1)}, u32[]{:S(2)}, u32[]{:S(2)}) %collective-permute-start.18) | collective-permute-done | bytes 524320 | tf_op jit(solution)/shard_map/ppermute | solution.py:150
  125.9 1.1 add_convert_fusion
  (46 shorter events, 0.5 us)
Async XLA Ops:
  0.0 17.6 %collective-permute-start = (bf16[512,512]{1,0:T(8,128)(2,1)}, bf16[512,512]{1,0:T(8,128)(2,1)S(1)}, u32[]{:S(2)}, u32[]{:S(2)}) collective-permute-start(bf16[512,512]{1,0:T(8,128)(2,1)} %refs_0_.1), channel_id=1, source_target_pairs={{0,6},{1,7},{2,0},{3,1},{4,2},{5,3},{6,4},{7,5},{8,14},{9,15},{10,... | collective-permute-start | bytes 1572872 | tf_op jit(solution)/shard_map/ppermute | solution.py:150
  3.1 15.3 %collective-permute-start.1 = (bf16[512,512]{1,0:T(8,128)(2,1)}, bf16[512,512]{1,0:T(8,128)(2,1)S(1)}, u32[]{:S(2)}, u32[]{:S(2)}) collective-permute-start(bf16[512,512]{1,0:T(8,128)(2,1)} %refs_0_.1), channel_id=1, source_target_pairs={{0,1},{1,0},{2,3},{3,2},{4,5},{5,4},{6,7},{7,6},{8,9},{9,8},{10,11... | collective-permute-start | bytes 1572872 | tf_op jit(solution)/shard_map/ppermute | solution.py:155
  6.1 14.9 %collective-permute-start.2 = (bf16[512,512]{1,0:T(8,128)(2,1)}, bf16[512,512]{1,0:T(8,128)(2,1)S(1)}, u32[]{:S(2)}, u32[]{:S(2)}) collective-permute-start(bf16[512,512]{1,0:T(8,128)(2,1)} %refs_0_.1), channel_id=1, source_target_pairs={{0,2},{1,3},{2,4},{3,5},{4,6},{5,7},{6,0},{7,1},{8,10},{9,11},{10,... | collective-permute-start | bytes 1572872 | tf_op jit(solution)/shard_map/ppermute | solution.py:150
  6.9 10.7 %collective-permute-start.3 = (bf16[16,512]{1,0:T(8,128)(2,1)S(1)}, bf16[16,512]{1,0:T(8,128)(2,1)S(1)}, u32[]{:S(2)}, u32[]{:S(2)}) collective-permute-start(bf16[16,512]{1,0:T(8,128)(2,1)S(1)} %slice.30), channel_id=1, source_target_pairs={{0,13},{1,12},{2,15},{3,14},{4,9},{5,8},{6,11},{7,10},{8,21},{9,20... | collective-permute-start | bytes 49160 | tf_op jit(solution)/shard_map/ppermute | solution.py:161
  9.5 1.2 copy-start.4
  21.0 15.6 %collective-permute-start.4 = (bf16[512,512]{1,0:T(8,128)(2,1)S(1)}, bf16[512,512]{1,0:T(8,128)(2,1)S(1)}, u32[]{:S(2)}, u32[]{:S(2)}) collective-permute-start(bf16[512,512]{1,0:T(8,128)(2,1)S(1)} %collective-permute-done.refs_2_), channel_id=1, source_target_pairs={{0,6},{1,7},{2,0},{3,1},{4,2},{5,3},{6,4},{7,5},{8,14},{9,15},{10,... | collective-permute-start | bytes 1572872 | tf_op jit(solution)/shard_map/ppermute | solution.py:150
  21.0 15.7 %collective-permute-start.5 = (bf16[512,512]{1,0:T(8,128)(2,1)S(1)}, bf16[512,512]{1,0:T(8,128)(2,1)S(1)}, u32[]{:S(2)}, u32[]{:S(2)}) collective-permute-start(bf16[512,512]{1,0:T(8,128)(2,1)S(1)} %collective-permute-done.refs_2_), channel_id=1, source_target_pairs={{0,1},{1,0},{2,3},{3,2},{4,5},{5,4},{6,7},{7,6},{8,9},{9,8},{10,11... | collective-permute-start | bytes 1572872 | tf_op jit(solution)/shard_map/ppermute | solution.py:155
  22.1 14.9 %collective-permute-start.6 = (bf16[512,512]{1,0:T(8,128)(2,1)S(1)}, bf16[512,512]{1,0:T(8,128)(2,1)S(1)}, u32[]{:S(2)}, u32[]{:S(2)}) collective-permute-start(bf16[512,512]{1,0:T(8,128)(2,1)S(1)} %collective-permute-done.1.refs_3_), channel_id=1, source_target_pairs={{0,2},{1,3},{2,4},{3,5},{4,6},{5,7},{6,0},{7,1},{8,10},{9,11},{10,... | collective-permute-start | bytes 1572872 | tf_op jit(solution)/shard_map/ppermute | solution.py:150
  23.4 26.4 %all-to-all-start.1 = ((bf16[16,32,512]{2,1,0:T(8,128)(2,1)}), bf16[16,32,512]{2,1,0:T(8,128)(2,1)}, u32[]{:S(2)}, u32[]{:S(2)}) async-start(bf16[16,32,512]{2,1,0:T(8,128)(2,1)} %bitcast.3), calls=%async_computation.1 | async-start | bytes 1048576 | tf_op jit(solution)/shard_map/all_to_all | solution.py:399
  29.9 1.0 copy-start.5
  31.0 9.5 %copy-start = (bf16[4096,3,512]{2,0,1:T(8,128)(2,1)S(1)}, bf16[4096,3,512]{2,0,1:T(8,128)(2,1)}, u32[]{:S(2)}) copy-start(bf16[4096,3,512]{2,0,1:T(8,128)(2,1)} %param.12) | copy-start | bytes 37748740
  37.1 9.4 %collective-permute-start.7 = (bf16[256,512]{1,0:T(8,128)(2,1)S(1)}, bf16[256,512]{1,0:T(8,128)(2,1)S(1)}, u32[]{:S(2)}, u32[]{:S(2)}) collective-permute-start(bf16[256,512]{1,0:T(8,128)(2,1)S(1)} %slice.31), channel_id=1, source_target_pairs={{0,2},{1,3},{2,4},{3,5},{4,6},{5,7},{6,0},{7,1},{8,10},{9,11},{10,... | collective-permute-start | bytes 786440 | tf_op jit(solution)/shard_map/ppermute | solution.py:150
  38.8 7.7 %copy-start.6 = (f32[3,3,512]{2,1,0:T(4,128)S(1)}, f32[3,3,512]{2,1,0:T(4,128)}, u32[]{:S(2)}) copy-start(f32[3,3,512]{2,1,0:T(4,128)} %taps.1) | copy-start | bytes 55300
  38.8 7.7 %collective-permute-start.8 = (bf16[256,512]{1,0:T(8,128)(2,1)S(1)}, bf16[256,512]{1,0:T(8,128)(2,1)S(1)}, u32[]{:S(2)}, u32[]{:S(2)}) collective-permute-start(bf16[256,512]{1,0:T(8,128)(2,1)S(1)} %slice.32), channel_id=1, source_target_pairs={{0,6},{1,7},{2,0},{3,1},{4,2},{5,3},{6,4},{7,5},{8,14},{9,15},{10,... | collective-permute-start | bytes 786440 | tf_op jit(solution)/shard_map/ppermute | solution.py:150
  43.1 2.2 %collective-permute-start.9 = (f32[3,16,512]{2,1,0:T(8,128)S(1)}, f32[3,16,512]{2,1,0:T(8,128)S(1)}, u32[]{:S(2)}, u32[]{:S(2)}) collective-permute-start(f32[3,16,512]{2,1,0:T(8,128)S(1)} %get-tuple-element.41), channel_id=1, source_target_pairs={{0,8},{8,16},{16,24},{24,32},{32,40},{40,48},{48,56},{56,64},{64,7... | collective-permute-start | bytes 294920 | tf_op jit(solution)/shard_map/ppermute | solution.py:145
  46.6 11.6 %copy-start.8 = (bf16[256,256]{1,0:T(8,128)(2,1)S(1)}, bf16[256,256]{1,0:T(8,128)(2,1)}, u32[]{:S(2)}) copy-start(bf16[256,256]{1,0:T(8,128)(2,1)} %constant.12.clone.forward) | copy-start | bytes 393220
  46.6 11.6 %copy-start.10 = (f32[2,72,128]{2,1,0:T(8,128)S(1)}, f32[2,72,128]{2,1,0:T(8,128)}, u32[]{:S(2)}) copy-start(f32[2,72,128]{2,1,0:T(8,128)} %constant.11.clone.tw) | copy-start | bytes 221188
  46.6 11.6 %copy-start.11 = (bf16[144,64]{1,0:T(8,128)(2,1)S(1)}, bf16[144,64]{1,0:T(8,128)(2,1)}, u32[]{:S(2)}) copy-start(bf16[144,64]{1,0:T(8,128)(2,1)} %constant.10.clone.first) | copy-start | bytes 55300
  49.8 19.1 %all-to-all-start = ((bf16[16,32,512]{2,1,0:T(8,128)(2,1)}), bf16[16,32,512]{2,1,0:T(8,128)(2,1)S(1)}, u32[]{:S(2)}, u32[]{:S(2)}) async-start(bf16[16,32,512]{2,1,0:T(8,128)(2,1)} %bitcast.15), calls=%async_computation | async-start | bytes 1048576 | tf_op jit(solution)/shard_map/all_to_all | solution.py:408
  58.1 10.8 %copy-start.9 = (bf16[256,256]{1,0:T(8,128)(2,1)S(1)}, bf16[256,256]{1,0:T(8,128)(2,1)}, u32[]{:S(2)}) copy-start(bf16[256,256]{1,0:T(8,128)(2,1)} %constant.13.clone.backward) | copy-start | bytes 393220
  58.2 10.8 %copy-start.12 = (bf16[64,144]{1,0:T(8,128)(2,1)S(1)}, bf16[64,144]{1,0:T(8,128)(2,1)}, u32[]{:S(2)}) copy-start(bf16[64,144]{1,0:T(8,128)(2,1)} %constant.14.clone.last) | copy-start | bytes 55300
  69.0 17.2 %copy-start.1 = (bf16[512,4096]{1,0:T(8,128)(2,1)S(1)}, bf16[512,4096]{1,0:T(8,128)(2,1)}, u32[]{:S(2)}) copy-start(bf16[512,4096]{1,0:T(8,128)(2,1)} %weight.5) | copy-start | bytes 12582916
  69.0 17.2 %copy-start.2 = (f32[512,512]{1,0:T(8,128)S(1)}, f32[512,512]{1,0:T(8,128)}, u32[]{:S(2)}) copy-start(f32[512,512]{1,0:T(8,128)} %get-tuple-element.44.signal) | copy-start | bytes 3145732
  69.0 17.2 %copy-start.3 = (f32[512,512]{1,0:T(8,128)S(1)}, f32[512,512]{1,0:T(8,128)}, u32[]{:S(2)}) copy-start(f32[512,512]{1,0:T(8,128)} %get-tuple-element.45.gate_out) | copy-start | bytes 3145732
  69.0 17.2 %copy-start.7 = (f32[512]{0:T(512)S(1)}, f32[512]{0:T(512)}, u32[]{:S(2)}) copy-start(f32[512]{0:T(512)} %param.15) | copy-start | bytes 6148
  87.1 7.0 %collective-permute-start.14 = (bf16[160,512]{1,0:T(8,128)(2,1)S(1)}, bf16[160,512]{1,0:T(8,128)(2,1)S(1)}, u32[]{:S(2)}, u32[]{:S(2)}) collective-permute-start(bf16[160,512]{1,0:T(8,128)(2,1)S(1)} %get-tuple-element.56), channel_id=1, source_target_pairs={{0,1},{1,0},{2,3},{3,2},{4,5},{5,4},{6,7},{7,6},{8,9},{9,8},{10,11... | collective-permute-start | bytes 491528 | tf_op jit(solution)/shard_map/ppermute | solution.py:155
  91.1 5.6 %collective-permute-start.10 = (bf16[176,512]{1,0:T(8,128)(2,1)S(1)}, bf16[176,512]{1,0:T(8,128)(2,1)S(1)}, u32[]{:S(2)}, u32[]{:S(2)}) collective-permute-start(bf16[176,512]{1,0:T(8,128)(2,1)S(1)} %get-tuple-element.49), channel_id=1, source_target_pairs={{0,6},{1,7},{2,0},{3,1},{4,2},{5,3},{6,4},{7,5},{8,14},{9,15},{10,... | collective-permute-start | bytes 540680 | tf_op jit(solution)/shard_map/ppermute | solution.py:150
  92.7 8.8 %collective-permute-start.16 = (bf16[176,512]{1,0:T(8,128)(2,1)S(1)}, bf16[176,512]{1,0:T(8,128)(2,1)S(1)}, u32[]{:S(2)}, u32[]{:S(2)}) collective-permute-start(bf16[176,512]{1,0:T(8,128)(2,1)S(1)} %get-tuple-element.58), channel_id=1, source_target_pairs={{0,2},{1,3},{2,4},{3,5},{4,6},{5,7},{6,0},{7,1},{8,10},{9,11},{10,... | collective-permute-start | bytes 540680 | tf_op jit(solution)/shard_map/ppermute | solution.py:150
  94.3 19.1 %collective-permute-start.15 = (bf16[512,512]{1,0:T(8,128)(2,1)S(1)}, bf16[512,512]{1,0:T(8,128)(2,1)S(1)}, u32[]{:S(2)}, u32[]{:S(2)}) collective-permute-start(bf16[512,512]{1,0:T(8,128)(2,1)S(1)} %pad_maximum_fusion.1), channel_id=1, source_target_pairs={{0,2},{1,3},{2,4},{3,5},{4,6},{5,7},{6,0},{7,1},{8,10},{9,11},{10,... | collective-permute-start | bytes 1572872 | tf_op jit(solution)/shard_map/ppermute | solution.py:150
  96.8 12.0 %collective-permute-start.11 = (bf16[512,512]{1,0:T(8,128)(2,1)S(1)}, bf16[512,512]{1,0:T(8,128)(2,1)S(1)}, u32[]{:S(2)}, u32[]{:S(2)}) collective-permute-start(bf16[512,512]{1,0:T(8,128)(2,1)S(1)} %pad_maximum_fusion), channel_id=1, source_target_pairs={{0,6},{1,7},{2,0},{3,1},{4,2},{5,3},{6,4},{7,5},{8,14},{9,15},{10,... | collective-permute-start | bytes 1572872 | tf_op jit(solution)/shard_map/ppermute | solution.py:150
  101.6 13.6 %collective-permute-start.17 = (bf16[512,512]{1,0:T(8,128)(2,1)S(1)}, bf16[512,512]{1,0:T(8,128)(2,1)S(1)}, u32[]{:S(2)}, u32[]{:S(2)}) collective-permute-start(bf16[512,512]{1,0:T(8,128)(2,1)S(1)} %pad_maximum_fusion.2), channel_id=1, source_target_pairs={{0,1},{1,0},{2,3},{3,2},{4,5},{5,4},{6,7},{7,6},{8,9},{9,8},{10,11... | collective-permute-start | bytes 1572872 | tf_op jit(solution)/shard_map/ppermute | solution.py:155
  109.0 15.0 %collective-permute-start.13 = (bf16[512,512]{1,0:T(8,128)(2,1)S(1)}, bf16[512,512]{1,0:T(8,128)(2,1)S(1)}, u32[]{:S(2)}, u32[]{:S(2)}) collective-permute-start(bf16[512,512]{1,0:T(8,128)(2,1)S(1)} %add_convert_fusion.2), channel_id=1, source_target_pairs={{0,1},{1,0},{2,3},{3,2},{4,5},{5,4},{6,7},{7,6},{8,9},{9,8},{10,11... | collective-permute-start | bytes 1572872 | tf_op jit(solution)/shard_map/ppermute | solution.py:155
  110.4 13.6 %collective-permute-start.12 = (bf16[512,512]{1,0:T(8,128)(2,1)S(1)}, bf16[512,512]{1,0:T(8,128)(2,1)S(1)}, u32[]{:S(2)}, u32[]{:S(2)}) collective-permute-start(bf16[512,512]{1,0:T(8,128)(2,1)S(1)} %get-tuple-element.51), channel_id=1, source_target_pairs={{0,6},{1,7},{2,0},{3,1},{4,2},{5,3},{6,4},{7,5},{8,14},{9,15},{10,... | collective-permute-start | bytes 1572872 | tf_op jit(solution)/shard_map/ppermute | solution.py:150
  115.4 10.5 %collective-permute-start.18 = (bf16[512,512]{1,0:T(8,128)(2,1)S(1)}, bf16[512,512]{1,0:T(8,128)(2,1)S(1)}, u32[]{:S(2)}, u32[]{:S(2)}) collective-permute-start(bf16[512,512]{1,0:T(8,128)(2,1)S(1)} %add_convert_fusion.1), channel_id=1, source_target_pairs={{0,2},{1,3},{2,4},{3,5},{4,6},{5,7},{6,0},{7,1},{8,10},{9,11},{10,... | collective-permute-start | bytes 1572872 | tf_op jit(solution)/shard_map/ppermute | solution.py:150

commit v5 on v4

--- a/solution.py
+++ b/solution.py
@@ -10,7 +10,7 @@
 from jax.sharding import PartitionSpec as P
 
 K1 = 72
-GROUP = 16
+GROUP = 32
 
 
 def fourier_tables(seqs, rows):
@@ -117,7 +117,7 @@
             pltpu.VMEM(shape, jnp.bfloat16),
             pltpu.SemaphoreType.DMA(shape[:1]),
         ],
-        compiler_params=params(10),
+        compiler_params=params(16),
         name="filter_spectrum",
         cost_estimate=pl.CostEstimate(flops=4_000_000_000, bytes_accessed=4_000_000, transcendentals=0),
     )(x, first, tw, forward)
@@ -133,7 +133,7 @@
         in_specs=[whole(), in_hbm()] + [whole()] * 5, out_specs=whole(),
         scratch_shapes=[pltpu.VMEM((x.shape[1] // 128, x.shape[0], 128), jnp.float32)] * 2
         + [pltpu.VMEM(spec.shape, spec.dtype), pltpu.SemaphoreType.DMA(spec.shape[:1])],
-        compiler_params=params(12),
+        compiler_params=params(20),
         name="convolve",
         cost_estimate=pl.CostEstimate(flops=5_000_000_000, bytes_accessed=4_000_000, transcendentals=0),
     )(x, from_hbm(spec), first, tw, forward, backward, last)
@@ -374,11 +374,6 @@
     )(gated, weight)
 
 
-def thirds(rows):
-    tiles = rows // 16
-    return (tiles + 2) // 3 * 16, 2 * ((tiles + 2) // 3) * 16
-
-
 def added(*terms):
     return sum(t.astype(jnp.float32) for t in terms).astype(jnp.bfloat16)
 
@@ -409,16 +404,16 @@
     conv = lax.all_to_all(conv, "seq", 0, 0, tiled=True)
 
     skip = skip_gain.reshape(1, width)
-    one, two = thirds(rows)
-    gated, *pieces = gate_and_project(conv, signal, gate_out, skip, (2, 1), (one, two - one, rows - two), out_weight, cols)
-    to_down, to_up, to_far = ring(pieces[0], -1), ring(pieces[1], 1), cross(pieces[2])
-    up_side, down_side, far = project_out(gated, [(1, 1), (-1, 1), (2, 0)], (1, 1, 1), out_weight, cols)
+    gated, to_far, to_up = gate_and_project(conv, signal, gate_out, skip, (2, 1), (half, half), out_weight, cols)
+    to_far, to_up = cross(to_far), ring(to_up, 1)
+    down_side, up_side, far = project_out(gated, [(-1, 1), (1, 1), (2, 0)], (1, 1, 1), out_weight, cols)
+    down_side = ring(down_side, -1)
     up, down, side, own = project_out(gated, [(1, 0), (-1, 0), (0, 1), (0, 0)], (1, 1, 1, 1), out_weight, cols)
-    down_side = ring(jnp.concatenate([added(down_side[:one], to_down), down_side[one:]], axis=0), -1)
-    up_side = cross(jnp.concatenate([up_side[:one], added(up_side[one:two], to_up), up_side[two:]], axis=0))
-    far = ring(jnp.concatenate([far[:two], added(far[two:], to_far)], axis=0), 1)
+    up_side = cross(jnp.concatenate([up_side[:half], added(up_side[half:], to_up)], axis=0))
+    far = ring(jnp.concatenate([added(far[:half], to_far), far[half:]], axis=0), 1)
     down_side, down = together((down_side, down))
-    side = cross(added(side, down_side))
+    up_side, side = together((up_side, added(side, down_side)))
+    side = cross(side)
     up = added(up, far, up_side)
     up, down = ring(up, 1), ring(down, -1)
     return added(own, down, side, up)

time: 129 us -> 126 us (0.977)
  waiting for transfers between devices: 40.7 us -> 39 us
    ppermute x5, waiting for transfers between devices: 11.9 us -> 2.74 us  [cross(): return lax.ppermute(array, 'chan', [(i, i ^ 1) for i in range(count)])]
    ppermute x12 -> x11, waiting for transfers between devices: 14.7 us -> 22.3 us  [ring(): lax.ppermute(array, 'chan', [(i, (i + 2 * by) % count) for i in range(cou...]
    ppermute x5, starting transfers between devices: 7.99 us -> 9.9 us  [cross(): return lax.ppermute(array, 'chan', [(i, i ^ 1) for i in range(count)])]
    ppermute x12 -> x11, starting transfers between devices: 16.7 us -> 15.2 us  [ring(): lax.ppermute(array, 'chan', [(i, (i + 2 * by) % count) for i in range(cou...]
  transfers between devices with their start and end apart: 21 -> 20, of which waited for: 14 -> 14; matrix products, arithmetic and copies ran while one was open for 1% -> 1% of each run, Pallas kernels for 15% -> 16%
where the time goes in v5:
time: 126 us; the launch traced here: 125 us
  starting transfers between devices  43.8 us (35%)
  waiting for transfers between devices  39 us (31%)
  Pallas kernels  23.7 us (19%)
  blocking collectives  13.5 us (11%)
  local copies, waits for them, and re-layouts  3.17 us (3%)
  other arithmetic  1.6 us (1%)
    ppermute x11, waiting for transfers between devices, ring(): lax.ppermute(array, 'chan', [(i, (i + 2 * by) % count) for i in range(cou...  22.3 us
    ppermute x11, starting transfers between devices, ring(): lax.ppermute(array, 'chan', [(i, (i + 2 * by) % count) for i in range(cou...  15.2 us
    all_to_all x1, blocking collectives, shards(): conv = lax.all_to_all(conv, 'seq', 0, 0, tiled=True)  13.5 us
    ppermute x5, starting transfers between devices, cross(): return lax.ppermute(array, 'chan', [(i, i ^ 1) for i in range(count)])  9.9 us
    all_to_all x1, starting transfers between devices, shards(): lax.all_to_all(signal_t, 'seq', 0, 0, tiled=True)  8.28 us
    all_to_all x1, waiting for transfers between devices, shards(): lax.all_to_all(signal_t, 'seq', 0, 0, tiled=True)  7.21 us
    all_to_all x1, starting transfers between devices, shards(): fil = lax.all_to_all(fil, 'seq', 0, 0, tiled=True)  6.5 us
    ppermute x1, waiting for transfers between devices, following_far(): return lax.ppermute(array, ('seq', 'chan'), pairs)  5.84 us
  transfers between devices with their start and end apart: 20, of which 14 were waited for; matrix products, arithmetic and copies ran while one was open for 1% of the time, Pallas kernels for 16%

profile of v5, /device:TPU:0, one launch (start us, length us, event | category | flops | bytes accessed | tf_op | source)
XLA Modules:
  0.0 125.1 jit_solution(10074811715621010462)
XLA Ops:
  0.0 3.1 %collective-permute-start = (bf16[512,512]{1,0:T(8,128)(2,1)}, bf16[512,512]{1,0:T(8,128)(2,1)S(1)}, u32[]{:S(2)}, u32[]{:S(2)}) collective-permute-start(bf16[512,512]{1,0:T(8,128)(2,1)} %refs_0_.1), channel_id=1, source_target_pairs={{0,6},{1,7},{2,0},{3,1},{4,2},{5,3},{6,4},{7,5},{8,14},{9,15},{10,... | collective-permute-start | bytes 1572872 | tf_op jit(solution)/shard_map/ppermute | solution.py:150
  3.1 3.0 %collective-permute-start.1 = (bf16[512,512]{1,0:T(8,128)(2,1)}, bf16[512,512]{1,0:T(8,128)(2,1)S(1)}, u32[]{:S(2)}, u32[]{:S(2)}) collective-permute-start(bf16[512,512]{1,0:T(8,128)(2,1)} %refs_0_.1), channel_id=1, source_target_pairs={{0,1},{1,0},{2,3},{3,2},{4,5},{5,4},{6,7},{7,6},{8,9},{9,8},{10,11... | collective-permute-start | bytes 1572872 | tf_op jit(solution)/shard_map/ppermute | solution.py:155
  6.1 0.8 slice.21
  6.9 2.6 %collective-permute-start.3 = (bf16[16,512]{1,0:T(8,128)(2,1)S(1)}, bf16[16,512]{1,0:T(8,128)(2,1)S(1)}, u32[]{:S(2)}, u32[]{:S(2)}) collective-permute-start(bf16[16,512]{1,0:T(8,128)(2,1)S(1)} %slice.21), channel_id=1, source_target_pairs={{0,13},{1,12},{2,15},{3,14},{4,9},{5,8},{6,11},{7,10},{8,21},{9,20... | collective-permute-start | bytes 49160 | tf_op jit(solution)/shard_map/ppermute | solution.py:161
  9.5 1.2 copy-done.4
  10.8 1.0 transposed.1
  11.7 5.8 %collective-permute-done.3.halo = bf16[16,512]{1,0:T(8,128)(2,1)S(1)} collective-permute-done((bf16[16,512]{1,0:T(8,128)(2,1)S(1)}, bf16[16,512]{1,0:T(8,128)(2,1)S(1)}, u32[]{:S(2)}, u32[]{:S(2)}) %collective-permute-start.3) | collective-permute-done | bytes 16416 | tf_op jit(solution)/shard_map/ppermute | solution.py:161
  17.6 0.8 collective-permute-done.1.refs_3_
  18.4 2.6 %collective-permute-done.2.refs_1_ = bf16[512,512]{1,0:T(8,128)(2,1)S(1)} collective-permute-done((bf16[512,512]{1,0:T(8,128)(2,1)}, bf16[512,512]{1,0:T(8,128)(2,1)S(1)}, u32[]{:S(2)}, u32[]{:S(2)}) %collective-permute-start.2) | collective-permute-done | bytes 524320 | tf_op jit(solution)/shard_map/ppermute | solution.py:150
  21.0 1.1 collective-permute-start.5
  22.1 1.3 %collective-permute-start.6 = (bf16[512,512]{1,0:T(8,128)(2,1)S(1)}, bf16[512,512]{1,0:T(8,128)(2,1)S(1)}, u32[]{:S(2)}, u32[]{:S(2)}) collective-permute-start(bf16[512,512]{1,0:T(8,128)(2,1)S(1)} %collective-permute-done.1.refs_3_), channel_id=1, source_target_pairs={{0,2},{1,3},{2,4},{3,5},{4,6},{5,7},{6,0},{7,1},{8,10},{9,11},{10,... | collective-permute-start | bytes 1572872 | tf_op jit(solution)/shard_map/ppermute | solution.py:150
  23.4 6.5 %all-to-all-start.1 = ((bf16[16,32,512]{2,1,0:T(8,128)(2,1)}), bf16[16,32,512]{2,1,0:T(8,128)(2,1)}, u32[]{:S(2)}, u32[]{:S(2)}) async-start(bf16[16,32,512]{2,1,0:T(8,128)(2,1)} %bitcast.3), calls=%async_computation.1 | async-start | bytes 1048576 | tf_op jit(solution)/shard_map/all_to_all | solution.py:394
  29.9 1.0 copy-done.5
  31.0 5.6 %first_round.1.refs_0_ = f32[3,512,512]{2,1,0:T(8,128)S(1)} custom-call(bf16[512,512]{1,0:T(8,128)(2,1)S(1)} %copy-done.5, bf16[512,512]{1,0:T(8,128)(2,1)S(1)} %collective-permute-done.2.refs_1_, bf16[512,512]{1,0:T(8,128)(2,1)S(1)} %collective-permute-done.refs_2_, bf16[512,512]{1,0:T(8,128)(2,1)S(1)} %collective-permute-done.1.refs_3_, ...), custom_call_target="tpu_custom_call" | custom-call | flops 3221225472 | bytes 6291456 | tf_op jit(solution)/shard_map/first_round/pallas_call | solution.py:256
  36.7 0.4 collective-permute-done.6.refs_1_
  37.1 1.7 %collective-permute-start.7 = (bf16[256,512]{1,0:T(8,128)(2,1)S(1)}, bf16[256,512]{1,0:T(8,128)(2,1)S(1)}, u32[]{:S(2)}, u32[]{:S(2)}) collective-permute-start(bf16[256,512]{1,0:T(8,128)(2,1)S(1)} %slice.22), channel_id=1, source_target_pairs={{0,2},{1,3},{2,4},{3,5},{4,6},{5,7},{6,0},{7,1},{8,10},{9,11},{10,... | collective-permute-start | bytes 786440 | tf_op jit(solution)/shard_map/ppermute | solution.py:150
  38.8 1.7 %collective-permute-start.8 = (bf16[256,512]{1,0:T(8,128)(2,1)S(1)}, bf16[256,512]{1,0:T(8,128)(2,1)S(1)}, u32[]{:S(2)}, u32[]{:S(2)}) collective-permute-start(bf16[256,512]{1,0:T(8,128)(2,1)S(1)} %slice.23), channel_id=1, source_target_pairs={{0,6},{1,7},{2,0},{3,1},{4,2},{5,3},{6,4},{7,5},{8,14},{9,15},{10,... | collective-permute-start | bytes 786440 | tf_op jit(solution)/shard_map/ppermute | solution.py:150
  40.5 2.6 %project_round.1 = (f32[3,512,512]{2,1,0:T(8,128)S(1)}, f32[3,16,512]{2,1,0:T(8,128)S(1)}) custom-call(f32[3,512,512]{2,1,0:T(8,128)S(1)} %first_round.1.refs_0_, bf16[512,512]{1,0:T(8,128)(2,1)S(1)} %collective-permute-done.6.refs_1_, bf16[512,512]{1,0:T(8,128)(2,1)S(1)} %collective-permute-done.5.refs_2_, ...), custom_call_target="tpu_custom_call" | custom-call | flops 2415919104 | bytes 4718592 | tf_op jit(solution)/shard_map/project_round/pallas_call | solution.py:220
  43.1 1.3 %collective-permute-start.9 = (f32[3,16,512]{2,1,0:T(8,128)S(1)}, f32[3,16,512]{2,1,0:T(8,128)S(1)}, u32[]{:S(2)}, u32[]{:S(2)}) collective-permute-start(f32[3,16,512]{2,1,0:T(8,128)S(1)} %get-tuple-element.42), channel_id=1, source_target_pairs={{0,8},{8,16},{16,24},{24,32},{32,40},{40,48},{48,56},{56,64},{64,7... | collective-permute-start | bytes 294920 | tf_op jit(solution)/shard_map/ppermute | solution.py:145
  44.4 0.9 collective-permute-done.9.halo_acc
  45.4 1.2 collective-permute-done.7.lo
  46.6 3.2 %signal_of.1 = (bf16[512,512]{1,0:T(8,128)(2,1)}, f32[512,512]{1,0:T(8,128)}, f32[512,512]{1,0:T(8,128)}) custom-call(f32[3,512,512]{2,1,0:T(8,128)S(1)} %get-tuple-element.40.acc, bf16[256,512]{1,0:T(8,128)(2,1)S(1)} %collective-permute-done.7.lo, bf16[256,512]{1,0:T(8,128)(2,1)S(1)} %collective-permute-done.8.hi, ...), custom_call_target="tpu_custom_call" | custom-call | flops 805306368 | bytes 4194304 | tf_op jit(solution)/shard_map/signal_of/pallas_call | solution.py:300
  49.8 8.3 %all-to-all-start = ((bf16[16,32,512]{2,1,0:T(8,128)(2,1)}), bf16[16,32,512]{2,1,0:T(8,128)(2,1)S(1)}, u32[]{:S(2)}, u32[]{:S(2)}) async-start(bf16[16,32,512]{2,1,0:T(8,128)(2,1)} %bitcast.15), calls=%async_computation | async-start | bytes 1048576 | tf_op jit(solution)/shard_map/all_to_all | solution.py:403
  58.2 3.6 %filter_spectrum.1.h_ref = bf16[1,2304,256]{2,1,0:T(8,128)(2,1)} custom-call(bf16[512,512]{1,0:T(8,128)(2,1)} %bitcast.4.x_ref, bf16[144,64]{1,0:T(8,128)(2,1)S(1)} %copy-done.11, f32[2,72,128]{2,1,0:T(8,128)S(1)} %copy-done.10, bf16[256,256]{1,0:T(8,128)(2,1)S(1)} %copy-done.8), custom_call_target="tpu_custom_call" | custom-call | flops 4000000000 | bytes 4000000 | tf_op jit(solution)/shard_map/filter_spectrum/pallas_call | solution.py:111
  61.8 7.2 %all-to-all-done = bf16[16,32,512]{2,1,0:T(8,128)(2,1)S(1)} async-done(((bf16[16,32,512]{2,1,0:T(8,128)(2,1)}), bf16[16,32,512]{2,1,0:T(8,128)(2,1)S(1)}, u32[]{:S(2)}, u32[]{:S(2)}) %all-to-all-start) | async-done | bytes 524320 | tf_op jit(solution)/shard_map/all_to_all | solution.py:403
  69.0 3.1 %convolve.1 = bf16[512,512]{1,0:T(8,128)(2,1)S(1)} custom-call(bf16[512,512]{1,0:T(8,128)(2,1)S(1)} %bitcast.12, bf16[1,2304,256]{2,1,0:T(8,128)(2,1)} %filter_spectrum.1.h_ref, bf16[144,64]{1,0:T(8,128)(2,1)S(1)} %copy-done.11, f32[2,72,128]{2,1,0:T(8,128)S(1)} %copy-done.10, bf16[256,256]{1,0:T(8,128)(2,1)S(1)} %copy-done.8, ...), custom_call_target="tpu_custom_call" | custom-call | flops 5000000000 | bytes 4000000 | tf_op jit(solution)/shard_map/convolve/pallas_call | solution.py:130
  72.1 13.5 %all_to_all.33 = bf16[16,32,512]{2,1,0:T(8,128)(2,1)S(1)} all-to-all(bf16[16,32,512]{2,1,0:T(8,128)(2,1)S(1)} %bitcast.13), channel_id=1, replica_groups=mesh['seq'=16,'chan'=8] {'seq'}, dimensions={0} | all-to-all | bytes 1048576 | tf_op jit(solution)/shard_map/all_to_all | solution.py:404
  85.6 0.9 gate_and_project.1
  86.5 0.8 collective-permute-start.12
  87.3 2.0 %collective-permute-start.15 = (bf16[256,512]{1,0:T(8,128)(2,1)S(1)}, bf16[256,512]{1,0:T(8,128)(2,1)S(1)}, u32[]{:S(2)}, u32[]{:S(2)}) collective-permute-start(bf16[256,512]{1,0:T(8,128)(2,1)S(1)} %get-tuple-element.59), channel_id=1, source_target_pairs={{0,1},{1,0},{2,3},{3,2},{4,5},{5,4},{6,7},{7,6},{8,9},{9,8},{10,11... | collective-permute-start | bytes 786440 | tf_op jit(solution)/shard_map/ppermute | solution.py:155
  89.4 1.6 %project_out.3 = (bf16[512,512]{1,0:T(8,128)(2,1)S(1)}, bf16[512,512]{1,0:T(8,128)(2,1)S(1)}, bf16[512,512]{1,0:T(8,128)(2,1)S(1)}) custom-call(bf16[512,512]{1,0:T(8,128)(2,1)S(1)} %get-tuple-element.47.g, bf16[512,4096]{1,0:T(8,128)(2,1)S(1)} %copy-done.1), custom_call_target="tpu_custom_call" | custom-call | flops 805306368 | bytes 3145728 | tf_op jit(solution)/shard_map/project_out/pallas_call | solution.py:366
  91.0 2.7 %collective-permute-start.10 = (bf16[512,512]{1,0:T(8,128)(2,1)S(1)}, bf16[512,512]{1,0:T(8,128)(2,1)S(1)}, u32[]{:S(2)}, u32[]{:S(2)}) collective-permute-start(bf16[512,512]{1,0:T(8,128)(2,1)S(1)} %get-tuple-element.49), channel_id=1, source_target_pairs={{0,6},{1,7},{2,0},{3,1},{4,2},{5,3},{6,4},{7,5},{8,14},{9,15},{10,... | collective-permute-start | bytes 1572872 | tf_op jit(solution)/shard_map/ppermute | solution.py:150
  93.7 1.6 %collective-permute-done.12 = bf16[256,512]{1,0:T(8,128)(2,1)S(1)} collective-permute-done((bf16[256,512]{1,0:T(8,128)(2,1)S(1)}, bf16[256,512]{1,0:T(8,128)(2,1)S(1)}, u32[]{:S(2)}, u32[]{:S(2)}) %collective-permute-start.12) | collective-permute-done | bytes 262176 | tf_op jit(solution)/shard_map/ppermute | solution.py:150
  95.4 2.3 %collective-permute-start.13 = (bf16[512,512]{1,0:T(8,128)(2,1)S(1)}, bf16[512,512]{1,0:T(8,128)(2,1)S(1)}, u32[]{:S(2)}, u32[]{:S(2)}) collective-permute-start(bf16[512,512]{1,0:T(8,128)(2,1)S(1)} %pad_maximum_fusion), channel_id=1, source_target_pairs={{0,1},{1,0},{2,3},{3,2},{4,5},{5,4},{6,7},{7,6},{8,9},{9,8},{10,11... | collective-permute-start | bytes 1572872 | tf_op jit(solution)/shard_map/ppermute | solution.py:155
  97.9 0.1 collective-permute-start.16
  97.9 2.1 %project_out.2 = (bf16[512,512]{1,0:T(8,128)(2,1)S(1)}, bf16[512,512]{1,0:T(8,128)(2,1)S(1)}, bf16[512,512]{1,0:T(8,128)(2,1)S(1)}, bf16[512,512]{1,0:T(8,128)(2,1)S(1)}) custom-call(bf16[512,512]{1,0:T(8,128)(2,1)S(1)} %get-tuple-element.47.g, bf16[512,4096]{1,0:T(8,128)(2,1)S(1)} %copy-done.1), custom_call_target="tpu_custom_call" | custom-call | flops 1073741824 | bytes 4194304 | tf_op jit(solution)/shard_map/project_out/pallas_call | solution.py:366
  100.1 3.8 %collective-permute-done.10 = bf16[512,512]{1,0:T(8,128)(2,1)S(1)} collective-permute-done((bf16[512,512]{1,0:T(8,128)(2,1)S(1)}, bf16[512,512]{1,0:T(8,128)(2,1)S(1)}, u32[]{:S(2)}, u32[]{:S(2)}) %collective-permute-start.10) | collective-permute-done | bytes 524320 | tf_op jit(solution)/shard_map/ppermute | solution.py:150
  103.8 3.7 %collective-permute-start.11 = (bf16[512,512]{1,0:T(8,128)(2,1)S(1)}, bf16[512,512]{1,0:T(8,128)(2,1)S(1)}, u32[]{:S(2)}, u32[]{:S(2)}) collective-permute-start(bf16[512,512]{1,0:T(8,128)(2,1)S(1)} %get-tuple-element.51), channel_id=1, source_target_pairs={{0,6},{1,7},{2,0},{3,1},{4,2},{5,3},{6,4},{7,5},{8,14},{9,15},{10,... | collective-permute-start | bytes 1572872 | tf_op jit(solution)/shard_map/ppermute | solution.py:150
  107.5 0.1 add_convert_fusion.2
  107.7 1.6 %collective-permute-done.13 = bf16[512,512]{1,0:T(8,128)(2,1)S(1)} collective-permute-done((bf16[512,512]{1,0:T(8,128)(2,1)S(1)}, bf16[512,512]{1,0:T(8,128)(2,1)S(1)}, u32[]{:S(2)}, u32[]{:S(2)}) %collective-permute-start.13) | collective-permute-done | bytes 524320 | tf_op jit(solution)/shard_map/ppermute | solution.py:155
  109.2 1.9 %collective-permute-done.16 = bf16[512,512]{1,0:T(8,128)(2,1)S(1)} collective-permute-done((bf16[512,512]{1,0:T(8,128)(2,1)S(1)}, bf16[512,512]{1,0:T(8,128)(2,1)S(1)}, u32[]{:S(2)}, u32[]{:S(2)}) %collective-permute-start.16) | collective-permute-done | bytes 524320 | tf_op jit(solution)/shard_map/ppermute | solution.py:150
  111.1 0.2 add_convert_fusion.1
  111.3 0.1 collective-permute-start.17
  111.4 1.4 %collective-permute-start.14 = (bf16[512,512]{1,0:T(8,128)(2,1)S(1)}, bf16[512,512]{1,0:T(8,128)(2,1)S(1)}, u32[]{:S(2)}, u32[]{:S(2)}) collective-permute-start(bf16[512,512]{1,0:T(8,128)(2,1)S(1)} %add_convert_fusion.2), channel_id=1, source_target_pairs={{0,1},{1,0},{2,3},{3,2},{4,5},{5,4},{6,7},{7,6},{8,9},{9,8},{10,11... | collective-permute-start | bytes 1572872 | tf_op jit(solution)/shard_map/ppermute | solution.py:155
  112.8 4.0 %collective-permute-done.11 = bf16[512,512]{1,0:T(8,128)(2,1)S(1)} collective-permute-done((bf16[512,512]{1,0:T(8,128)(2,1)S(1)}, bf16[512,512]{1,0:T(8,128)(2,1)S(1)}, u32[]{:S(2)}, u32[]{:S(2)}) %collective-permute-start.11) | collective-permute-done | bytes 524320 | tf_op jit(solution)/shard_map/ppermute | solution.py:150
  116.7 6.9 %collective-permute-done.17 = bf16[512,512]{1,0:T(8,128)(2,1)S(1)} collective-permute-done((bf16[512,512]{1,0:T(8,128)(2,1)S(1)}, bf16[512,512]{1,0:T(8,128)(2,1)S(1)}, u32[]{:S(2)}, u32[]{:S(2)}) %collective-permute-start.17) | collective-permute-done | bytes 524320 | tf_op jit(solution)/shard_map/ppermute | solution.py:150
  123.6 0.4 collective-permute-done.14
  124.0 1.1 add_convert_fusion
  (40 shorter events, 0.4 us)
Async XLA Ops:
  0.0 17.6 %collective-permute-start = (bf16[512,512]{1,0:T(8,128)(2,1)}, bf16[512,512]{1,0:T(8,128)(2,1)S(1)}, u32[]{:S(2)}, u32[]{:S(2)}) collective-permute-start(bf16[512,512]{1,0:T(8,128)(2,1)} %refs_0_.1), channel_id=1, source_target_pairs={{0,6},{1,7},{2,0},{3,1},{4,2},{5,3},{6,4},{7,5},{8,14},{9,15},{10,... | collective-permute-start | bytes 1572872 | tf_op jit(solution)/shard_map/ppermute | solution.py:150
  3.1 15.3 %collective-permute-start.1 = (bf16[512,512]{1,0:T(8,128)(2,1)}, bf16[512,512]{1,0:T(8,128)(2,1)S(1)}, u32[]{:S(2)}, u32[]{:S(2)}) collective-permute-start(bf16[512,512]{1,0:T(8,128)(2,1)} %refs_0_.1), channel_id=1, source_target_pairs={{0,1},{1,0},{2,3},{3,2},{4,5},{5,4},{6,7},{7,6},{8,9},{9,8},{10,11... | collective-permute-start | bytes 1572872 | tf_op jit(solution)/shard_map/ppermute | solution.py:155
  6.1 14.9 %collective-permute-start.2 = (bf16[512,512]{1,0:T(8,128)(2,1)}, bf16[512,512]{1,0:T(8,128)(2,1)S(1)}, u32[]{:S(2)}, u32[]{:S(2)}) collective-permute-start(bf16[512,512]{1,0:T(8,128)(2,1)} %refs_0_.1), channel_id=1, source_target_pairs={{0,2},{1,3},{2,4},{3,5},{4,6},{5,7},{6,0},{7,1},{8,10},{9,11},{10,... | collective-permute-start | bytes 1572872 | tf_op jit(solution)/shard_map/ppermute | solution.py:150
  6.9 10.7 %collective-permute-start.3 = (bf16[16,512]{1,0:T(8,128)(2,1)S(1)}, bf16[16,512]{1,0:T(8,128)(2,1)S(1)}, u32[]{:S(2)}, u32[]{:S(2)}) collective-permute-start(bf16[16,512]{1,0:T(8,128)(2,1)S(1)} %slice.21), channel_id=1, source_target_pairs={{0,13},{1,12},{2,15},{3,14},{4,9},{5,8},{6,11},{7,10},{8,21},{9,20... | collective-permute-start | bytes 49160 | tf_op jit(solution)/shard_map/ppermute | solution.py:161
  9.5 1.2 copy-start.4
  21.0 15.6 %collective-permute-start.4 = (bf16[512,512]{1,0:T(8,128)(2,1)S(1)}, bf16[512,512]{1,0:T(8,128)(2,1)S(1)}, u32[]{:S(2)}, u32[]{:S(2)}) collective-permute-start(bf16[512,512]{1,0:T(8,128)(2,1)S(1)} %collective-permute-done.refs_2_), channel_id=1, source_target_pairs={{0,6},{1,7},{2,0},{3,1},{4,2},{5,3},{6,4},{7,5},{8,14},{9,15},{10,... | collective-permute-start | bytes 1572872 | tf_op jit(solution)/shard_map/ppermute | solution.py:150
  21.0 15.7 %collective-permute-start.5 = (bf16[512,512]{1,0:T(8,128)(2,1)S(1)}, bf16[512,512]{1,0:T(8,128)(2,1)S(1)}, u32[]{:S(2)}, u32[]{:S(2)}) collective-permute-start(bf16[512,512]{1,0:T(8,128)(2,1)S(1)} %collective-permute-done.refs_2_), channel_id=1, source_target_pairs={{0,1},{1,0},{2,3},{3,2},{4,5},{5,4},{6,7},{7,6},{8,9},{9,8},{10,11... | collective-permute-start | bytes 1572872 | tf_op jit(solution)/shard_map/ppermute | solution.py:155
  22.1 14.9 %collective-permute-start.6 = (bf16[512,512]{1,0:T(8,128)(2,1)S(1)}, bf16[512,512]{1,0:T(8,128)(2,1)S(1)}, u32[]{:S(2)}, u32[]{:S(2)}) collective-permute-start(bf16[512,512]{1,0:T(8,128)(2,1)S(1)} %collective-permute-done.1.refs_3_), channel_id=1, source_target_pairs={{0,2},{1,3},{2,4},{3,5},{4,6},{5,7},{6,0},{7,1},{8,10},{9,11},{10,... | collective-permute-start | bytes 1572872 | tf_op jit(solution)/shard_map/ppermute | solution.py:150
  23.4 26.4 %all-to-all-start.1 = ((bf16[16,32,512]{2,1,0:T(8,128)(2,1)}), bf16[16,32,512]{2,1,0:T(8,128)(2,1)}, u32[]{:S(2)}, u32[]{:S(2)}) async-start(bf16[16,32,512]{2,1,0:T(8,128)(2,1)} %bitcast.3), calls=%async_computation.1 | async-start | bytes 1048576 | tf_op jit(solution)/shard_map/all_to_all | solution.py:394
  29.9 1.0 copy-start.5
  31.0 9.5 %copy-start = (bf16[4096,3,512]{2,0,1:T(8,128)(2,1)S(1)}, bf16[4096,3,512]{2,0,1:T(8,128)(2,1)}, u32[]{:S(2)}) copy-start(bf16[4096,3,512]{2,0,1:T(8,128)(2,1)} %param.12) | copy-start | bytes 37748740
  37.1 9.4 %collective-permute-start.7 = (bf16[256,512]{1,0:T(8,128)(2,1)S(1)}, bf16[256,512]{1,0:T(8,128)(2,1)S(1)}, u32[]{:S(2)}, u32[]{:S(2)}) collective-permute-start(bf16[256,512]{1,0:T(8,128)(2,1)S(1)} %slice.22), channel_id=1, source_target_pairs={{0,2},{1,3},{2,4},{3,5},{4,6},{5,7},{6,0},{7,1},{8,10},{9,11},{10,... | collective-permute-start | bytes 786440 | tf_op jit(solution)/shard_map/ppermute | solution.py:150
  38.8 7.7 %copy-start.6 = (f32[3,3,512]{2,1,0:T(4,128)S(1)}, f32[3,3,512]{2,1,0:T(4,128)}, u32[]{:S(2)}) copy-start(f32[3,3,512]{2,1,0:T(4,128)} %taps.1) | copy-start | bytes 55300
  38.8 7.7 %collective-permute-start.8 = (bf16[256,512]{1,0:T(8,128)(2,1)S(1)}, bf16[256,512]{1,0:T(8,128)(2,1)S(1)}, u32[]{:S(2)}, u32[]{:S(2)}) collective-permute-start(bf16[256,512]{1,0:T(8,128)(2,1)S(1)} %slice.23), channel_id=1, source_target_pairs={{0,6},{1,7},{2,0},{3,1},{4,2},{5,3},{6,4},{7,5},{8,14},{9,15},{10,... | collective-permute-start | bytes 786440 | tf_op jit(solution)/shard_map/ppermute | solution.py:150
  43.1 2.2 %collective-permute-start.9 = (f32[3,16,512]{2,1,0:T(8,128)S(1)}, f32[3,16,512]{2,1,0:T(8,128)S(1)}, u32[]{:S(2)}, u32[]{:S(2)}) collective-permute-start(f32[3,16,512]{2,1,0:T(8,128)S(1)} %get-tuple-element.42), channel_id=1, source_target_pairs={{0,8},{8,16},{16,24},{24,32},{32,40},{40,48},{48,56},{56,64},{64,7... | collective-permute-start | bytes 294920 | tf_op jit(solution)/shard_map/ppermute | solution.py:145
  46.6 11.6 %copy-start.8 = (bf16[256,256]{1,0:T(8,128)(2,1)S(1)}, bf16[256,256]{1,0:T(8,128)(2,1)}, u32[]{:S(2)}) copy-start(bf16[256,256]{1,0:T(8,128)(2,1)} %constant.12.clone.forward) | copy-start | bytes 393220
  46.6 11.6 %copy-start.10 = (f32[2,72,128]{2,1,0:T(8,128)S(1)}, f32[2,72,128]{2,1,0:T(8,128)}, u32[]{:S(2)}) copy-start(f32[2,72,128]{2,1,0:T(8,128)} %constant.11.clone.tw) | copy-start | bytes 221188
  46.6 11.6 %copy-start.11 = (bf16[144,64]{1,0:T(8,128)(2,1)S(1)}, bf16[144,64]{1,0:T(8,128)(2,1)}, u32[]{:S(2)}) copy-start(bf16[144,64]{1,0:T(8,128)(2,1)} %constant.10.clone.first) | copy-start | bytes 55300
  49.8 19.2 %all-to-all-start = ((bf16[16,32,512]{2,1,0:T(8,128)(2,1)}), bf16[16,32,512]{2,1,0:T(8,128)(2,1)S(1)}, u32[]{:S(2)}, u32[]{:S(2)}) async-start(bf16[16,32,512]{2,1,0:T(8,128)(2,1)} %bitcast.15), calls=%async_computation | async-start | bytes 1048576 | tf_op jit(solution)/shard_map/all_to_all | solution.py:403
  58.1 10.8 %copy-start.9 = (bf16[256,256]{1,0:T(8,128)(2,1)S(1)}, bf16[256,256]{1,0:T(8,128)(2,1)}, u32[]{:S(2)}) copy-start(bf16[256,256]{1,0:T(8,128)(2,1)} %constant.13.clone.backward) | copy-start | bytes 393220
  58.2 10.8 %copy-start.12 = (bf16[64,144]{1,0:T(8,128)(2,1)S(1)}, bf16[64,144]{1,0:T(8,128)(2,1)}, u32[]{:S(2)}) copy-start(bf16[64,144]{1,0:T(8,128)(2,1)} %constant.14.clone.last) | copy-start | bytes 55300
  69.0 16.6 %copy-start.1 = (bf16[512,4096]{1,0:T(8,128)(2,1)S(1)}, bf16[512,4096]{1,0:T(8,128)(2,1)}, u32[]{:S(2)}) copy-start(bf16[512,4096]{1,0:T(8,128)(2,1)} %weight.5) | copy-start | bytes 12582916
  69.0 16.6 %copy-start.2 = (f32[512,512]{1,0:T(8,128)S(1)}, f32[512,512]{1,0:T(8,128)}, u32[]{:S(2)}) copy-start(f32[512,512]{1,0:T(8,128)} %get-tuple-element.45.signal) | copy-start | bytes 3145732
  69.0 16.6 %copy-start.3 = (f32[512,512]{1,0:T(8,128)S(1)}, f32[512,512]{1,0:T(8,128)}, u32[]{:S(2)}) copy-start(f32[512,512]{1,0:T(8,128)} %get-tuple-element.46.gate_out) | copy-start | bytes 3145732
  69.0 16.6 %copy-start.7 = (f32[512]{0:T(512)S(1)}, f32[512]{0:T(512)}, u32[]{:S(2)}) copy-start(f32[512]{0:T(512)} %param.15) | copy-start | bytes 6148
  86.5 8.8 %collective-permute-start.12 = (bf16[256,512]{1,0:T(8,128)(2,1)S(1)}, bf16[256,512]{1,0:T(8,128)(2,1)S(1)}, u32[]{:S(2)}, u32[]{:S(2)}) collective-permute-start(bf16[256,512]{1,0:T(8,128)(2,1)S(1)} %get-tuple-element.53), channel_id=1, source_target_pairs={{0,2},{1,3},{2,4},{3,5},{4,6},{5,7},{6,0},{7,1},{8,10},{9,11},{10,... | collective-permute-start | bytes 786440 | tf_op jit(solution)/shard_map/ppermute | solution.py:150
  87.3 10.4 %collective-permute-start.15 = (bf16[256,512]{1,0:T(8,128)(2,1)S(1)}, bf16[256,512]{1,0:T(8,128)(2,1)S(1)}, u32[]{:S(2)}, u32[]{:S(2)}) collective-permute-start(bf16[256,512]{1,0:T(8,128)(2,1)S(1)} %get-tuple-element.59), channel_id=1, source_target_pairs={{0,1},{1,0},{2,3},{3,2},{4,5},{5,4},{6,7},{7,6},{8,9},{9,8},{10,11... | collective-permute-start | bytes 786440 | tf_op jit(solution)/shard_map/ppermute | solution.py:155
  91.0 12.9 %collective-permute-start.10 = (bf16[512,512]{1,0:T(8,128)(2,1)S(1)}, bf16[512,512]{1,0:T(8,128)(2,1)S(1)}, u32[]{:S(2)}, u32[]{:S(2)}) collective-permute-start(bf16[512,512]{1,0:T(8,128)(2,1)S(1)} %get-tuple-element.49), channel_id=1, source_target_pairs={{0,6},{1,7},{2,0},{3,1},{4,2},{5,3},{6,4},{7,5},{8,14},{9,15},{10,... | collective-permute-start | bytes 1572872 | tf_op jit(solution)/shard_map/ppermute | solution.py:150
  95.4 13.8 %collective-permute-start.13 = (bf16[512,512]{1,0:T(8,128)(2,1)S(1)}, bf16[512,512]{1,0:T(8,128)(2,1)S(1)}, u32[]{:S(2)}, u32[]{:S(2)}) collective-permute-start(bf16[512,512]{1,0:T(8,128)(2,1)S(1)} %pad_maximum_fusion), channel_id=1, source_target_pairs={{0,1},{1,0},{2,3},{3,2},{4,5},{5,4},{6,7},{7,6},{8,9},{9,8},{10,11... | collective-permute-start | bytes 1572872 | tf_op jit(solution)/shard_map/ppermute | solution.py:155
  97.9 13.2 %collective-permute-start.16 = (bf16[512,512]{1,0:T(8,128)(2,1)S(1)}, bf16[512,512]{1,0:T(8,128)(2,1)S(1)}, u32[]{:S(2)}, u32[]{:S(2)}) collective-permute-start(bf16[512,512]{1,0:T(8,128)(2,1)S(1)} %pad_maximum_fusion.1), channel_id=1, source_target_pairs={{0,2},{1,3},{2,4},{3,5},{4,6},{5,7},{6,0},{7,1},{8,10},{9,11},{10,... | collective-permute-start | bytes 1572872 | tf_op jit(solution)/shard_map/ppermute | solution.py:150
  103.8 12.9 %collective-permute-start.11 = (bf16[512,512]{1,0:T(8,128)(2,1)S(1)}, bf16[512,512]{1,0:T(8,128)(2,1)S(1)}, u32[]{:S(2)}, u32[]{:S(2)}) collective-permute-start(bf16[512,512]{1,0:T(8,128)(2,1)S(1)} %get-tuple-element.51), channel_id=1, source_target_pairs={{0,6},{1,7},{2,0},{3,1},{4,2},{5,3},{6,4},{7,5},{8,14},{9,15},{10,... | collective-permute-start | bytes 1572872 | tf_op jit(solution)/shard_map/ppermute | solution.py:150
  111.3 12.3 %collective-permute-start.17 = (bf16[512,512]{1,0:T(8,128)(2,1)S(1)}, bf16[512,512]{1,0:T(8,128)(2,1)S(1)}, u32[]{:S(2)}, u32[]{:S(2)}) collective-permute-start(bf16[512,512]{1,0:T(8,128)(2,1)S(1)} %add_convert_fusion.1), channel_id=1, source_target_pairs={{0,2},{1,3},{2,4},{3,5},{4,6},{5,7},{6,0},{7,1},{8,10},{9,11},{10,... | collective-permute-start | bytes 1572872 | tf_op jit(solution)/shard_map/ppermute | solution.py:150
  111.4 12.6 %collective-permute-start.14 = (bf16[512,512]{1,0:T(8,128)(2,1)S(1)}, bf16[512,512]{1,0:T(8,128)(2,1)S(1)}, u32[]{:S(2)}, u32[]{:S(2)}) collective-permute-start(bf16[512,512]{1,0:T(8,128)(2,1)S(1)} %add_convert_fusion.2), channel_id=1, source_target_pairs={{0,1},{1,0},{2,3},{3,2},{4,5},{5,4},{6,7},{7,6},{8,9},{9,8},{10,11... | collective-permute-start | bytes 1572872 | tf_op jit(solution)/shard_map/ppermute | solution.py:155

commit v6 on v5

--- a/solution.py
+++ b/solution.py
@@ -407,12 +407,14 @@
     gated, to_far, to_up = gate_and_project(conv, signal, gate_out, skip, (2, 1), (half, half), out_weight, cols)
     to_far, to_up = cross(to_far), ring(to_up, 1)
     down_side, up_side, far = project_out(gated, [(-1, 1), (1, 1), (2, 0)], (1, 1, 1), out_weight, cols)
+    to_up, down_side = together((to_up, down_side))
     down_side = ring(down_side, -1)
     up, down, side, own = project_out(gated, [(1, 0), (-1, 0), (0, 1), (0, 0)], (1, 1, 1, 1), out_weight, cols)
     up_side = cross(jnp.concatenate([up_side[:half], added(up_side[half:], to_up)], axis=0))
     far = ring(jnp.concatenate([added(far[:half], to_far), far[half:]], axis=0), 1)
     down_side, down = together((down_side, down))
-    up_side, side = together((up_side, added(side, down_side)))
+    up_side, own = together((up_side, own))
+    side = added(side, down_side)
     side = cross(side)
     up = added(up, far, up_side)
     up, down = ring(up, 1), ring(down, -1)

time: 126 us -> 126 us (level)
    ppermute x5, waiting for transfers between devices: 2.74 us -> 8.12 us  [cross(): return lax.ppermute(array, 'chan', [(i, i ^ 1) for i in range(count)])]
    ppermute x11, waiting for transfers between devices: 22.3 us -> 17.2 us  [ring(): lax.ppermute(array, 'chan', [(i, (i + 2 * by) % count) for i in range(cou...]
    ppermute x11, starting transfers between devices: 15.2 us -> 13.4 us  [ring(): lax.ppermute(array, 'chan', [(i, (i + 2 * by) % count) for i in range(cou...]
    ppermute x5, starting transfers between devices: 9.9 us -> 11.2 us  [cross(): return lax.ppermute(array, 'chan', [(i, i ^ 1) for i in range(count)])]
  transfers between devices with their start and end apart: 20 -> 20, of which waited for: 14 -> 12; matrix products, arithmetic and copies ran while one was open for 1% -> 1% of each run, Pallas kernels for 16% -> 16%
where the time goes in v6:
time: 126 us; the launch traced here: 125 us
  starting transfers between devices  43.3 us (34%)
  waiting for transfers between devices  39.3 us (31%)
  Pallas kernels  23.7 us (19%)
  blocking collectives  13.5 us (11%)
  local copies, waits for them, and re-layouts  3.17 us (3%)
  other arithmetic  1.6 us (1%)
    ppermute x11, waiting for transfers between devices, ring(): lax.ppermute(array, 'chan', [(i, (i + 2 * by) % count) for i in range(cou...  17.2 us
    all_to_all x1, blocking collectives, shards(): conv = lax.all_to_all(conv, 'seq', 0, 0, tiled=True)  13.5 us
    ppermute x11, starting transfers between devices, ring(): lax.ppermute(array, 'chan', [(i, (i + 2 * by) % count) for i in range(cou...  13.4 us
    ppermute x5, starting transfers between devices, cross(): return lax.ppermute(array, 'chan', [(i, i ^ 1) for i in range(count)])  11.2 us
    all_to_all x1, starting transfers between devices, shards(): lax.all_to_all(signal_t, 'seq', 0, 0, tiled=True)  8.28 us
    ppermute x5, waiting for transfers between devices, cross(): return lax.ppermute(array, 'chan', [(i, i ^ 1) for i in range(count)])  8.12 us
    all_to_all x1, waiting for transfers between devices, shards(): lax.all_to_all(signal_t, 'seq', 0, 0, tiled=True)  7.21 us
    all_to_all x1, starting transfers between devices, shards(): fil = lax.all_to_all(fil, 'seq', 0, 0, tiled=True)  6.5 us
  transfers between devices with their start and end apart: 20, of which 12 were waited for; matrix products, arithmetic and copies ran while one was open for 1% of the time, Pallas kernels for 16%

profile of v6, /device:TPU:0, one launch (start us, length us, event | category | flops | bytes accessed | tf_op | source)
XLA Modules:
  0.0 124.8 jit_solution(3724513164739569924)
XLA Ops:
  0.0 3.1 %collective-permute-start = (bf16[512,512]{1,0:T(8,128)(2,1)}, bf16[512,512]{1,0:T(8,128)(2,1)S(1)}, u32[]{:S(2)}, u32[]{:S(2)}) collective-permute-start(bf16[512,512]{1,0:T(8,128)(2,1)} %refs_0_.1), channel_id=1, source_target_pairs={{0,6},{1,7},{2,0},{3,1},{4,2},{5,3},{6,4},{7,5},{8,14},{9,15},{10,... | collective-permute-start | bytes 1572872 | tf_op jit(solution)/shard_map/ppermute | solution.py:150
  3.1 3.0 %collective-permute-start.1 = (bf16[512,512]{1,0:T(8,128)(2,1)}, bf16[512,512]{1,0:T(8,128)(2,1)S(1)}, u32[]{:S(2)}, u32[]{:S(2)}) collective-permute-start(bf16[512,512]{1,0:T(8,128)(2,1)} %refs_0_.1), channel_id=1, source_target_pairs={{0,1},{1,0},{2,3},{3,2},{4,5},{5,4},{6,7},{7,6},{8,9},{9,8},{10,11... | collective-permute-start | bytes 1572872 | tf_op jit(solution)/shard_map/ppermute | solution.py:155
  6.1 0.8 slice.21
  6.9 2.6 %collective-permute-start.3 = (bf16[16,512]{1,0:T(8,128)(2,1)S(1)}, bf16[16,512]{1,0:T(8,128)(2,1)S(1)}, u32[]{:S(2)}, u32[]{:S(2)}) collective-permute-start(bf16[16,512]{1,0:T(8,128)(2,1)S(1)} %slice.21), channel_id=1, source_target_pairs={{0,13},{1,12},{2,15},{3,14},{4,9},{5,8},{6,11},{7,10},{8,21},{9,20... | collective-permute-start | bytes 49160 | tf_op jit(solution)/shard_map/ppermute | solution.py:161
  9.5 1.2 copy-done.4
  10.8 1.0 transposed.1
  11.7 5.8 %collective-permute-done.3.halo = bf16[16,512]{1,0:T(8,128)(2,1)S(1)} collective-permute-done((bf16[16,512]{1,0:T(8,128)(2,1)S(1)}, bf16[16,512]{1,0:T(8,128)(2,1)S(1)}, u32[]{:S(2)}, u32[]{:S(2)}) %collective-permute-start.3) | collective-permute-done | bytes 16416 | tf_op jit(solution)/shard_map/ppermute | solution.py:161
  17.6 0.8 collective-permute-done.1.refs_3_
  18.4 2.6 %collective-permute-done.2.refs_1_ = bf16[512,512]{1,0:T(8,128)(2,1)S(1)} collective-permute-done((bf16[512,512]{1,0:T(8,128)(2,1)}, bf16[512,512]{1,0:T(8,128)(2,1)S(1)}, u32[]{:S(2)}, u32[]{:S(2)}) %collective-permute-start.2) | collective-permute-done | bytes 524320 | tf_op jit(solution)/shard_map/ppermute | solution.py:150
  21.0 1.1 collective-permute-start.5
  22.1 1.3 %collective-permute-start.6 = (bf16[512,512]{1,0:T(8,128)(2,1)S(1)}, bf16[512,512]{1,0:T(8,128)(2,1)S(1)}, u32[]{:S(2)}, u32[]{:S(2)}) collective-permute-start(bf16[512,512]{1,0:T(8,128)(2,1)S(1)} %collective-permute-done.1.refs_3_), channel_id=1, source_target_pairs={{0,2},{1,3},{2,4},{3,5},{4,6},{5,7},{6,0},{7,1},{8,10},{9,11},{10,... | collective-permute-start | bytes 1572872 | tf_op jit(solution)/shard_map/ppermute | solution.py:150
  23.4 6.5 %all-to-all-start.1 = ((bf16[16,32,512]{2,1,0:T(8,128)(2,1)}), bf16[16,32,512]{2,1,0:T(8,128)(2,1)}, u32[]{:S(2)}, u32[]{:S(2)}) async-start(bf16[16,32,512]{2,1,0:T(8,128)(2,1)} %bitcast.3), calls=%async_computation.1 | async-start | bytes 1048576 | tf_op jit(solution)/shard_map/all_to_all | solution.py:394
  29.9 1.0 copy-done.5
  31.0 5.6 %first_round.1.refs_0_ = f32[3,512,512]{2,1,0:T(8,128)S(1)} custom-call(bf16[512,512]{1,0:T(8,128)(2,1)S(1)} %copy-done.5, bf16[512,512]{1,0:T(8,128)(2,1)S(1)} %collective-permute-done.2.refs_1_, bf16[512,512]{1,0:T(8,128)(2,1)S(1)} %collective-permute-done.refs_2_, bf16[512,512]{1,0:T(8,128)(2,1)S(1)} %collective-permute-done.1.refs_3_, ...), custom_call_target="tpu_custom_call" | custom-call | flops 3221225472 | bytes 6291456 | tf_op jit(solution)/shard_map/first_round/pallas_call | solution.py:256
  36.7 0.4 collective-permute-done.6.refs_1_
  37.1 1.7 %collective-permute-start.7 = (bf16[256,512]{1,0:T(8,128)(2,1)S(1)}, bf16[256,512]{1,0:T(8,128)(2,1)S(1)}, u32[]{:S(2)}, u32[]{:S(2)}) collective-permute-start(bf16[256,512]{1,0:T(8,128)(2,1)S(1)} %slice.22), channel_id=1, source_target_pairs={{0,2},{1,3},{2,4},{3,5},{4,6},{5,7},{6,0},{7,1},{8,10},{9,11},{10,... | collective-permute-start | bytes 786440 | tf_op jit(solution)/shard_map/ppermute | solution.py:150
  38.8 1.7 %collective-permute-start.8 = (bf16[256,512]{1,0:T(8,128)(2,1)S(1)}, bf16[256,512]{1,0:T(8,128)(2,1)S(1)}, u32[]{:S(2)}, u32[]{:S(2)}) collective-permute-start(bf16[256,512]{1,0:T(8,128)(2,1)S(1)} %slice.23), channel_id=1, source_target_pairs={{0,6},{1,7},{2,0},{3,1},{4,2},{5,3},{6,4},{7,5},{8,14},{9,15},{10,... | collective-permute-start | bytes 786440 | tf_op jit(solution)/shard_map/ppermute | solution.py:150
  40.5 2.6 %project_round.1 = (f32[3,512,512]{2,1,0:T(8,128)S(1)}, f32[3,16,512]{2,1,0:T(8,128)S(1)}) custom-call(f32[3,512,512]{2,1,0:T(8,128)S(1)} %first_round.1.refs_0_, bf16[512,512]{1,0:T(8,128)(2,1)S(1)} %collective-permute-done.6.refs_1_, bf16[512,512]{1,0:T(8,128)(2,1)S(1)} %collective-permute-done.5.refs_2_, ...), custom_call_target="tpu_custom_call" | custom-call | flops 2415919104 | bytes 4718592 | tf_op jit(solution)/shard_map/project_round/pallas_call | solution.py:220
  43.1 1.3 %collective-permute-start.9 = (f32[3,16,512]{2,1,0:T(8,128)S(1)}, f32[3,16,512]{2,1,0:T(8,128)S(1)}, u32[]{:S(2)}, u32[]{:S(2)}) collective-permute-start(f32[3,16,512]{2,1,0:T(8,128)S(1)} %get-tuple-element.44), channel_id=1, source_target_pairs={{0,8},{8,16},{16,24},{24,32},{32,40},{40,48},{48,56},{56,64},{64,7... | collective-permute-start | bytes 294920 | tf_op jit(solution)/shard_map/ppermute | solution.py:145
  44.4 0.9 collective-permute-done.9.halo_acc
  45.4 1.2 collective-permute-done.7.lo
  46.6 0.0 copy-start.10
  46.6 3.2 %signal_of.1 = (bf16[512,512]{1,0:T(8,128)(2,1)}, f32[512,512]{1,0:T(8,128)}, f32[512,512]{1,0:T(8,128)}) custom-call(f32[3,512,512]{2,1,0:T(8,128)S(1)} %get-tuple-element.42.acc, bf16[256,512]{1,0:T(8,128)(2,1)S(1)} %collective-permute-done.7.lo, bf16[256,512]{1,0:T(8,128)(2,1)S(1)} %collective-permute-done.8.hi, ...), custom_call_target="tpu_custom_call" | custom-call | flops 805306368 | bytes 4194304 | tf_op jit(solution)/shard_map/signal_of/pallas_call | solution.py:300
  49.8 8.3 %all-to-all-start = ((bf16[16,32,512]{2,1,0:T(8,128)(2,1)}), bf16[16,32,512]{2,1,0:T(8,128)(2,1)S(1)}, u32[]{:S(2)}, u32[]{:S(2)}) async-start(bf16[16,32,512]{2,1,0:T(8,128)(2,1)} %bitcast.15), calls=%async_computation | async-start | bytes 1048576 | tf_op jit(solution)/shard_map/all_to_all | solution.py:403
  58.2 3.6 %filter_spectrum.1.h_ref = bf16[1,2304,256]{2,1,0:T(8,128)(2,1)} custom-call(bf16[512,512]{1,0:T(8,128)(2,1)} %bitcast.4.x_ref, bf16[144,64]{1,0:T(8,128)(2,1)S(1)} %copy-done.11, f32[2,72,128]{2,1,0:T(8,128)S(1)} %copy-done.10, bf16[256,256]{1,0:T(8,128)(2,1)S(1)} %copy-done.8), custom_call_target="tpu_custom_call" | custom-call | flops 4000000000 | bytes 4000000 | tf_op jit(solution)/shard_map/filter_spectrum/pallas_call | solution.py:111
  61.8 7.2 %all-to-all-done = bf16[16,32,512]{2,1,0:T(8,128)(2,1)S(1)} async-done(((bf16[16,32,512]{2,1,0:T(8,128)(2,1)}), bf16[16,32,512]{2,1,0:T(8,128)(2,1)S(1)}, u32[]{:S(2)}, u32[]{:S(2)}) %all-to-all-start) | async-done | bytes 524320 | tf_op jit(solution)/shard_map/all_to_all | solution.py:403
  69.0 3.1 %convolve.1 = bf16[512,512]{1,0:T(8,128)(2,1)S(1)} custom-call(bf16[512,512]{1,0:T(8,128)(2,1)S(1)} %bitcast.12, bf16[1,2304,256]{2,1,0:T(8,128)(2,1)} %filter_spectrum.1.h_ref, bf16[144,64]{1,0:T(8,128)(2,1)S(1)} %copy-done.11, f32[2,72,128]{2,1,0:T(8,128)S(1)} %copy-done.10, bf16[256,256]{1,0:T(8,128)(2,1)S(1)} %copy-done.8, ...), custom_call_target="tpu_custom_call" | custom-call | flops 5000000000 | bytes 4000000 | tf_op jit(solution)/shard_map/convolve/pallas_call | solution.py:130
  72.1 13.5 %all_to_all.33 = bf16[16,32,512]{2,1,0:T(8,128)(2,1)S(1)} all-to-all(bf16[16,32,512]{2,1,0:T(8,128)(2,1)S(1)} %bitcast.13), channel_id=1, replica_groups=mesh['seq'=16,'chan'=8] {'seq'}, dimensions={0} | all-to-all | bytes 1048576 | tf_op jit(solution)/shard_map/all_to_all | solution.py:404
  85.6 0.9 gate_and_project.1
  86.5 0.8 collective-permute-start.10
  87.3 2.0 %collective-permute-start.15 = (bf16[256,512]{1,0:T(8,128)(2,1)S(1)}, bf16[256,512]{1,0:T(8,128)(2,1)S(1)}, u32[]{:S(2)}, u32[]{:S(2)}) collective-permute-start(bf16[256,512]{1,0:T(8,128)(2,1)S(1)} %get-tuple-element.63), channel_id=1, source_target_pairs={{0,1},{1,0},{2,3},{3,2},{4,5},{5,4},{6,7},{7,6},{8,9},{9,8},{10,11... | collective-permute-start | bytes 786440 | tf_op jit(solution)/shard_map/ppermute | solution.py:155
  89.4 1.6 %project_out.2 = (bf16[512,512]{1,0:T(8,128)(2,1)S(1)}, bf16[512,512]{1,0:T(8,128)(2,1)S(1)}, bf16[512,512]{1,0:T(8,128)(2,1)S(1)}) custom-call(bf16[512,512]{1,0:T(8,128)(2,1)S(1)} %get-tuple-element.49.g, bf16[512,4096]{1,0:T(8,128)(2,1)S(1)} %copy-done.1), custom_call_target="tpu_custom_call" | custom-call | flops 805306368 | bytes 3145728 | tf_op jit(solution)/shard_map/project_out/pallas_call | solution.py:366
  91.0 4.3 %collective-permute-done.10 = bf16[256,512]{1,0:T(8,128)(2,1)S(1)} collective-permute-done((bf16[256,512]{1,0:T(8,128)(2,1)S(1)}, bf16[256,512]{1,0:T(8,128)(2,1)S(1)}, u32[]{:S(2)}, u32[]{:S(2)}) %collective-permute-start.10) | collective-permute-done | bytes 262176 | tf_op jit(solution)/shard_map/ppermute | solution.py:150
  95.3 0.1 add_convert_fusion.4
  95.4 2.6 %collective-permute-start.11 = (bf16[512,512]{1,0:T(8,128)(2,1)S(1)}, bf16[512,512]{1,0:T(8,128)(2,1)S(1)}, u32[]{:S(2)}, u32[]{:S(2)}) collective-permute-start(bf16[512,512]{1,0:T(8,128)(2,1)S(1)} %pad_maximum_fusion), channel_id=1, source_target_pairs={{0,1},{1,0},{2,3},{3,2},{4,5},{5,4},{6,7},{7,6},{8,9},{9,8},{10,11... | collective-permute-start | bytes 1572872 | tf_op jit(solution)/shard_map/ppermute | solution.py:155
  98.0 0.1 add_convert_fusion.3
  98.2 1.8 %collective-permute-start.16 = (bf16[512,512]{1,0:T(8,128)(2,1)S(1)}, bf16[512,512]{1,0:T(8,128)(2,1)S(1)}, u32[]{:S(2)}, u32[]{:S(2)}) collective-permute-start(bf16[512,512]{1,0:T(8,128)(2,1)S(1)} %pad_maximum_fusion.1), channel_id=1, source_target_pairs={{0,2},{1,3},{2,4},{3,5},{4,6},{5,7},{6,0},{7,1},{8,10},{9,11},{10,... | collective-permute-start | bytes 1572872 | tf_op jit(solution)/shard_map/ppermute | solution.py:150
  100.0 2.1 %project_out.3 = (bf16[512,512]{1,0:T(8,128)(2,1)S(1)}, bf16[512,512]{1,0:T(8,128)(2,1)S(1)}, bf16[512,512]{1,0:T(8,128)(2,1)S(1)}, bf16[512,512]{1,0:T(8,128)(2,1)S(1)}) custom-call(bf16[512,512]{1,0:T(8,128)(2,1)S(1)} %get-tuple-element.49.g, bf16[512,4096]{1,0:T(8,128)(2,1)S(1)} %copy-done.1), custom_call_target="tpu_custom_call" | custom-call | flops 1073741824 | bytes 4194304 | tf_op jit(solution)/shard_map/project_out/pallas_call | solution.py:366
  102.1 5.5 %collective-permute-done.12 = bf16[512,512]{1,0:T(8,128)(2,1)S(1)} collective-permute-done((bf16[512,512]{1,0:T(8,128)(2,1)S(1)}, bf16[512,512]{1,0:T(8,128)(2,1)S(1)}, u32[]{:S(2)}, u32[]{:S(2)}) %collective-permute-start.12) | collective-permute-done | bytes 524320 | tf_op jit(solution)/shard_map/ppermute | solution.py:150
  107.5 0.1 add_convert_fusion.2
  107.7 2.3 %collective-permute-start.14 = (bf16[512,512]{1,0:T(8,128)(2,1)S(1)}, bf16[512,512]{1,0:T(8,128)(2,1)S(1)}, u32[]{:S(2)}, u32[]{:S(2)}) collective-permute-start(bf16[512,512]{1,0:T(8,128)(2,1)S(1)} %add_convert_fusion.2), channel_id=1, source_target_pairs={{0,1},{1,0},{2,3},{3,2},{4,5},{5,4},{6,7},{7,6},{8,9},{9,8},{10,11... | collective-permute-start | bytes 1572872 | tf_op jit(solution)/shard_map/ppermute | solution.py:155
  110.0 1.5 %collective-permute-start.13 = (bf16[512,512]{1,0:T(8,128)(2,1)S(1)}, bf16[512,512]{1,0:T(8,128)(2,1)S(1)}, u32[]{:S(2)}, u32[]{:S(2)}) collective-permute-start(bf16[512,512]{1,0:T(8,128)(2,1)S(1)} %get-tuple-element.58), channel_id=1, source_target_pairs={{0,6},{1,7},{2,0},{3,1},{4,2},{5,3},{6,4},{7,5},{8,14},{9,15},{10,... | collective-permute-start | bytes 1572872 | tf_op jit(solution)/shard_map/ppermute | solution.py:150
  111.5 0.2 add_convert_fusion.1
  111.7 1.5 %collective-permute-start.17 = (bf16[512,512]{1,0:T(8,128)(2,1)S(1)}, bf16[512,512]{1,0:T(8,128)(2,1)S(1)}, u32[]{:S(2)}, u32[]{:S(2)}) collective-permute-start(bf16[512,512]{1,0:T(8,128)(2,1)S(1)} %add_convert_fusion.1), channel_id=1, source_target_pairs={{0,2},{1,3},{2,4},{3,5},{4,6},{5,7},{6,0},{7,1},{8,10},{9,11},{10,... | collective-permute-start | bytes 1572872 | tf_op jit(solution)/shard_map/ppermute | solution.py:150
  113.3 7.3 %collective-permute-done.14 = bf16[512,512]{1,0:T(8,128)(2,1)S(1)} collective-permute-done((bf16[512,512]{1,0:T(8,128)(2,1)S(1)}, bf16[512,512]{1,0:T(8,128)(2,1)S(1)}, u32[]{:S(2)}, u32[]{:S(2)}) %collective-permute-start.14) | collective-permute-done | bytes 524320 | tf_op jit(solution)/shard_map/ppermute | solution.py:155
  120.6 0.5 collective-permute-done.13
  121.1 2.7 %collective-permute-done.17 = bf16[512,512]{1,0:T(8,128)(2,1)S(1)} collective-permute-done((bf16[512,512]{1,0:T(8,128)(2,1)S(1)}, bf16[512,512]{1,0:T(8,128)(2,1)S(1)}, u32[]{:S(2)}, u32[]{:S(2)}) %collective-permute-start.17) | collective-permute-done | bytes 524320 | tf_op jit(solution)/shard_map/ppermute | solution.py:150
  123.8 1.1 add_convert_fusion
  (40 shorter events, 0.2 us)
Async XLA Ops:
  0.0 17.6 %collective-permute-start = (bf16[512,512]{1,0:T(8,128)(2,1)}, bf16[512,512]{1,0:T(8,128)(2,1)S(1)}, u32[]{:S(2)}, u32[]{:S(2)}) collective-permute-start(bf16[512,512]{1,0:T(8,128)(2,1)} %refs_0_.1), channel_id=1, source_target_pairs={{0,6},{1,7},{2,0},{3,1},{4,2},{5,3},{6,4},{7,5},{8,14},{9,15},{10,... | collective-permute-start | bytes 1572872 | tf_op jit(solution)/shard_map/ppermute | solution.py:150
  3.1 15.3 %collective-permute-start.1 = (bf16[512,512]{1,0:T(8,128)(2,1)}, bf16[512,512]{1,0:T(8,128)(2,1)S(1)}, u32[]{:S(2)}, u32[]{:S(2)}) collective-permute-start(bf16[512,512]{1,0:T(8,128)(2,1)} %refs_0_.1), channel_id=1, source_target_pairs={{0,1},{1,0},{2,3},{3,2},{4,5},{5,4},{6,7},{7,6},{8,9},{9,8},{10,11... | collective-permute-start | bytes 1572872 | tf_op jit(solution)/shard_map/ppermute | solution.py:155
  6.1 14.9 %collective-permute-start.2 = (bf16[512,512]{1,0:T(8,128)(2,1)}, bf16[512,512]{1,0:T(8,128)(2,1)S(1)}, u32[]{:S(2)}, u32[]{:S(2)}) collective-permute-start(bf16[512,512]{1,0:T(8,128)(2,1)} %refs_0_.1), channel_id=1, source_target_pairs={{0,2},{1,3},{2,4},{3,5},{4,6},{5,7},{6,0},{7,1},{8,10},{9,11},{10,... | collective-permute-start | bytes 1572872 | tf_op jit(solution)/shard_map/ppermute | solution.py:150
  6.9 10.7 %collective-permute-start.3 = (bf16[16,512]{1,0:T(8,128)(2,1)S(1)}, bf16[16,512]{1,0:T(8,128)(2,1)S(1)}, u32[]{:S(2)}, u32[]{:S(2)}) collective-permute-start(bf16[16,512]{1,0:T(8,128)(2,1)S(1)} %slice.21), channel_id=1, source_target_pairs={{0,13},{1,12},{2,15},{3,14},{4,9},{5,8},{6,11},{7,10},{8,21},{9,20... | collective-permute-start | bytes 49160 | tf_op jit(solution)/shard_map/ppermute | solution.py:161
  9.5 1.2 copy-start.4
  21.0 15.6 %collective-permute-start.4 = (bf16[512,512]{1,0:T(8,128)(2,1)S(1)}, bf16[512,512]{1,0:T(8,128)(2,1)S(1)}, u32[]{:S(2)}, u32[]{:S(2)}) collective-permute-start(bf16[512,512]{1,0:T(8,128)(2,1)S(1)} %collective-permute-done.refs_2_), channel_id=1, source_target_pairs={{0,6},{1,7},{2,0},{3,1},{4,2},{5,3},{6,4},{7,5},{8,14},{9,15},{10,... | collective-permute-start | bytes 1572872 | tf_op jit(solution)/shard_map/ppermute | solution.py:150
  21.0 15.7 %collective-permute-start.5 = (bf16[512,512]{1,0:T(8,128)(2,1)S(1)}, bf16[512,512]{1,0:T(8,128)(2,1)S(1)}, u32[]{:S(2)}, u32[]{:S(2)}) collective-permute-start(bf16[512,512]{1,0:T(8,128)(2,1)S(1)} %collective-permute-done.refs_2_), channel_id=1, source_target_pairs={{0,1},{1,0},{2,3},{3,2},{4,5},{5,4},{6,7},{7,6},{8,9},{9,8},{10,11... | collective-permute-start | bytes 1572872 | tf_op jit(solution)/shard_map/ppermute | solution.py:155
  22.1 14.9 %collective-permute-start.6 = (bf16[512,512]{1,0:T(8,128)(2,1)S(1)}, bf16[512,512]{1,0:T(8,128)(2,1)S(1)}, u32[]{:S(2)}, u32[]{:S(2)}) collective-permute-start(bf16[512,512]{1,0:T(8,128)(2,1)S(1)} %collective-permute-done.1.refs_3_), channel_id=1, source_target_pairs={{0,2},{1,3},{2,4},{3,5},{4,6},{5,7},{6,0},{7,1},{8,10},{9,11},{10,... | collective-permute-start | bytes 1572872 | tf_op jit(solution)/shard_map/ppermute | solution.py:150
  23.4 26.4 %all-to-all-start.1 = ((bf16[16,32,512]{2,1,0:T(8,128)(2,1)}), bf16[16,32,512]{2,1,0:T(8,128)(2,1)}, u32[]{:S(2)}, u32[]{:S(2)}) async-start(bf16[16,32,512]{2,1,0:T(8,128)(2,1)} %bitcast.3), calls=%async_computation.1 | async-start | bytes 1048576 | tf_op jit(solution)/shard_map/all_to_all | solution.py:394
  29.9 1.0 copy-start.5
  31.0 9.5 %copy-start = (bf16[4096,3,512]{2,0,1:T(8,128)(2,1)S(1)}, bf16[4096,3,512]{2,0,1:T(8,128)(2,1)}, u32[]{:S(2)}) copy-start(bf16[4096,3,512]{2,0,1:T(8,128)(2,1)} %param.12) | copy-start | bytes 37748740
  37.1 9.4 %collective-permute-start.7 = (bf16[256,512]{1,0:T(8,128)(2,1)S(1)}, bf16[256,512]{1,0:T(8,128)(2,1)S(1)}, u32[]{:S(2)}, u32[]{:S(2)}) collective-permute-start(bf16[256,512]{1,0:T(8,128)(2,1)S(1)} %slice.22), channel_id=1, source_target_pairs={{0,2},{1,3},{2,4},{3,5},{4,6},{5,7},{6,0},{7,1},{8,10},{9,11},{10,... | collective-permute-start | bytes 786440 | tf_op jit(solution)/shard_map/ppermute | solution.py:150
  38.8 7.7 %copy-start.6 = (f32[3,3,512]{2,1,0:T(4,128)S(1)}, f32[3,3,512]{2,1,0:T(4,128)}, u32[]{:S(2)}) copy-start(f32[3,3,512]{2,1,0:T(4,128)} %taps.1) | copy-start | bytes 55300
  38.8 7.7 %collective-permute-start.8 = (bf16[256,512]{1,0:T(8,128)(2,1)S(1)}, bf16[256,512]{1,0:T(8,128)(2,1)S(1)}, u32[]{:S(2)}, u32[]{:S(2)}) collective-permute-start(bf16[256,512]{1,0:T(8,128)(2,1)S(1)} %slice.23), channel_id=1, source_target_pairs={{0,6},{1,7},{2,0},{3,1},{4,2},{5,3},{6,4},{7,5},{8,14},{9,15},{10,... | collective-permute-start | bytes 786440 | tf_op jit(solution)/shard_map/ppermute | solution.py:150
  43.1 2.2 %collective-permute-start.9 = (f32[3,16,512]{2,1,0:T(8,128)S(1)}, f32[3,16,512]{2,1,0:T(8,128)S(1)}, u32[]{:S(2)}, u32[]{:S(2)}) collective-permute-start(f32[3,16,512]{2,1,0:T(8,128)S(1)} %get-tuple-element.44), channel_id=1, source_target_pairs={{0,8},{8,16},{16,24},{24,32},{32,40},{40,48},{48,56},{56,64},{64,7... | collective-permute-start | bytes 294920 | tf_op jit(solution)/shard_map/ppermute | solution.py:145
  46.6 11.6 %copy-start.8 = (bf16[256,256]{1,0:T(8,128)(2,1)S(1)}, bf16[256,256]{1,0:T(8,128)(2,1)}, u32[]{:S(2)}) copy-start(bf16[256,256]{1,0:T(8,128)(2,1)} %constant.12.clone.forward) | copy-start | bytes 393220
  46.6 11.6 %copy-start.10 = (f32[2,72,128]{2,1,0:T(8,128)S(1)}, f32[2,72,128]{2,1,0:T(8,128)}, u32[]{:S(2)}) copy-start(f32[2,72,128]{2,1,0:T(8,128)} %constant.11.clone.tw) | copy-start | bytes 221188
  46.6 11.6 %copy-start.11 = (bf16[144,64]{1,0:T(8,128)(2,1)S(1)}, bf16[144,64]{1,0:T(8,128)(2,1)}, u32[]{:S(2)}) copy-start(bf16[144,64]{1,0:T(8,128)(2,1)} %constant.10.clone.first) | copy-start | bytes 55300
  49.8 19.2 %all-to-all-start = ((bf16[16,32,512]{2,1,0:T(8,128)(2,1)}), bf16[16,32,512]{2,1,0:T(8,128)(2,1)S(1)}, u32[]{:S(2)}, u32[]{:S(2)}) async-start(bf16[16,32,512]{2,1,0:T(8,128)(2,1)} %bitcast.15), calls=%async_computation | async-start | bytes 1048576 | tf_op jit(solution)/shard_map/all_to_all | solution.py:403
  58.1 10.8 %copy-start.9 = (bf16[256,256]{1,0:T(8,128)(2,1)S(1)}, bf16[256,256]{1,0:T(8,128)(2,1)}, u32[]{:S(2)}) copy-start(bf16[256,256]{1,0:T(8,128)(2,1)} %constant.13.clone.backward) | copy-start | bytes 393220
  58.2 10.8 %copy-start.12 = (bf16[64,144]{1,0:T(8,128)(2,1)S(1)}, bf16[64,144]{1,0:T(8,128)(2,1)}, u32[]{:S(2)}) copy-start(bf16[64,144]{1,0:T(8,128)(2,1)} %constant.14.clone.last) | copy-start | bytes 55300
  69.0 16.6 %copy-start.1 = (bf16[512,4096]{1,0:T(8,128)(2,1)S(1)}, bf16[512,4096]{1,0:T(8,128)(2,1)}, u32[]{:S(2)}) copy-start(bf16[512,4096]{1,0:T(8,128)(2,1)} %weight.5) | copy-start | bytes 12582916
  69.0 16.6 %copy-start.2 = (f32[512,512]{1,0:T(8,128)S(1)}, f32[512,512]{1,0:T(8,128)}, u32[]{:S(2)}) copy-start(f32[512,512]{1,0:T(8,128)} %get-tuple-element.47.signal) | copy-start | bytes 3145732
  69.0 16.6 %copy-start.3 = (f32[512,512]{1,0:T(8,128)S(1)}, f32[512,512]{1,0:T(8,128)}, u32[]{:S(2)}) copy-start(f32[512,512]{1,0:T(8,128)} %get-tuple-element.48.gate_out) | copy-start | bytes 3145732
  69.0 16.6 %copy-start.7 = (f32[512]{0:T(512)S(1)}, f32[512]{0:T(512)}, u32[]{:S(2)}) copy-start(f32[512]{0:T(512)} %param.15) | copy-start | bytes 6148
  86.5 8.8 %collective-permute-start.10 = (bf16[256,512]{1,0:T(8,128)(2,1)S(1)}, bf16[256,512]{1,0:T(8,128)(2,1)S(1)}, u32[]{:S(2)}, u32[]{:S(2)}) collective-permute-start(bf16[256,512]{1,0:T(8,128)(2,1)S(1)} %get-tuple-element.51), channel_id=1, source_target_pairs={{0,2},{1,3},{2,4},{3,5},{4,6},{5,7},{6,0},{7,1},{8,10},{9,11},{10,... | collective-permute-start | bytes 786440 | tf_op jit(solution)/shard_map/ppermute | solution.py:150
  87.3 10.7 %collective-permute-start.15 = (bf16[256,512]{1,0:T(8,128)(2,1)S(1)}, bf16[256,512]{1,0:T(8,128)(2,1)S(1)}, u32[]{:S(2)}, u32[]{:S(2)}) collective-permute-start(bf16[256,512]{1,0:T(8,128)(2,1)S(1)} %get-tuple-element.63), channel_id=1, source_target_pairs={{0,1},{1,0},{2,3},{3,2},{4,5},{5,4},{6,7},{7,6},{8,9},{9,8},{10,11... | collective-permute-start | bytes 786440 | tf_op jit(solution)/shard_map/ppermute | solution.py:155
  95.3 12.2 %collective-permute-start.12 = (bf16[512,512]{1,0:T(8,128)(2,1)S(1)}, bf16[512,512]{1,0:T(8,128)(2,1)S(1)}, u32[]{:S(2)}, u32[]{:S(2)}) collective-permute-start(bf16[512,512]{1,0:T(8,128)(2,1)S(1)} %get-tuple-element.56), channel_id=1, source_target_pairs={{0,6},{1,7},{2,0},{3,1},{4,2},{5,3},{6,4},{7,5},{8,14},{9,15},{10,... | collective-permute-start | bytes 1572872 | tf_op jit(solution)/shard_map/ppermute | solution.py:150
  95.4 16.1 %collective-permute-start.11 = (bf16[512,512]{1,0:T(8,128)(2,1)S(1)}, bf16[512,512]{1,0:T(8,128)(2,1)S(1)}, u32[]{:S(2)}, u32[]{:S(2)}) collective-permute-start(bf16[512,512]{1,0:T(8,128)(2,1)S(1)} %pad_maximum_fusion), channel_id=1, source_target_pairs={{0,1},{1,0},{2,3},{3,2},{4,5},{5,4},{6,7},{7,6},{8,9},{9,8},{10,11... | collective-permute-start | bytes 1572872 | tf_op jit(solution)/shard_map/ppermute | solution.py:155
  98.2 13.4 %collective-permute-start.16 = (bf16[512,512]{1,0:T(8,128)(2,1)S(1)}, bf16[512,512]{1,0:T(8,128)(2,1)S(1)}, u32[]{:S(2)}, u32[]{:S(2)}) collective-permute-start(bf16[512,512]{1,0:T(8,128)(2,1)S(1)} %pad_maximum_fusion.1), channel_id=1, source_target_pairs={{0,2},{1,3},{2,4},{3,5},{4,6},{5,7},{6,0},{7,1},{8,10},{9,11},{10,... | collective-permute-start | bytes 1572872 | tf_op jit(solution)/shard_map/ppermute | solution.py:150
  107.7 12.9 %collective-permute-start.14 = (bf16[512,512]{1,0:T(8,128)(2,1)S(1)}, bf16[512,512]{1,0:T(8,128)(2,1)S(1)}, u32[]{:S(2)}, u32[]{:S(2)}) collective-permute-start(bf16[512,512]{1,0:T(8,128)(2,1)S(1)} %add_convert_fusion.2), channel_id=1, source_target_pairs={{0,1},{1,0},{2,3},{3,2},{4,5},{5,4},{6,7},{7,6},{8,9},{9,8},{10,11... | collective-permute-start | bytes 1572872 | tf_op jit(solution)/shard_map/ppermute | solution.py:155
  110.0 11.0 %collective-permute-start.13 = (bf16[512,512]{1,0:T(8,128)(2,1)S(1)}, bf16[512,512]{1,0:T(8,128)(2,1)S(1)}, u32[]{:S(2)}, u32[]{:S(2)}) collective-permute-start(bf16[512,512]{1,0:T(8,128)(2,1)S(1)} %get-tuple-element.58), channel_id=1, source_target_pairs={{0,6},{1,7},{2,0},{3,1},{4,2},{5,3},{6,4},{7,5},{8,14},{9,15},{10,... | collective-permute-start | bytes 1572872 | tf_op jit(solution)/shard_map/ppermute | solution.py:150
  111.7 12.0 %collective-permute-start.17 = (bf16[512,512]{1,0:T(8,128)(2,1)S(1)}, bf16[512,512]{1,0:T(8,128)(2,1)S(1)}, u32[]{:S(2)}, u32[]{:S(2)}) collective-permute-start(bf16[512,512]{1,0:T(8,128)(2,1)S(1)} %add_convert_fusion.1), channel_id=1, source_target_pairs={{0,2},{1,3},{2,4},{3,5},{4,6},{5,7},{6,0},{7,1},{8,10},{9,11},{10,... | collective-permute-start | bytes 1572872 | tf_op jit(solution)/shard_map/ppermute | solution.py:150
